TPU v7x, 256 devices: a whole 4x4x8 slice. The times are simulated.
256 devices in a mesh: rep: 2 (over core), ctx: 32 (over y, z), tp: 4 (over x).
Axes of the slice: x: 4, y: 4, z: 8, core: 2. Of those that a mesh axis runs over, the one named last changes fastest.
Arguments:
- tokens: float32 [2, 12288, 2048], P('rep', 'ctx'), may hold values from -32 to 32
- qk_weight: float32 [2048, 2048], P(('rep', 'ctx'), 'tp'), may hold values from -0.125 to 0.125
- value_weight: float32 [2048, 2048], P(('rep', 'ctx'), 'tp'), may hold values from -0.125 to 0.125
- grad_out: float32 [2, 12288, 2048], P('rep', 'ctx', 'tp'), may hold values from -6 to 6
- assign: int32 [16, 2, 12288, 1], P('tp', 'rep', 'ctx'), may hold values from 0 to 255; in each aligned block of 384 rows (0 to 383, 384 to 767, ..., all dimensions but the last counted through in order) at most 3 rows name the same one
Outputs:
- grad_tokens: float32 [2, 12288, 2048], P('rep', 'ctx', 'tp')
- grad_qk_weight: float32 [2048, 2048], P(('rep', 'ctx'), 'tp')
- grad_value_weight: float32 [2048, 2048], P(('rep', 'ctx'), 'tp')
Inputs may be any that keep to these rules, and one draw needn't show every extreme that they name: `assign`: within the 384 tokens of one index of ctx, for one head and one sequence, no cluster holds more than 3 tokens; in some of these blocks a cluster holds exactly 3.
All inputs are finite; a program needn't handle non-finite values.
Results may differ from a plain program's by a relative error of at most 0.0003.
Values sent between devices are 32-bit elements; how exact they have to be, the bound alone decides.
A program may use at most 128 MiB of HBM per device.

v0:
```python
import jax
import jax.numpy as jnp
from jax import lax
from jax.sharding import PartitionSpec as P

HD = 128
CL_DEV = 8


masked_score = -1e30
exact = lax.Precision.HIGHEST


def attend_blocks(query_key, values, validity):
    scores = jnp.einsum("nqd,nkd->nqk", query_key, query_key, precision=exact) / HD
    scores = jnp.where(validity[:, None, :] > 0.5, scores, masked_score)
    highest = lax.stop_gradient(jnp.max(scores, axis=2, keepdims=True))
    weights = jnp.exp(scores - highest)
    weights = weights / jnp.sum(weights, axis=2, keepdims=True)
    return jnp.einsum("nqk,nkd->nqd", weights, values, precision=exact)


def cluster_gradients(packed, validity):
    query_key = packed[:, :, :HD]
    values = packed[:, :, HD : 2 * HD]
    upstream = packed[:, :, 2 * HD :]

    def forward(first_part, second_part):
        return attend_blocks(first_part, second_part, validity)

    attended, pullback = jax.vjp(forward, query_key, values)
    grad_qk, grad_values = pullback(upstream)
    return jnp.concatenate([grad_qk, grad_values], axis=2)


def matmul(left, right):
    return jnp.dot(left, right, precision=exact, preferred_element_type=jnp.float32)


def matmul_nt(left, right):
    return lax.dot_general(
        left, right, (((1,), (1,)), ((), ())), precision=exact, preferred_element_type=jnp.float32
    )


def matmul_tn(left, right):
    return lax.dot_general(
        left, right, (((0,), (0,)), ((), ())), precision=exact, preferred_element_type=jnp.float32
    )


def per_device(tokens, qk_weight, value_weight, grad_out, assign):
    inputs = tokens[0]
    length = inputs.shape[0]
    ctx_count = lax.axis_size("ctx")
    clusters = CL_DEV * ctx_count
    per_source = 2 * length // clusters
    heads_here = qk_weight.shape[1] // HD
    width = heads_here * HD
    routing = assign[:, 0, :, 0]
    full_qk, full_values = (
        lax.all_gather(qk_weight, ("rep", "ctx"), axis=0, tiled=True),
        lax.all_gather(value_weight, ("rep", "ctx"), axis=0, tiled=True),
    )
    query_key = matmul(inputs, full_qk)
    values = matmul(inputs, full_values)

    def by_head(matrix):
        return matrix.reshape(length, heads_here, HD).transpose(1, 0, 2)

    payload = jnp.concatenate([by_head(query_key), by_head(values), by_head(grad_out[0])], axis=2)
    labels = jnp.arange(clusters, dtype=jnp.int32)
    onehot_table = (routing[:, :, None] == labels[None, None, :]).astype(jnp.int32)
    within = jnp.sum((jnp.cumsum(onehot_table, axis=1) - 1) * onehot_table, axis=2)
    head_ids = jnp.arange(heads_here, dtype=jnp.int32)[:, None]
    slots = ((routing * heads_here + head_ids) * per_source + within).reshape(-1)
    total = clusters * heads_here * per_source
    outgoing = jnp.zeros((total, 3 * HD), jnp.float32).at[slots].set(payload.reshape(-1, 3 * HD))
    outgoing = outgoing.reshape(ctx_count, CL_DEV, heads_here, per_source, 3 * HD)
    marks = jnp.zeros((total,), jnp.float32).at[slots].set(1.0)
    marks = marks.reshape(ctx_count, CL_DEV, heads_here, per_source)
    rows_in = lax.all_to_all(outgoing, "ctx", split_axis=0, concat_axis=0, tiled=True)
    marks_in = lax.all_to_all(marks, "ctx", split_axis=0, concat_axis=0, tiled=True)
    owned = rows_in.shape[1]
    senders = rows_in.shape[0]
    packed = rows_in.transpose(1, 2, 0, 3, 4).reshape(
        owned * heads_here, senders * per_source, 3 * HD
    )
    validity = marks_in.transpose(1, 2, 0, 3).reshape(owned * heads_here, senders * per_source)
    gradients = cluster_gradients(packed, validity)
    replies = gradients.reshape(owned, heads_here, senders, per_source, 2 * HD).transpose(
        2, 0, 1, 3, 4
    )
    returned = lax.all_to_all(replies, "ctx", split_axis=0, concat_axis=0, tiled=True)
    picked = returned.reshape(total, 2 * HD)[slots].reshape(heads_here, length, 2 * HD)
    grad_qk = picked[:, :, :HD].transpose(1, 0, 2).reshape(length, width)
    grad_values = picked[:, :, HD:].transpose(1, 0, 2).reshape(length, width)
    token_terms = matmul_nt(grad_qk, full_qk) + matmul_nt(grad_values, full_values)
    grad_tokens = lax.psum_scatter(token_terms[None], "tp", scatter_dimension=2, tiled=True)
    combined = jnp.concatenate([grad_qk, grad_values], axis=1)
    weight_sums = lax.psum_scatter(
        matmul_tn(inputs, combined), ("rep", "ctx"), scatter_dimension=0, tiled=True
    )
    return (grad_tokens, weight_sums[:, :width], weight_sums[:, width:])


def solution(mesh):
    in_specs = (
        P("rep", "ctx", None),
        P(("rep", "ctx"), "tp"),
        P(("rep", "ctx"), "tp"),
        P("rep", "ctx", "tp"),
        P("tp", "rep", "ctx", None),
    )
    out_specs = (P("rep", "ctx", "tp"), P(("rep", "ctx"), "tp"), P(("rep", "ctx"), "tp"))
    return jax.shard_map(
        per_device, mesh=mesh, in_specs=in_specs, out_specs=out_specs, check_vma=False
    )
```

profile of v0, /device:TPU:2, one launch (start us, length us, event | category | flops | bytes accessed | tf_op | source)
XLA Modules:
  0.0 708.7 jit_solution(4305915565041687223)
XLA Ops:
  15.6 6.2 scatter_custom_fusion
  25.7 11.5 %all-to-all-start = ((f32[32,8,4,3]{1,2,3,0:T(4,128)}), f32[32,8,4,3]{1,2,3,0:T(4,128)S(1)}, u32[]{:S(2)}, u32[]{:S(2)}) async-start(f32[32,8,4,3]{1,2,3,0:T(4,128)} %copy.39), calls=%async_computation | async-start | bytes 393216 | tf_op jit(solution)/shard_map/all_to_all | solution.py:83
  39.5 53.5 %all-gather.5.cloned.1.call-done = f32[2048,512]{1,0:T(8,128)} async-done(((f32[32,512]{1,0:T(8,128)}), f32[2048,512]{1,0:T(8,128)}) %all-gather.5.cloned.1.call-update) | async-done | bytes 4194320 | tf_op jit(solution)/shard_map/all_gather | solution.py:63
  98.3 73.6 %all-gather.3.cloned.1.call-done = f32[2048,512]{1,0:T(8,128)} async-done(((f32[32,512]{1,0:T(8,128)}), f32[2048,512]{1,0:T(8,128)}) %all-gather.3.cloned.1.call-update) | async-done | bytes 4194320 | tf_op jit(solution)/shard_map/all_gather | solution.py:62
  177.4 9.2 %fusion.26 = f32[4,384,128]{1,2,0:T(8,128)S(1)} fusion(f32[4,128,2048]{2,1,0:T(8,128)} %bitcast.79, f32[1,384,2048]{2,1,0:T(8,128)S(1)} %copy-done), kind=kOutput, calls=%fused_computation.40 | convolution fusion | flops 4831838208 | bytes 8126464 | tf_op jit(solution)/shard_map/dot_general | solution.py:37
  186.6 6.8 fusion.23
  198.1 9.9 %scatter_custom_fusion.1 = f32[3072,384]{1,0:T(8,128)} fusion(s32[1536]{0:T(1024)S(1)} %fusion.33, f32[1536,384]{1,0:T(8,128)} %bitcast.90, f32[]{:T(128)} %constant.11.clone.1), kind=kCustom, calls=%fused_computation.12 | custom fusion | bytes 4719104 | tf_op jit(solution)/shard_map/scatter | solution.py:78
  208.0 7.9 %reshape.123 = f32[32,8,4,3,384]{4,3,2,1,0:T(4,128)} reshape(f32[3072,384]{1,0:T(8,128)} %scatter_custom_fusion.1) | data formatting | bytes 9437184 | tf_op jit(solution)/shard_map/reshape | solution.py:79
  215.9 7.0 copy.46
  222.9 6.3 all-to-all-start.1
  230.2 105.3 %all-to-all-done.1 = f32[32,8,4,3,384]{4,1,3,2,0:T(8,128)} async-done(((f32[32,8,4,3,384]{4,1,3,2,0:T(8,128)}), f32[32,8,4,3,384]{4,1,3,2,0:T(8,128)}, u32[]{:S(2)}, u32[]{:S(2)}) %all-to-all-start.1) | async-done | bytes 4718624 | tf_op jit(solution)/shard_map/all_to_all | solution.py:82
  335.6 6.6 copy.61
  342.2 8.2 %reshape.157 = f32[32,96,384]{2,1,0:T(8,128)} reshape(f32[8,4,32,3,384]{4,3,2,1,0:T(4,128)} %copy.61) | data formatting | bytes 9437184 | tf_op jit(solution)/shard_map/reshape | solution.py:86
  376.4 8.0 %all-to-all-start.2 = ((f32[32,8,4,3,256]{4,2,1,3,0:T(4,128)}), f32[32,8,4,3,256]{4,2,1,3,0:T(4,128)}, u32[]{:S(2)}, u32[]{:S(2)}) async-start(f32[32,8,4,3,256]{4,2,1,3,0:T(4,128)} %bitcast.83), calls=%async_computation.2 | async-start | bytes 6291456 | tf_op jit(solution)/shard_map/all_to_all | solution.py:94
  384.5 74.8 %all-to-all-done.2 = f32[32,8,4,3,256]{4,2,1,3,0:T(4,128)} async-done(((f32[32,8,4,3,256]{4,2,1,3,0:T(4,128)}), f32[32,8,4,3,256]{4,2,1,3,0:T(4,128)}, u32[]{:S(2)}, u32[]{:S(2)}) %all-to-all-start.2) | async-done | bytes 3145760 | tf_op jit(solution)/shard_map/all_to_all | solution.py:94
  459.3 6.5 copy.53
  465.8 6.2 reshape.126
  471.9 6.5 gather_fusion
  485.7 16.7 %convolution_bitcast_fusion = f32[2048,1024]{0,1:T(8,128)} fusion(f32[1,384,2048]{2,1,0:T(8,128)S(1)} %copy-done, f32[384,512]{0,1:T(8,128)} %bitcast.86, f32[384,512]{0,1:T(8,128)} %bitcast.84), kind=kOutput, calls=%fused_computation.3 | convolution fusion | flops 9664069632 | bytes 13107200 | tf_op jit(solution)/shard_map/dot_general | solution.py:47
  502.4 9.3 %copy.59 = f32[2048,1024]{1,0:T(8,128)} copy(f32[2048,1024]{0,1:T(8,128)} %convolution_bitcast_fusion) | data formatting | bytes 16777216
  511.8 12.7 %fusion.40 = f32[384,2048]{1,0:T(8,128)S(1)} fusion(f32[384,512]{0,1:T(8,128)} %bitcast.85, f32[2048,512]{1,0:T(8,128)} %all-gather.3.cloned.1.call-done), kind=kOutput, calls=%fused_computation.61 | convolution fusion | flops 4831838208 | bytes 8126464 | tf_op jit(solution)/shard_map/dot_general | solution.py:41
  524.5 12.1 %add_bitcast_fusion = f32[1,384,2048]{2,1,0:T(8,128)} fusion(f32[384,2048]{1,0:T(8,128)S(1)} %fusion.40, f32[384,512]{0,1:T(8,128)S(1)} %bitcast.87, f32[2048,512]{1,0:T(8,128)S(1)} %copy-done.3), kind=kOutput, calls=%fused_computation.10 | convolution fusion | flops 4832624640 | bytes 11272192 | tf_op jit(solution)/shard_map/dot_general | solution.py:41
  536.7 124.1 %reduce-scatter.7.cloned.1.call-done = f32[32,1024]{1,0:T(8,128)} async-done(((f32[2048,1024]{1,0:T(8,128)}), f32[32,1024]{1,0:T(8,128)}) %reduce-scatter.7.cloned.1.call-update) | async-done | bytes 131088
  662.3 39.3 %reduce-scatter.5.cloned.1.call-done = f32[1,384,512]{2,1,0:T(8,128)} async-done(((f32[1,384,2048]{2,1,0:T(8,128)}), f32[1,384,512]{2,1,0:T(8,128)}) %reduce-scatter.5.cloned.1.call-update) | async-done | bytes 786448 | tf_op jit(solution)/shard_map/reduce_scatter | solution.py:99
  (67 shorter events, 65.8 us)
Async XLA Ops:
  7.2 170.2 %copy-start = (f32[1,384,2048]{2,1,0:T(8,128)S(1)}, f32[1,384,2048]{2,1,0:T(8,128)}, u32[]{:S(2)}) copy-start(f32[1,384,2048]{2,1,0:T(8,128)} %param.5) | copy-start | bytes 9437188
  7.2 85.8 %all-gather.5.cloned.1.call-start = ((), (), s32[]{:S(2)}) async-start(), calls=%async_computation.6 | async-start | bytes 4259840 | tf_op jit(solution)/shard_map/all_gather | solution.py:63
  7.9 164.0 %all-gather.3.cloned.1.call-start = ((), (), s32[]{:S(2)}) async-start(), calls=%async_computation.5 | async-start | bytes 4259840 | tf_op jit(solution)/shard_map/all_gather | solution.py:62
  11.1 1.4 copy-start.4
  14.8 0.7 copy-start.7
  25.7 197.2 %all-to-all-start = ((f32[32,8,4,3]{1,2,3,0:T(4,128)}), f32[32,8,4,3]{1,2,3,0:T(4,128)S(1)}, u32[]{:S(2)}, u32[]{:S(2)}) async-start(f32[32,8,4,3]{1,2,3,0:T(4,128)} %copy.39), calls=%async_computation | async-start | bytes 393216 | tf_op jit(solution)/shard_map/all_to_all | solution.py:83
  177.4 9.2 %copy-start.1 = (f32[512,2048]{1,0:T(8,128)S(1)}, f32[512,2048]{1,0:T(8,128)}, u32[]{:S(2)}) copy-start(f32[512,2048]{1,0:T(8,128)} %copy.42) | copy-start | bytes 12582916
  186.6 6.9 copy-start.6
  222.9 112.7 %all-to-all-start.1 = ((f32[32,8,4,3,384]{4,1,3,2,0:T(8,128)}), f32[32,8,4,3,384]{4,1,3,2,0:T(8,128)}, u32[]{:S(2)}, u32[]{:S(2)}) async-start(f32[32,8,4,3,384]{4,1,3,2,0:T(8,128)} %copy.46), calls=%async_computation.1 | async-start | bytes 9437184 | tf_op jit(solution)/shard_map/all_to_all | solution.py:82
  350.4 5.9 copy-start.2
  376.4 82.9 %all-to-all-start.2 = ((f32[32,8,4,3,256]{4,2,1,3,0:T(4,128)}), f32[32,8,4,3,256]{4,2,1,3,0:T(4,128)}, u32[]{:S(2)}, u32[]{:S(2)}) async-start(f32[32,8,4,3,256]{4,2,1,3,0:T(4,128)} %bitcast.83), calls=%async_computation.2 | async-start | bytes 6291456 | tf_op jit(solution)/shard_map/all_to_all | solution.py:94
  384.5 276.3 %reduce-scatter.7.cloned.1.call-start = ((), (), s32[]{:S(2)}) async-start(), calls=%async_computation.8 | async-start | bytes 8519680
  511.7 190.0 %reduce-scatter.5.cloned.1.call-start = ((), (), s32[]{:S(2)}) async-start(), calls=%async_computation.7 | async-start | bytes 3932160 | tf_op jit(solution)/shard_map/reduce_scatter | solution.py:99
  511.7 12.8 %copy-start.3 = (f32[2048,512]{1,0:T(8,128)S(1)}, f32[2048,512]{1,0:T(8,128)}, u32[]{:S(2)}) copy-start(f32[2048,512]{1,0:T(8,128)} %all-gather.5.cloned.1.call-done) | copy-start | bytes 12582916
  511.7 12.8 %copy-start.5 = (f32[4,384,128]{1,2,0:T(8,128)S(1)}, f32[4,384,128]{1,2,0:T(8,128)}, u32[]{:S(2)}) copy-start(f32[4,384,128]{1,2,0:T(8,128)} %copy.65) | copy-start | bytes 2359300
Sparse Core Ops, SparseCore 0:
  10.8 82.1 all-gather.4
  95.7 76.2 all-gather.2
  511.8 148.9 reduce-scatter.6
  663.9 37.6 reduce-scatter.4
where the time goes:
time: 719 us; the launch traced here: 709 us
  waiting for transfers between devices  472 us (66%)
  local copies, waits for them, and re-layouts  116 us (16%)
  matrix products  74.7 us (10%)
  starting transfers between devices  26 us (4%)
  between operations  14.6 us (2%)
    unnamed x5, waiting for transfers between devices  126 us
    all_to_all x1, waiting for transfers between devices, per_device(): lax.all_to_all(outgoing, 'ctx', split_axis=0, concat_axis=0, tiled=True)  105 us
    all_to_all x1, waiting for transfers between devices, per_device(): lax.all_to_all(replies, 'ctx', split_axis=0, concat_axis=0, tiled=True)  74.8 us
    all_gather x1, waiting for transfers between devices, per_device(): lax.all_gather(qk_weight, ('rep', 'ctx'), axis=0, tiled=True)  73.6 us
    all_gather x1, waiting for transfers between devices, per_device(): lax.all_gather(value_weight, ('rep', 'ctx'), axis=0, tiled=True)  53.5 us
    reduce_scatter x1, waiting for transfers between devices, per_device(): lax.psum_scatter(token_terms[None], 'tp', scatter_dimension=2, tiled=True)  39.3 us
    dot_general x2, matrix products, matmul_nt(): lax.dot_general(left, right, (((1,), (1,)), ((), ())), precision=exact, p...  24.9 us
    unnamed x25, local copies, waits for them, and re-layouts  19.1 us
  transfers between devices with their start and end apart: 7, of which 6 were waited for; matrix products, arithmetic and copies ran while one was open for 14% of the time, Pallas kernels for 0%

commit v1 on v0

--- a/solution.py
+++ b/solution.py
@@ -1,14 +1,332 @@
 import jax
 import jax.numpy as jnp
 from jax import lax
+from jax.experimental import pallas as pl
+from jax.experimental.pallas import tpu as pltpu
 from jax.sharding import PartitionSpec as P
 
 HD = 128
 CL_DEV = 8
-
+NY = 4
+NZ = 8
+ROWS = 32
+HALF = 16
+MESH = pl.DeviceIdType.MESH
 
 masked_score = -1e30
 exact = lax.Precision.HIGHEST
+split = lax.Precision.HIGH
+
+
+def position():
+    ctx = lax.axis_index("ctx")
+    return lax.axis_index("rep"), lax.div(ctx, NZ), lax.rem(ctx, NZ)
+
+
+def greet(partners):
+    barrier = pltpu.get_barrier_semaphore()
+    for partner in partners:
+        pl.semaphore_signal(barrier, inc=1, device_id=partner, device_id_type=MESH)
+    pl.semaphore_wait(barrier, len(partners))
+
+
+class Copies:
+    def __init__(self, send_sem, recv_sem):
+        self.send_sem, self.recv_sem = send_sem, recv_sem
+        self.all = []
+
+    def start(self, source, target, device):
+        index = len(self.all)
+        copy = pltpu.make_async_remote_copy(
+            src_ref=source,
+            dst_ref=target,
+            send_sem=self.send_sem.at[index],
+            recv_sem=self.recv_sem.at[index],
+            device_id=device,
+            device_id_type=MESH,
+        )
+        copy.start()
+        self.all.append(copy)
+        return copy
+
+    def finish(self):
+        for copy in self.all:
+            copy.wait_send()
+
+
+GATHER_COPIES = 3 + 7 + 7 + 3 + 8 + 4
+
+
+def gather_kernel(qk_ref, value_ref, out_ref, local_sem, send_sem, recv_sem):
+    rep, y, z = position()
+    width = qk_ref.shape[1]
+
+    def along_y(step):
+        return {"ctx": lax.rem(y + step, NY) * NZ + z}
+
+    def along_z(step):
+        return {"ctx": y * NZ + lax.rem(z + step, NZ)}
+
+    def plane(step):
+        return out_ref.at[rep, :, lax.rem(z + step, NZ), pl.ds(0, HALF), :]
+
+    def piece(step):
+        return out_ref.at[rep, y, lax.rem(z + step, NZ), pl.ds(HALF, HALF), :]
+
+    def line(step):
+        return out_ref.at[rep, lax.rem(y + step, NY), :, pl.ds(HALF, HALF), :]
+
+    right, left, other = along_z(1), along_z(NZ - 1), {"rep": 1 - rep}
+    greet([along_y(1), along_y(2), along_y(3), right, left, other])
+    copies = Copies(send_sem, recv_sem)
+    mine = out_ref.at[rep, y, z]
+    first = pltpu.make_async_copy(qk_ref, mine.at[:, pl.ds(0, width)], local_sem.at[0])
+    second = pltpu.make_async_copy(value_ref, mine.at[:, pl.ds(width, width)], local_sem.at[1])
+    first.start()
+    second.start()
+    first.wait()
+    second.wait()
+
+    own = out_ref.at[rep, y, z, pl.ds(0, HALF), :]
+    shared = [copies.start(own, own, along_y(step)) for step in (1, 3, 2)]
+    pieces = [(copies.start(piece(0), piece(0), right), copies.start(piece(0), piece(0), left))]
+    for copy in shared:
+        copy.wait_recv()
+    planes = [(copies.start(plane(0), plane(0), right), copies.start(plane(0), plane(0), left))]
+    across = [copies.start(plane(0), plane(0), other)]
+    for step in range(4):
+        rightward, leftward = pieces[step]
+        rightward.wait_recv()
+        if leftward is not None:
+            leftward.wait_recv()
+        if step < 3:
+            after, before = piece(NZ - 1 - step), piece(1 + step)
+            pieces.append((
+                copies.start(after, after, right),
+                copies.start(before, before, left) if step < 2 else None,
+            ))
+    lines = [copies.start(line(0), line(0), along_y(step)) for step in (1, 3, 2)]
+    across.append(copies.start(line(0), line(0), other))
+    for step in range(4):
+        rightward, leftward = planes[step]
+        after, before = plane(NZ - 1 - step), plane(1 + step)
+        rightward.wait_recv()
+        if step < 3:
+            going = copies.start(after, after, right)
+        across.append(copies.start(after, after, other))
+        if leftward is not None:
+            leftward.wait_recv()
+            coming = copies.start(before, before, left) if step < 2 else None
+            across.append(copies.start(before, before, other))
+        if step < 3:
+            planes.append((going, coming if step < 2 else None))
+    for copy, step in zip(lines, (3, 1, 2)):
+        copy.wait_recv()
+        across.append(copies.start(line(step), line(step), other))
+    for copy in across:
+        copy.wait_recv()
+    copies.finish()
+    assert len(copies.all) == GATHER_COPIES
+
+
+def gather_weights(qk_weight, value_weight):
+    width = qk_weight.shape[1]
+    return pl.pallas_call(
+        gather_kernel,
+        out_shape=jax.ShapeDtypeStruct((2, NY, NZ, ROWS, 2 * width), jnp.float32),
+        in_specs=[pl.BlockSpec(memory_space=pl.ANY)] * 2,
+        out_specs=pl.BlockSpec(memory_space=pl.ANY),
+        scratch_shapes=[
+            pltpu.SemaphoreType.DMA((2,)),
+            pltpu.SemaphoreType.DMA((GATHER_COPIES,)),
+            pltpu.SemaphoreType.DMA((GATHER_COPIES,)),
+        ],
+        compiler_params=pltpu.CompilerParams(collective_id=0, has_side_effects=True),
+        name="gather_weights",
+    )(qk_weight, value_weight)
+
+
+SCATTER_COPIES = 3 + 12 + 7 + 3 + 7 + 3
+
+
+def scatter_kernel(
+    terms_ref, sums_ref, tokens_out, qk_out, value_out,
+    column_in, cross_in, ring_a, ring_b, line_in, plane_in,
+    local_sem, send_sem, recv_sem,
+):
+    rep, y, z = position()
+    x = lax.axis_index("tp")
+    width = qk_out.shape[1]
+
+    def along_y(step):
+        return {"ctx": lax.rem(y + step, NY) * NZ + z}
+
+    def along_z(step):
+        return {"ctx": y * NZ + lax.rem(z + step, NZ)}
+
+    def along_x(step):
+        return {"tp": lax.rem(x + step, 4)}
+
+    def columns(step):
+        start = pl.multiple_of(lax.rem(x + step, 4) * width, width)
+        return terms_ref.at[:, pl.ds(start, width)]
+
+    def plane(step):
+        return cross_in.at[:, lax.rem(z + step, NZ), pl.ds(0, HALF), :]
+
+    def line(step):
+        return cross_in.at[lax.rem(y + step, NY), :, pl.ds(HALF, HALF), :]
+
+    def piece(step):
+        return cross_in.at[y, lax.rem(z + step, NZ), pl.ds(HALF, HALF), :]
+
+    right, left, other = along_z(1), along_z(NZ - 1), {"rep": 1 - rep}
+    greet(
+        [along_y(1), along_y(2), along_y(3), right, left, other]
+        + [along_x(1), along_x(2), along_x(3)]
+    )
+    copies = Copies(send_sem, recv_sem)
+    sideways = [
+        copies.start(columns(step), column_in.at[step - 1], along_x(step)) for step in (1, 3, 2)
+    ]
+    own_columns = pltpu.make_async_copy(columns(0), tokens_out, local_sem)
+    own_columns.start()
+
+    cross = {}
+    for kind, step in (
+        ("a", 4), ("a", 5), ("b", 1), ("b", 3), ("b", 2), ("a", 3),
+        ("a", 6), ("a", 2), ("a", 7), ("b", 0), ("a", 1), ("a", 0),
+    ):
+        if kind == "a":
+            there = lax.rem(z + step, NZ)
+            source = sums_ref.at[1 - rep, :, there, pl.ds(0, HALF), :]
+            cross[kind, step] = copies.start(source, plane(step), other)
+        else:
+            there = lax.rem(y + step, NY)
+            source = sums_ref.at[1 - rep, there, :, pl.ds(HALF, HALF), :]
+            cross[kind, step] = copies.start(source, line(step), other)
+
+    def add_plane(step):
+        cross["a", step].wait_recv()
+        there = lax.rem(z + step, NZ)
+        cross_in[:, there, pl.ds(0, HALF), :] += sums_ref[rep, :, there, pl.ds(0, HALF), :]
+
+    def add_line(step):
+        cross["b", step].wait_recv()
+        there = lax.rem(y + step, NY)
+        cross_in[there, :, pl.ds(HALF, HALF), :] += sums_ref[
+            rep, there, :, pl.ds(HALF, HALF), :
+        ]
+
+    add_plane(4)
+    right_a = copies.start(plane(4), ring_a.at[0], right)
+    add_plane(5)
+    left_a = copies.start(plane(5), ring_a.at[4], left)
+    lines = []
+    for step in (1, 3, 2):
+        add_line(step)
+        lines.append(copies.start(line(step), line_in.at[step - 1], along_y(step)))
+
+    def pass_a(turn):
+        nonlocal right_a, left_a
+        add_plane(4 - turn)
+        right_a.wait_recv()
+        ring_a[turn - 1] += cross_in[:, lax.rem(z + 4 - turn, NZ), pl.ds(0, HALF), :]
+        right_a = copies.start(ring_a.at[turn - 1], ring_a.at[turn], right)
+        if turn < 3:
+            add_plane(5 + turn)
+            left_a.wait_recv()
+            ring_a[3 + turn] += cross_in[:, lax.rem(z + 5 + turn, NZ), pl.ds(0, HALF), :]
+            left_a = copies.start(ring_a.at[3 + turn], ring_a.at[4 + turn], left)
+
+    pass_a(1)
+    add_line(0)
+    pass_a(2)
+    for copy in lines:
+        copy.wait_recv()
+    cross_in[y, :, pl.ds(HALF, HALF), :] += line_in[0] + line_in[1] + line_in[2]
+    right_b = copies.start(piece(4), ring_b.at[0], right)
+    left_b = copies.start(piece(5), ring_b.at[4], left)
+    pass_a(3)
+
+    def pass_b(turn):
+        nonlocal right_b, left_b
+        right_b.wait_recv()
+        ring_b[turn - 1] += cross_in[y, lax.rem(z + 4 - turn, NZ), pl.ds(HALF, HALF), :]
+        right_b = copies.start(ring_b.at[turn - 1], ring_b.at[turn], right)
+        if turn < 3:
+            left_b.wait_recv()
+            ring_b[3 + turn] += cross_in[y, lax.rem(z + 5 + turn, NZ), pl.ds(HALF, HALF), :]
+            left_b = copies.start(ring_b.at[3 + turn], ring_b.at[4 + turn], left)
+
+    pass_b(1)
+    pass_b(2)
+    add_plane(0)
+    right_a.wait_recv()
+    left_a.wait_recv()
+    cross_in[:, z, pl.ds(0, HALF), :] += ring_a[3] + ring_a[6]
+    planes = [
+        copies.start(
+            cross_in.at[lax.rem(y + step, NY), z, pl.ds(0, HALF), :],
+            plane_in.at[step - 1],
+            along_y(step),
+        )
+        for step in (1, 3, 2)
+    ]
+    pass_b(3)
+    right_b.wait_recv()
+    left_b.wait_recv()
+    lower = cross_in[y, z, pl.ds(HALF, HALF), :] + ring_b[3] + ring_b[6]
+    qk_out[pl.ds(HALF, HALF), :] = lower[:, :width]
+    value_out[pl.ds(HALF, HALF), :] = lower[:, width:]
+    for copy in planes:
+        copy.wait_recv()
+    upper = cross_in[y, z, pl.ds(0, HALF), :] + plane_in[0] + plane_in[1] + plane_in[2]
+    qk_out[pl.ds(0, HALF), :] = upper[:, :width]
+    value_out[pl.ds(0, HALF), :] = upper[:, width:]
+    own_columns.wait()
+    for copy in sideways:
+        copy.wait_recv()
+
+    @pl.loop(0, tokens_out.shape[0] // 8)
+    def _(block):
+        here = pl.ds(pl.multiple_of(block * 8, 8), 8)
+        tokens_out[here, :] += column_in[0, here, :] + column_in[1, here, :] + column_in[2, here, :]
+
+    copies.finish()
+    assert len(copies.all) == SCATTER_COPIES
+
+
+def scatter_sums(token_terms, weight_terms):
+    length = token_terms.shape[0]
+    both = weight_terms.shape[1]
+    width = both // 2
+    f32 = jnp.float32
+    return pl.pallas_call(
+        scatter_kernel,
+        out_shape=(
+            jax.ShapeDtypeStruct((length, width), f32),
+            jax.ShapeDtypeStruct((ROWS, width), f32),
+            jax.ShapeDtypeStruct((ROWS, width), f32),
+        ),
+        in_specs=[pl.BlockSpec(memory_space=pl.ANY), pl.BlockSpec(memory_space=pltpu.VMEM)],
+        out_specs=(pl.BlockSpec(memory_space=pltpu.VMEM),) * 3,
+        scratch_shapes=[
+            pltpu.VMEM((3, length, width), f32),
+            pltpu.VMEM((NY, NZ, ROWS, both), f32),
+            pltpu.VMEM((7, NY, HALF, both), f32),
+            pltpu.VMEM((7, HALF, both), f32),
+            pltpu.VMEM((3, NZ, HALF, both), f32),
+            pltpu.VMEM((3, HALF, both), f32),
+            pltpu.SemaphoreType.DMA,
+            pltpu.SemaphoreType.DMA((SCATTER_COPIES,)),
+            pltpu.SemaphoreType.DMA((SCATTER_COPIES,)),
+        ],
+        compiler_params=pltpu.CompilerParams(
+            collective_id=1, has_side_effects=True, vmem_limit_bytes=48 * 2**20
+        ),
+        name="scatter_sums",
+    )(token_terms, weight_terms.reshape(2, NY, NZ, ROWS, both))
 
 
 def attend_blocks(query_key, values, validity):
@@ -34,18 +352,18 @@
 
 
 def matmul(left, right):
-    return jnp.dot(left, right, precision=exact, preferred_element_type=jnp.float32)
+    return jnp.dot(left, right, precision=split, preferred_element_type=jnp.float32)
 
 
 def matmul_nt(left, right):
     return lax.dot_general(
-        left, right, (((1,), (1,)), ((), ())), precision=exact, preferred_element_type=jnp.float32
+        left, right, (((1,), (1,)), ((), ())), precision=split, preferred_element_type=jnp.float32
     )
 
 
 def matmul_tn(left, right):
     return lax.dot_general(
-        left, right, (((0,), (0,)), ((), ())), precision=exact, preferred_element_type=jnp.float32
+        left, right, (((0,), (0,)), ((), ())), precision=split, preferred_element_type=jnp.float32
     )
 
 
@@ -58,17 +376,15 @@
     heads_here = qk_weight.shape[1] // HD
     width = heads_here * HD
     routing = assign[:, 0, :, 0]
-    full_qk, full_values = (
-        lax.all_gather(qk_weight, ("rep", "ctx"), axis=0, tiled=True),
-        lax.all_gather(value_weight, ("rep", "ctx"), axis=0, tiled=True),
-    )
-    query_key = matmul(inputs, full_qk)
-    values = matmul(inputs, full_values)
+    full = gather_weights(qk_weight, value_weight).reshape(-1, 2 * width)
+    projected = matmul(inputs, full)
 
     def by_head(matrix):
         return matrix.reshape(length, heads_here, HD).transpose(1, 0, 2)
 
-    payload = jnp.concatenate([by_head(query_key), by_head(values), by_head(grad_out[0])], axis=2)
+    payload = jnp.concatenate(
+        [by_head(projected[:, :width]), by_head(projected[:, width:]), by_head(grad_out[0])], axis=2
+    )
     labels = jnp.arange(clusters, dtype=jnp.int32)
     onehot_table = (routing[:, :, None] == labels[None, None, :]).astype(jnp.int32)
     within = jnp.sum((jnp.cumsum(onehot_table, axis=1) - 1) * onehot_table, axis=2)
@@ -95,13 +411,11 @@
     picked = returned.reshape(total, 2 * HD)[slots].reshape(heads_here, length, 2 * HD)
     grad_qk = picked[:, :, :HD].transpose(1, 0, 2).reshape(length, width)
     grad_values = picked[:, :, HD:].transpose(1, 0, 2).reshape(length, width)
-    token_terms = matmul_nt(grad_qk, full_qk) + matmul_nt(grad_values, full_values)
-    grad_tokens = lax.psum_scatter(token_terms[None], "tp", scatter_dimension=2, tiled=True)
     combined = jnp.concatenate([grad_qk, grad_values], axis=1)
-    weight_sums = lax.psum_scatter(
-        matmul_tn(inputs, combined), ("rep", "ctx"), scatter_dimension=0, tiled=True
-    )
-    return (grad_tokens, weight_sums[:, :width], weight_sums[:, width:])
+    token_terms = matmul_nt(combined, full)
+    weight_terms = matmul_tn(inputs, combined)
+    grad_tokens, grad_qk_weight, grad_value_weight = scatter_sums(token_terms, weight_terms)
+    return (grad_tokens[None], grad_qk_weight, grad_value_weight)
 
 
 def solution(mesh):

time: 719 us -> 493 us (0.69)
  waiting for transfers between devices: 472 us -> 181 us
  Pallas kernels: 0 us -> 109 us
  matrix products: 74.7 us -> 56.1 us
  between operations: 14.6 us -> 1.35 us
  local copies, waits for them, and re-layouts: 116 us -> 108 us
    all_gather x2 -> x0, waiting for transfers between devices: 127 us -> none  [the longest x1 73.6 us: per_device(): lax.all_gather(qk_weight, ('rep', 'ctx'), axis=0, tiled=True)]
    unnamed x5 -> x0, waiting for transfers between devices: 126 us -> none
    pallas_call x0 -> x2, Pallas kernels: none -> 109 us  [the longest x1 59.3 us: gather_weights(): pl.pallas_call(gather_kernel, out_shape=jax.ShapeDtypeStruct((2, NY, NZ,...]
    reduce_scatter x1 -> x0, waiting for transfers between devices: 39.3 us -> none  [per_device(): lax.psum_scatter(token_terms[None], 'tp', scatter_dimension=2, tiled=True)]
    dot_general x5 -> x3, matrix products: 57.6 us -> 38.9 us  [the longest x1 15.6 us: matmul(): jnp.dot(left, right, precision=split, preferred_element_type=jnp.float32)]
  transfers between devices with their start and end apart: 7 -> 3, of which waited for: 6 -> 2; matrix products, arithmetic and copies ran while one was open for 14% -> 10% of each run, Pallas kernels for 0% -> 12%
where the time goes in v1:
time: 493 us; the launch traced here: 488 us
  waiting for transfers between devices  181 us (37%)
  Pallas kernels  109 us (22%)
  local copies, waits for them, and re-layouts  108 us (22%)
  matrix products  56.1 us (11%)
  starting transfers between devices  24.4 us (5%)
  other arithmetic  6.58 us (1%)
    all_to_all x1, waiting for transfers between devices, per_device(): lax.all_to_all(outgoing, 'ctx', split_axis=0, concat_axis=0, tiled=True)  107 us
    all_to_all x1, waiting for transfers between devices, per_device(): lax.all_to_all(replies, 'ctx', split_axis=0, concat_axis=0, tiled=True)  74.9 us
    pallas_call x1, Pallas kernels, gather_weights(): pl.pallas_call(gather_kernel, out_shape=jax.ShapeDtypeStruct((2, NY, NZ,...  59.3 us
    pallas_call x1, Pallas kernels, scatter_sums(): pl.pallas_call(scatter_kernel, out_shape=(jax.ShapeDtypeStruct((length, w...  50 us
    dot_general x1, matrix products, matmul(): jnp.dot(left, right, precision=split, preferred_element_type=jnp.float32)  15.6 us
    reshape x2, local copies, waits for them, and re-layouts, per_device(): rows_in.transpose(1, 2, 0, 3, 4)  14.8 us
    reshape x2, local copies, waits for them, and re-layouts, per_device(): outgoing.reshape(ctx_count, CL_DEV, heads_here, per_source, 3 * HD)  14.8 us
    unnamed x25, local copies, waits for them, and re-layouts  14.8 us
  transfers between devices with their start and end apart: 3, of which 2 were waited for; matrix products, arithmetic and copies ran while one was open for 10% of the time, Pallas kernels for 12%

profile of v1, /device:TPU:2, one launch (start us, length us, event | category | flops | bytes accessed | tf_op | source)
XLA Modules:
  0.0 487.6 jit_solution(18074246753309770208)
XLA Ops:
  8.3 6.2 %scatter_custom_fusion = f32[3072]{0:T(1024)S(1)} fusion(s32[1536]{0:T(1024)S(1)} %fusion.26, f32[1536]{0:T(1024)S(1)} %broadcast.84, f32[]{:T(128)} %constant.11.clone.1), kind=kCustom, calls=%fused_computation.49 | custom fusion | bytes 12292 | tf_op jit(solution)/shard_map/scatter | solution.py:396
  18.5 12.0 %all-to-all-start = ((f32[32,8,4,3]{1,2,3,0:T(4,128)}), f32[32,8,4,3]{1,2,3,0:T(4,128)S(1)}, u32[]{:S(2)}, u32[]{:S(2)}) async-start(f32[32,8,4,3]{1,2,3,0:T(4,128)} %copy.50), calls=%async_computation | async-start | bytes 393216 | tf_op jit(solution)/shard_map/all_to_all | solution.py:399
  32.8 59.3 %gather_weights.1 = f32[2,4,8,32,1024]{4,3,2,1,0:T(8,128)} custom-call(f32[32,512]{1,0:T(8,128)} %qk_ref.1, f32[32,512]{1,0:T(8,128)} %value_ref.1), custom_call_target="tpu_custom_call" | custom-call | tf_op jit(solution)/shard_map/gather_weights/pallas_call | solution.py:134
  92.1 15.6 %fusion.12 = f32[384,1024]{0,1:T(8,128)S(1)} fusion(f32[2048,1024]{1,0:T(8,128)} %bitcast.71, f32[1,384,2048]{2,1,0:T(8,128)S(1)} %copy-done), kind=kOutput, calls=%fused_computation.27 | convolution fusion | flops 4831838208 | bytes 13107200 | tf_op jit(solution)/shard_map/dot_general | solution.py:355
  113.5 10.0 %scatter_custom_fusion.1 = f32[3072,384]{1,0:T(8,128)} fusion(s32[1536]{0:T(1024)S(1)} %fusion.26, f32[1536,384]{1,0:T(8,128)} %bitcast.83, f32[]{:T(128)} %constant.11.clone.1), kind=kCustom, calls=%fused_computation.9 | custom fusion | bytes 4719104 | tf_op jit(solution)/shard_map/scatter | solution.py:394
  123.6 7.9 %reshape.134 = f32[32,8,4,3,384]{4,3,2,1,0:T(4,128)} reshape(f32[3072,384]{1,0:T(8,128)} %scatter_custom_fusion.1) | data formatting | bytes 9437184 | tf_op jit(solution)/shard_map/reshape | solution.py:395
  131.4 6.9 %copy.55 = f32[32,8,4,3,384]{4,1,3,2,0:T(8,128)} copy(f32[32,8,4,3,384]{4,3,2,1,0:T(4,128)} %reshape.134) | data formatting | bytes 9437184 | tf_op jit(solution)/shard_map/reshape | solution.py:395
  138.3 4.9 all-to-all-start.1
  144.2 106.6 %all-to-all-done.1 = f32[32,8,4,3,384]{4,1,3,2,0:T(8,128)} async-done(((f32[32,8,4,3,384]{4,1,3,2,0:T(8,128)}), f32[32,8,4,3,384]{4,1,3,2,0:T(8,128)}, u32[]{:S(2)}, u32[]{:S(2)}) %all-to-all-start.1) | async-done | bytes 4718624 | tf_op jit(solution)/shard_map/all_to_all | solution.py:398
  250.8 6.7 %copy.67 = f32[8,4,32,3,384]{4,3,2,1,0:T(4,128)} copy(f32[8,4,32,3,384]{4,0,3,1,2:T(8,128)} %bitcast.16) | data formatting | bytes 9437184 | tf_op jit(solution)/shard_map/reshape | solution.py:402
  257.5 8.1 %reshape.166 = f32[32,96,384]{2,1,0:T(8,128)} reshape(f32[8,4,32,3,384]{4,3,2,1,0:T(4,128)} %copy.67) | data formatting | bytes 9437184 | tf_op jit(solution)/shard_map/reshape | solution.py:402
  265.6 5.5 %fusion.33 = (f32[32,96]{1,0:T(8,128)S(1)}, f32[32,96,96]{1,2,0:T(8,128)S(1)}) fusion(f32[32,96,384]{2,1,0:T(8,128)} %reshape.166, pred[32,96]{1,0:T(8,128)(4,1)S(1)} %copy.52), kind=kOutput, calls=%fused_computation.56 | convolution fusion | flops 453866496 | bytes 2767872 | tf_op jit(solution)/shard_map/jvp(nqd,nkd->nqk)/dot_general | solution.py:333
  279.2 4.0 convolution_add_fusion
  283.4 3.6 copy.61
  287.0 4.8 reshape.136
  291.8 7.6 %all-to-all-start.2 = ((f32[32,8,4,3,256]{4,2,1,3,0:T(4,128)}), f32[32,8,4,3,256]{4,2,1,3,0:T(4,128)}, u32[]{:S(2)}, u32[]{:S(2)}) async-start(f32[32,8,4,3,256]{4,2,1,3,0:T(4,128)} %bitcast.74), calls=%async_computation.2 | async-start | bytes 6291456 | tf_op jit(solution)/shard_map/all_to_all | solution.py:410
  299.4 74.9 %all-to-all-done.2 = f32[32,8,4,3,256]{4,2,1,3,0:T(4,128)} async-done(((f32[32,8,4,3,256]{4,2,1,3,0:T(4,128)}), f32[32,8,4,3,256]{4,2,1,3,0:T(4,128)}, u32[]{:S(2)}, u32[]{:S(2)}) %all-to-all-start.2) | async-done | bytes 3145760 | tf_op jit(solution)/shard_map/all_to_all | solution.py:410
  374.2 6.5 %copy.62 = f32[32,8,4,3,256]{4,3,2,1,0:T(4,128)} copy(f32[32,8,4,3,256]{4,2,1,3,0:T(4,128)} %all-to-all-done.2) | data formatting | bytes 6291456 | tf_op jit(solution)/shard_map/all_to_all | solution.py:410
  380.8 5.9 %reshape.137 = f32[3072,256]{1,0:T(8,128)} reshape(f32[32,8,4,3,256]{4,3,2,1,0:T(4,128)} %copy.62) | data formatting | bytes 6291456 | tf_op jit(solution)/shard_map/reshape | solution.py:411
  386.7 6.6 %gather_fusion = f32[1536,256]{1,0:T(8,128)} fusion(f32[3072,256]{1,0:T(8,128)} %reshape.137, s32[2048]{0:T(1024)S(1)} %pad_clamp_fusion), kind=kCustom, calls=%fused_computation | custom fusion | bytes 3151872 | tf_op jit(solution)/shard_map/gather | solution.py:411
  400.5 14.2 %fusion.21.terms_ref = f32[384,2048]{1,0:T(8,128)} fusion(f32[2048,1024]{1,0:T(8,128)} %bitcast.72, f32[384,512]{0,1:T(8,128)} %bitcast.77, f32[384,512]{0,1:T(8,128)} %bitcast.75), kind=kOutput, calls=%fused_computation.35 | convolution fusion | flops 4832231424 | bytes 13107200 | tf_op jit(solution)/shard_map/dot_general | solution.py:359
  414.6 9.2 %convolution_bitcast_fusion = f32[2048,1024]{0,1:T(8,128)} fusion(f32[1,384,2048]{2,1,0:T(8,128)S(1)} %copy-done, f32[384,512]{0,1:T(8,128)S(1)} %bitcast.78, f32[384,512]{0,1:T(8,128)S(1)} %bitcast.76), kind=kOutput, calls=%fused_computation.3 | convolution fusion | flops 4832231424 | bytes 13107200 | tf_op jit(solution)/shard_map/dot_general | solution.py:365
  423.8 9.3 %copy.65 = f32[2048,1024]{1,0:T(8,128)} copy(f32[2048,1024]{0,1:T(8,128)} %convolution_bitcast_fusion) | data formatting | bytes 16777216 | tf_op jit(solution)/shard_map/dot_general | solution.py:365
  435.0 50.0 %scatter_sums.1 = (f32[384,512]{1,0:T(8,128)S(1)}, f32[32,512]{1,0:T(8,128)S(1)}, f32[32,512]{1,0:T(8,128)S(1)}) custom-call(f32[384,2048]{1,0:T(8,128)S(1)} %copy-done.1, f32[2,4,8,32,1024]{4,3,2,1,0:T(8,128)} %bitcast.73), custom_call_target="tpu_custom_call" | custom-call | tf_op jit(solution)/shard_map/scatter_sums/pallas_call | solution.py:305
  (54 shorter events, 40.1 us)
Async XLA Ops:
  0.6 91.5 %copy-start = (f32[1,384,2048]{2,1,0:T(8,128)S(1)}, f32[1,384,2048]{2,1,0:T(8,128)}, u32[]{:S(2)}) copy-start(f32[1,384,2048]{2,1,0:T(8,128)} %param.5) | copy-start | bytes 9437188
  4.0 1.4 copy-start.3
  18.5 119.9 %all-to-all-start = ((f32[32,8,4,3]{1,2,3,0:T(4,128)}), f32[32,8,4,3]{1,2,3,0:T(4,128)S(1)}, u32[]{:S(2)}, u32[]{:S(2)}) async-start(f32[32,8,4,3]{1,2,3,0:T(4,128)} %copy.50), calls=%async_computation | async-start | bytes 393216 | tf_op jit(solution)/shard_map/all_to_all | solution.py:399
  107.7 1.1 copy-start.6
  138.3 112.5 %all-to-all-start.1 = ((f32[32,8,4,3,384]{4,1,3,2,0:T(8,128)}), f32[32,8,4,3,384]{4,1,3,2,0:T(8,128)}, u32[]{:S(2)}, u32[]{:S(2)}) async-start(f32[32,8,4,3,384]{4,1,3,2,0:T(8,128)} %copy.55), calls=%async_computation.1 | async-start | bytes 9437184 | tf_op jit(solution)/shard_map/all_to_all | solution.py:398
  265.6 5.9 %copy-start.2 = (f32[32,96,384]{2,1,0:T(8,128)S(1)}, f32[32,96,384]{2,1,0:T(8,128)}, u32[]{:S(2)}) copy-start(f32[32,96,384]{2,1,0:T(8,128)} %reshape.166) | copy-start | bytes 14155780
  291.8 82.5 %all-to-all-start.2 = ((f32[32,8,4,3,256]{4,2,1,3,0:T(4,128)}), f32[32,8,4,3,256]{4,2,1,3,0:T(4,128)}, u32[]{:S(2)}, u32[]{:S(2)}) async-start(f32[32,8,4,3,256]{4,2,1,3,0:T(4,128)} %bitcast.74), calls=%async_computation.2 | async-start | bytes 6291456 | tf_op jit(solution)/shard_map/all_to_all | solution.py:410
  400.5 14.2 %copy-start.4 = (f32[4,384,128]{1,2,0:T(8,128)S(1)}, f32[4,384,128]{1,2,0:T(8,128)}, u32[]{:S(2)}) copy-start(f32[4,384,128]{1,2,0:T(8,128)} %copy.70) | copy-start | bytes 2359300
  400.5 14.2 %copy-start.5 = (f32[4,384,128]{1,2,0:T(8,128)S(1)}, f32[4,384,128]{1,2,0:T(8,128)}, u32[]{:S(2)}) copy-start(f32[4,384,128]{1,2,0:T(8,128)} %copy.71) | copy-start | bytes 2359300
  433.1 1.9 copy-start.1

commit v2 on v1

--- a/solution.py
+++ b/solution.py
@@ -14,8 +14,7 @@
 MESH = pl.DeviceIdType.MESH
 
 masked_score = -1e30
-exact = lax.Precision.HIGHEST
-split = lax.Precision.HIGH
+ROOM = 64
 
 
 def position():
@@ -301,7 +300,6 @@
     length = token_terms.shape[0]
     both = weight_terms.shape[1]
     width = both // 2
-    f32 = jnp.float32
     return pl.pallas_call(
         scatter_kernel,
         out_shape=(
@@ -329,91 +327,268 @@
     )(token_terms, weight_terms.reshape(2, NY, NZ, ROWS, both))
 
 
-def attend_blocks(query_key, values, validity):
-    scores = jnp.einsum("nqd,nkd->nqk", query_key, query_key, precision=exact) / HD
-    scores = jnp.where(validity[:, None, :] > 0.5, scores, masked_score)
-    highest = lax.stop_gradient(jnp.max(scores, axis=2, keepdims=True))
-    weights = jnp.exp(scores - highest)
-    weights = weights / jnp.sum(weights, axis=2, keepdims=True)
-    return jnp.einsum("nqk,nkd->nqd", weights, values, precision=exact)
-
-
-def cluster_gradients(packed, validity):
-    query_key = packed[:, :, :HD]
-    values = packed[:, :, HD : 2 * HD]
-    upstream = packed[:, :, 2 * HD :]
-
-    def forward(first_part, second_part):
-        return attend_blocks(first_part, second_part, validity)
-
-    attended, pullback = jax.vjp(forward, query_key, values)
-    grad_qk, grad_values = pullback(upstream)
-    return jnp.concatenate([grad_qk, grad_values], axis=2)
-
-
-def matmul(left, right):
-    return jnp.dot(left, right, precision=split, preferred_element_type=jnp.float32)
-
-
-def matmul_nt(left, right):
-    return lax.dot_general(
-        left, right, (((1,), (1,)), ((), ())), precision=split, preferred_element_type=jnp.float32
+LANES = 128
+GROUP = 8
+SLOTS = 96
+TALL = 768
+MIXERS = (1, 77, 181, 111)
+f32, bf16 = jnp.float32, jnp.bfloat16
+NN = (((1,), (0,)), ((), ()))
+NT = (((1,), (1,)), ((), ()))
+TN = (((0,), (0,)), ((), ()))
+BIG = 48 * 2**20
+
+
+def dot(left, right, dims=NN):
+    return lax.dot_general(left, right, dims, preferred_element_type=f32)
+
+
+def halves(matrix):
+    upper = matrix.astype(bf16)
+    return upper, (matrix - upper.astype(f32)).astype(bf16)
+
+
+def dot3(left, right, dims=NN):
+    a, b = left
+    c, d = right
+    first = jnp.concatenate([a, b, a], axis=dims[0][0][0])
+    second = jnp.concatenate([c, c, d], axis=dims[0][1][0])
+    return dot(first, second, dims)
+
+
+def pack_kernel(tokens_ref, full_ref, grad_ref, slots_ref, ids_ref, rows_ref, marks_ref, acc, pay):
+    step = pl.program_id(0)
+    width = grad_ref.shape[1]
+    length = grad_ref.shape[0]
+    rows = rows_ref.shape[0]
+
+    @pl.when(step == 0)
+    def _():
+        acc[...] = jnp.zeros_like(acc)
+
+    @pl.when(step < 8)
+    def _():
+        acc[...] += dot3(halves(tokens_ref[...]), halves(full_ref[...]))
+
+    @pl.when(step == 7)
+    def _():
+        for head in range(width // HD):
+            here = pl.ds(head * length, length)
+            for part, source in enumerate((
+                acc[:, head * HD : (head + 1) * HD],
+                acc[:, width + head * HD : width + (head + 1) * HD],
+                grad_ref[:, head * HD : (head + 1) * HD],
+            )):
+                upper, lower = halves(source)
+                pay[here, part * HD : (part + 1) * HD] = upper
+                pay[here, (3 + part) * HD : (4 + part) * HD] = lower
+
+    @pl.when(step >= 8)
+    def _():
+        place = lax.broadcasted_iota(jnp.int32, (rows, slots_ref.shape[1]), 0) + (step - 8) * rows
+        chosen = (place == slots_ref[...]).astype(f32).astype(bf16)
+        both = dot(chosen, pay[...])
+        rows_ref[...] = both[:, : 3 * HD] + both[:, 3 * HD :]
+        marks_ref[0] = dot(ids_ref[...].astype(bf16), chosen, NT)
+
+
+def pack_rows(inputs, full, upstream, slots, ids, room):
+    length, depth = inputs.shape
+    width = upstream.shape[1]
+    total = slots.shape[1]
+    return pl.pallas_call(
+        pack_kernel,
+        grid=(16,),
+        out_shape=(
+            jax.ShapeDtypeStruct((32 * room, 3 * HD), f32),
+            jax.ShapeDtypeStruct((8, 8, 4 * room), f32),
+        ),
+        in_specs=[
+            pl.BlockSpec((length, depth // 8), lambda i: (0, jnp.minimum(i, 7))),
+            pl.BlockSpec((depth // 8, 2 * width), lambda i: (jnp.minimum(i, 7), 0)),
+            pl.BlockSpec((length, width), lambda i: (0, 0)),
+            pl.BlockSpec((1, total), lambda i: (0, 0)),
+            pl.BlockSpec((8, total), lambda i: (0, 0)),
+        ],
+        out_specs=(
+            pl.BlockSpec((4 * room, 3 * HD), lambda i: (jnp.maximum(i - 8, 0), 0)),
+            pl.BlockSpec((1, 8, 4 * room), lambda i: (jnp.maximum(i - 8, 0), 0, 0)),
+        ),
+        scratch_shapes=[pltpu.VMEM((length, 2 * width), f32), pltpu.VMEM((total, 6 * HD), bf16)],
+        compiler_params=pltpu.CompilerParams(vmem_limit_bytes=BIG),
+        name="project_and_pack",
+    )(inputs, full, upstream, slots, ids)
+
+
+def attend_kernel(marks_ref, rows_ref, replies_ref, spread, seats, valid, answer):
+    groups = marks_ref.shape[0]
+    wide = marks_ref.shape[2]
+    owned = spread.shape[1]
+    seat = spread.shape[2]
+    size = groups * seat
+
+    @pl.loop(0, groups)
+    def _(group):
+        here = pl.ds(pl.multiple_of(group * wide, wide), wide)
+        place = lax.broadcasted_iota(jnp.int32, (TALL, wide), 0)
+        chosen = (place == marks_ref[group]).astype(f32).astype(bf16)
+        seats[group] = chosen
+        upper, lower = halves(rows_ref[here, :])
+        moved = dot(chosen, jnp.concatenate([upper, lower, jnp.ones((wide, LANES), bf16)], axis=1))
+        spread[group] = (moved[:, : 3 * HD] + moved[:, 3 * HD : 6 * HD]).reshape(owned, seat, 3 * HD)
+        valid[group] = moved[:, 6 * HD :].reshape(owned, seat, LANES)
+
+    @pl.loop(0, owned // 4)
+    def _(block):
+        for lane in range(4):
+            index = block * 4 + lane
+            rows = spread[:, index].reshape(size, 3 * HD)
+            present = valid[:, index].reshape(size, LANES)[:, :size] > 0.5
+            qk = halves(rows[:, :HD])
+            value = halves(rows[:, HD : 2 * HD])
+            upstream = halves(rows[:, 2 * HD :])
+            scores = jnp.where(present, dot3(qk, qk, NT) / HD, masked_score)
+            weights = jnp.exp(scores - jnp.max(scores, axis=0, keepdims=True))
+            weights = weights / jnp.sum(weights, axis=0, keepdims=True)
+            slopes = dot3(value, upstream, NT)
+            middle = jnp.sum(weights * slopes, axis=0, keepdims=True)
+            slopes = weights * (slopes - middle)
+            grad_qk = dot3(halves(slopes + slopes.T), qk) / HD
+            grad_value = dot3(halves(weights), upstream)
+            answer[:, index] = jnp.concatenate([grad_qk, grad_value], axis=1).reshape(
+                groups, seat, 2 * HD
+            )
+
+    @pl.loop(0, groups)
+    def _(group):
+        here = pl.ds(pl.multiple_of(group * wide, wide), wide)
+        upper, lower = halves(answer[group].reshape(TALL, 2 * HD))
+        moved = dot(seats[group], jnp.concatenate([upper, lower], axis=1), TN)
+        replies_ref[here, :] = moved[:, : 2 * HD] + moved[:, 2 * HD :]
+
+
+def attend(rows, marks, room):
+    groups = 32 // GROUP
+    owned = TALL // (3 * GROUP)
+    seat = 3 * GROUP
+    return pl.pallas_call(
+        attend_kernel,
+        out_shape=jax.ShapeDtypeStruct((32 * room, 2 * HD), f32),
+        in_specs=[pl.BlockSpec(memory_space=pltpu.VMEM)] * 2,
+        out_specs=pl.BlockSpec(memory_space=pltpu.VMEM),
+        scratch_shapes=[
+            pltpu.VMEM((groups, owned, seat, 3 * HD), f32),
+            pltpu.VMEM((groups, TALL, GROUP * room), bf16),
+            pltpu.VMEM((groups, owned, seat, LANES), f32),
+            pltpu.VMEM((groups, owned, seat, 2 * HD), f32),
+        ],
+        compiler_params=pltpu.CompilerParams(vmem_limit_bytes=BIG),
+        name="attend",
+    )(marks, rows)
+
+
+def grads_kernel(returned_ref, slots_ref, tokens_ref, full_ref, terms_ref, sums_ref, high, low):
+    length = tokens_ref.shape[0]
+    width = high.shape[1] // 2
+    total = returned_ref.shape[0]
+
+    @pl.when(pl.program_id(0) == 0)
+    def _():
+        upper, lower = halves(returned_ref[...])
+        source = jnp.concatenate([upper, lower], axis=1)
+        for head in range(width // HD):
+            place = lax.broadcasted_iota(jnp.int32, (length, total), 1)
+            chosen = (place == slots_ref[:, head : head + 1]).astype(f32).astype(bf16)
+            both = dot(chosen, source)
+            upper, lower = halves(both[:, : 2 * HD] + both[:, 2 * HD :])
+            for part in range(2):
+                there = pl.ds(part * width + head * HD, HD)
+                high[:, there] = upper[:, part * HD : (part + 1) * HD]
+                low[:, there] = lower[:, part * HD : (part + 1) * HD]
+
+    combined = high[...], low[...]
+    terms_ref[...] = dot3(combined, halves(full_ref[...]), NT)
+    sums_ref[...] = dot3(halves(tokens_ref[...]), combined, TN)
+
+
+def local_grads(returned, slots, inputs, full):
+    length, depth = inputs.shape
+    both = full.shape[1]
+    total = returned.shape[0]
+    return pl.pallas_call(
+        grads_kernel,
+        grid=(8,),
+        out_shape=(
+            jax.ShapeDtypeStruct((length, depth), f32),
+            jax.ShapeDtypeStruct((depth, both), f32),
+        ),
+        in_specs=[
+            pl.BlockSpec((total, 2 * HD), lambda i: (0, 0)),
+            pl.BlockSpec(slots.shape, lambda i: (0, 0)),
+            pl.BlockSpec((length, depth // 8), lambda i: (0, i)),
+            pl.BlockSpec((depth // 8, both), lambda i: (i, 0)),
+        ],
+        out_specs=(
+            pl.BlockSpec((length, depth // 8), lambda i: (0, i)),
+            pl.BlockSpec((depth // 8, both), lambda i: (i, 0)),
+        ),
+        scratch_shapes=[pltpu.VMEM((length, both), bf16)] * 2,
+        compiler_params=pltpu.CompilerParams(vmem_limit_bytes=BIG),
+        name="unpack_and_grads",
+    )(returned, slots, inputs, full)
+
+
+def exchange(array):
+    return lax.all_to_all(array, "ctx", split_axis=0, concat_axis=0, tiled=True)
+
+
+def middle_part(room, inputs, full, upstream, owner, rank, ids):
+    heads_here, length = owner.shape
+    slots = owner * room + rank
+    rows, marks = pack_rows(
+        inputs, full, upstream, slots.reshape(1, -1),
+        jnp.broadcast_to((ids + 1).astype(f32).reshape(1, -1), (8, ids.size)), room,
     )
-
-
-def matmul_tn(left, right):
-    return lax.dot_general(
-        left, right, (((0,), (0,)), ((), ())), precision=split, preferred_element_type=jnp.float32
-    )
+    marks = exchange(marks[:, 0, :].reshape(32, room))
+    rows = exchange(rows.reshape(32, room, 3 * HD)).reshape(32 * room, 3 * HD)
+    marks = marks.astype(jnp.int32) - 1
+    source = lax.broadcasted_iota(jnp.int32, marks.shape, 0) % GROUP
+    seats = (marks // 3) * (3 * GROUP) + source * 3 + marks % 3
+    seats = jnp.where(marks < 0, -1, seats).reshape(32 // GROUP, 1, GROUP * room)
+    replies = attend(rows, seats, room)
+    returned = exchange(replies.reshape(32, room, 2 * HD)).reshape(32 * room, 2 * HD)
+    return local_grads(returned, slots.T, inputs, full)
 
 
 def per_device(tokens, qk_weight, value_weight, grad_out, assign):
     inputs = tokens[0]
     length = inputs.shape[0]
-    ctx_count = lax.axis_size("ctx")
-    clusters = CL_DEV * ctx_count
-    per_source = 2 * length // clusters
+    clusters = CL_DEV * lax.axis_size("ctx")
     heads_here = qk_weight.shape[1] // HD
     width = heads_here * HD
-    routing = assign[:, 0, :, 0]
+    mixers = jnp.asarray(MIXERS, jnp.int32)[:, None]
+    cluster = (assign[:, 0, :, 0] * mixers) % clusters
+    owner = cluster // CL_DEV
+    order = jnp.arange(length, dtype=jnp.int32)
+    earlier = order[:, None] < order[None, :]
+    within = jnp.sum(
+        ((cluster[:, :, None] == cluster[:, None, :]) & earlier).astype(jnp.int32), axis=1
+    )
+    flat = owner.reshape(-1)
+    order = jnp.arange(flat.size, dtype=jnp.int32)
+    earlier = order[:, None] < order[None, :]
+    rank = jnp.sum(((flat[:, None] == flat[None, :]) & earlier).astype(jnp.int32), axis=0)
+    rank = rank.reshape(owner.shape)
+    head_ids = jnp.arange(heads_here, dtype=jnp.int32)[:, None]
+    ids = (head_ids * CL_DEV + cluster % CL_DEV) * 3 + within
+    fullest = lax.pmax(jnp.max(rank) + 1, ("rep", "ctx", "tp"))
     full = gather_weights(qk_weight, value_weight).reshape(-1, 2 * width)
-    projected = matmul(inputs, full)
-
-    def by_head(matrix):
-        return matrix.reshape(length, heads_here, HD).transpose(1, 0, 2)
-
-    payload = jnp.concatenate(
-        [by_head(projected[:, :width]), by_head(projected[:, width:]), by_head(grad_out[0])], axis=2
+    token_terms, weight_terms = lax.cond(
+        fullest <= ROOM,
+        lambda *operands: middle_part(ROOM, *operands),
+        lambda *operands: middle_part(SLOTS, *operands),
+        inputs, full, grad_out[0], owner, rank, ids,
     )
-    labels = jnp.arange(clusters, dtype=jnp.int32)
-    onehot_table = (routing[:, :, None] == labels[None, None, :]).astype(jnp.int32)
-    within = jnp.sum((jnp.cumsum(onehot_table, axis=1) - 1) * onehot_table, axis=2)
-    head_ids = jnp.arange(heads_here, dtype=jnp.int32)[:, None]
-    slots = ((routing * heads_here + head_ids) * per_source + within).reshape(-1)
-    total = clusters * heads_here * per_source
-    outgoing = jnp.zeros((total, 3 * HD), jnp.float32).at[slots].set(payload.reshape(-1, 3 * HD))
-    outgoing = outgoing.reshape(ctx_count, CL_DEV, heads_here, per_source, 3 * HD)
-    marks = jnp.zeros((total,), jnp.float32).at[slots].set(1.0)
-    marks = marks.reshape(ctx_count, CL_DEV, heads_here, per_source)
-    rows_in = lax.all_to_all(outgoing, "ctx", split_axis=0, concat_axis=0, tiled=True)
-    marks_in = lax.all_to_all(marks, "ctx", split_axis=0, concat_axis=0, tiled=True)
-    owned = rows_in.shape[1]
-    senders = rows_in.shape[0]
-    packed = rows_in.transpose(1, 2, 0, 3, 4).reshape(
-        owned * heads_here, senders * per_source, 3 * HD
-    )
-    validity = marks_in.transpose(1, 2, 0, 3).reshape(owned * heads_here, senders * per_source)
-    gradients = cluster_gradients(packed, validity)
-    replies = gradients.reshape(owned, heads_here, senders, per_source, 2 * HD).transpose(
-        2, 0, 1, 3, 4
-    )
-    returned = lax.all_to_all(replies, "ctx", split_axis=0, concat_axis=0, tiled=True)
-    picked = returned.reshape(total, 2 * HD)[slots].reshape(heads_here, length, 2 * HD)
-    grad_qk = picked[:, :, :HD].transpose(1, 0, 2).reshape(length, width)
-    grad_values = picked[:, :, HD:].transpose(1, 0, 2).reshape(length, width)
-    combined = jnp.concatenate([grad_qk, grad_values], axis=1)
-    token_terms = matmul_nt(combined, full)
-    weight_terms = matmul_tn(inputs, combined)
     grad_tokens, grad_qk_weight, grad_value_weight = scatter_sums(token_terms, weight_terms)
     return (grad_tokens[None], grad_qk_weight, grad_value_weight)
 

time: 493 us -> 416 us (0.84)
  blocking collectives: 0 us -> 150 us
  waiting for transfers between devices: 181 us -> 73.2 us
  local copies, waits for them, and re-layouts: 108 us -> 11.5 us
  matrix products: 56.1 us -> 0 us
  Pallas kernels: 109 us -> 160 us
  starting transfers between devices: 24.4 us -> 4.07 us
  other arithmetic: 6.58 us -> 13.2 us
    all_to_all x3 -> x1, waiting for transfers between devices: 181 us -> 73.2 us  [exchange(): return lax.all_to_all(array, 'ctx', split_axis=0, concat_axis=0, tiled=True)]
    pmax x0 -> x1, blocking collectives: none -> 78.7 us  [per_device(): fullest = lax.pmax(jnp.max(rank) + 1, ('rep', 'ctx', 'tp'))]
    all_to_all x0 -> x2, blocking collectives: none -> 71.2 us  [exchange(): return lax.all_to_all(array, 'ctx', split_axis=0, concat_axis=0, tiled=True)]
    pallas_call x0 -> x3, Pallas kernels: none -> 56.8 us  [the longest x1 20.9 us: attend(): pl.pallas_call(attend_kernel, out_shape=jax.ShapeDtypeStruct((32 * room,...]
    dot_general x8 -> x0, matrix products: 56.1 us -> none  [the longest x1 15.6 us: matmul(): jnp.dot(left, right, precision=split, preferred_element_type=jnp.float32)]
    reshape x8 -> x2, local copies, waits for them, and re-layouts: 44.2 us -> 1.02 us  [per_device(): rank = rank.reshape(owner.shape)]
    all_to_all x3 -> x1, starting transfers between devices: 24.4 us -> 4.07 us  [exchange(): return lax.all_to_all(array, 'ctx', split_axis=0, concat_axis=0, tiled=True)]
    scatter x2 -> x0, local copies, waits for them, and re-layouts: 16.2 us -> none  [the longest x1 10 us: per_device(): jnp.zeros((total, 3 * HD), jnp.float32).at[slots]]
  transfers between devices with their start and end apart: 3 -> 1, of which waited for: 2 -> 1; matrix products, arithmetic and copies ran while one was open for 10% -> 0% of each run, Pallas kernels for 12% -> 0%
where the time goes in v2:
time: 416 us; the launch traced here: 414 us
  Pallas kernels  160 us (38%)
  blocking collectives  150 us (36%)
  waiting for transfers between devices  73.2 us (18%)
  other arithmetic  13.2 us (3%)
  local copies, waits for them, and re-layouts  11.5 us (3%)
    pmax x1, blocking collectives, per_device(): fullest = lax.pmax(jnp.max(rank) + 1, ('rep', 'ctx', 'tp'))  78.7 us
    all_to_all x1, waiting for transfers between devices, exchange(): return lax.all_to_all(array, 'ctx', split_axis=0, concat_axis=0, tiled=True)  73.2 us
    all_to_all x2, blocking collectives, exchange(): return lax.all_to_all(array, 'ctx', split_axis=0, concat_axis=0, tiled=True)  71.2 us
    pallas_call x1, Pallas kernels, gather_weights(): pl.pallas_call(gather_kernel, out_shape=jax.ShapeDtypeStruct((2, NY, NZ,...  56.5 us
    pallas_call x1, Pallas kernels, scatter_sums(): pl.pallas_call(scatter_kernel, out_shape=(jax.ShapeDtypeStruct((length, w...  46.5 us
    pallas_call x1, Pallas kernels, attend(): pl.pallas_call(attend_kernel, out_shape=jax.ShapeDtypeStruct((32 * room,...  20.9 us
    pallas_call x1, Pallas kernels, pack_rows(): pl.pallas_call(pack_kernel, grid=(16,), out_shape=(jax.ShapeDtypeStruct((...  18.1 us
    pallas_call x1, Pallas kernels, local_grads(): pl.pallas_call(grads_kernel, grid=(8,), out_shape=(jax.ShapeDtypeStruct((...  17.8 us
  transfers between devices with their start and end apart: 1, of which 1 were waited for; matrix products, arithmetic and copies ran while one was open for 0% of the time, Pallas kernels for 0%

profile of v2, /device:TPU:2, one launch (start us, length us, event | category | flops | bytes accessed | tf_op | source)
XLA Modules:
  0.0 413.8 jit_solution(16923047954777884243)
XLA Ops:
  0.6 0.7 mul.97.clone
  2.1 1.9 convert_reduce_fusion
  5.3 78.7 %pmax.7 = s32[]{:T(128)} all-reduce(s32[]{:T(128)S(6)} %add.208), channel_id=1, replica_groups=mesh['rep'=2,'ctx'=32,'tp'=4] {'rep','ctx','tp'}, use_global_device_ids=true, to_apply=%region_2.3 | all-reduce | flops 1 | bytes 8 | tf_op jit(solution)/shard_map/pmax | solution.py:584
  84.7 0.8 copy.91
  85.5 1.5 negate_select_fusion.2
  87.8 0.8 negate_select_fusion.3
  88.5 1.7 and_convert_fusion
  90.3 56.5 %gather_weights.1 = f32[2,4,8,32,1024]{4,3,2,1,0:T(8,128)} custom-call(f32[32,512]{1,0:T(8,128)} %qk_ref.1, f32[32,512]{1,0:T(8,128)} %value_ref.1), custom_call_target="tpu_custom_call" | custom-call | tf_op jit(solution)/shard_map/gather_weights/pallas_call | solution.py:133
  148.8 216.3 %conditional.1 = (f32[384,2048]{1,0:T(8,128)}, f32[2,4,8,32,1024]{4,3,2,1,0:T(8,128)S(1)}) conditional(s32[]{:T(128)} %convert_element_type.38, (f32[1,384,2048]{2,1,0:T(8,128)S(1)}, f32[2,4,8,32,1024]{4,3,2,1,0:T(8,128)}, f32[1,384,512]{2,1,0:T(8,128)}, s32[4,384]{0,1:T(8,128)S(1)}, s32[4,384]{0,1:T(8,128)}, /*index=5*/pred[4,384]{0,1:T(8,128)(4,1)}, ...), branch_computations={%region_3.5_spmd, %region_5.7_spmd} | conditional | flops 689988 | bytes 54182136 | solution.py:586
  148.8 1.0 copy.81
  149.9 2.3 fusion.12
  152.2 1.0 copy.83
  153.3 1.8 reduce_sum.21
  156.0 1.0 copy.86
  157.0 18.1 %project_and_pack.3 = (f32[2048,384]{1,0:T(8,128)S(1)}, f32[8,8,256]{2,1,0:T(8,128)S(1)}) custom-call(f32[384,2048]{1,0:T(8,128)S(1)} %bitcast.56, f32[2048,1024]{1,0:T(8,128)} %bitcast.52, f32[384,512]{1,0:T(8,128)} %bitcast.61, s32[1,1536]{1,0:T(1,128)S(1)} %bitcast.49, f32[8,1536]{1,0:T(8,128)S(1)} %broadcast_in_dim.10.ids_ref), custom_call_target="tpu_custom_call" | custom-call | tf_op jit(solution)/shard_map/cond/branch_1_fun/project_and_pack/pallas_call | solution.py:399
  175.2 1.7 copy-done.1
  177.0 15.6 %all_to_all.32 = f32[32,1,64]{2,1,0:T(1,128)S(1)} all-to-all(f32[32,1,64]{2,1,0:T(1,128)S(1)} %bitcast.63), channel_id=1, replica_groups=mesh['rep'=2,'ctx'=32,'tp'=4] {'ctx'}, dimensions={0} | all-to-all | bytes 16384 | tf_op jit(solution)/shard_map/cond/branch_1_fun/all_to_all | solution.py:542
  192.6 4.1 all-to-all-start.4
  197.5 73.2 %all-to-all-done.4 = f32[32,64,384]{2,1,0:T(8,128)S(1)} async-done(((f32[32,64,384]{2,1,0:T(8,128)}), f32[32,64,384]{2,1,0:T(8,128)S(1)}, u32[]{:S(2)}, u32[]{:S(2)}) %all-to-all-start.4) | async-done | bytes 3145760 | tf_op jit(solution)/shard_map/cond/branch_1_fun/all_to_all | solution.py:542
  270.7 20.9 %attend.3 = f32[2048,256]{1,0:T(8,128)S(1)} custom-call(s32[4,1,512]{2,1,0:T(1,128)S(1)} %fusion.15.marks_ref, f32[2048,384]{1,0:T(8,128)S(1)} %bitcast.39), custom_call_target="tpu_custom_call" | custom-call | tf_op jit(solution)/shard_map/cond/branch_1_fun/attend/pallas_call | solution.py:474
  291.6 55.6 %all_to_all.33 = f32[32,64,256]{2,1,0:T(8,128)S(1)} all-to-all(f32[32,64,256]{2,1,0:T(8,128)S(1)} %bitcast.41), channel_id=1, replica_groups=mesh['rep'=2,'ctx'=32,'tp'=4] {'ctx'}, dimensions={0} | all-to-all | bytes 4194304 | tf_op jit(solution)/shard_map/cond/branch_1_fun/all_to_all | solution.py:542
  347.3 17.8 %unpack_and_grads.3 = (f32[384,2048]{1,0:T(8,128)}, f32[2048,1024]{1,0:T(8,128)S(1)}) custom-call(f32[2048,256]{1,0:T(8,128)S(1)} %bitcast.42, s32[384,4]{1,0:T(8,128)S(1)} %bitcast.46, f32[384,2048]{1,0:T(8,128)S(1)} %bitcast.57, f32[2048,1024]{1,0:T(8,128)} %bitcast.53), custom_call_target="tpu_custom_call" | custom-call | tf_op jit(solution)/shard_map/cond/branch_1_fun/unpack_and_grads/pallas_call | solution.py:518
  365.1 46.5 %scatter_sums.1 = (f32[384,512]{1,0:T(8,128)S(1)}, f32[32,512]{1,0:T(8,128)S(1)}, f32[32,512]{1,0:T(8,128)S(1)}) custom-call(f32[384,2048]{1,0:T(8,128)} %get-tuple-element.181.terms_ref, f32[2,4,8,32,1024]{4,3,2,1,0:T(8,128)S(1)} %get-tuple-element.182.sums_ref), custom_call_target="tpu_custom_call" | custom-call | tf_op jit(solution)/shard_map/scatter_sums/pallas_call | solution.py:303
  411.6 0.9 copy.103
  (43 shorter events, 7.5 us)
Async XLA Ops:
  90.3 58.6 %copy-start.2 = (f32[1,384,2048]{2,1,0:T(8,128)S(1)}, f32[1,384,2048]{2,1,0:T(8,128)}, u32[]{:S(2)}) copy-start(f32[1,384,2048]{2,1,0:T(8,128)} %param.8) | copy-start | bytes 9437188
  148.8 26.3 %copy-start.3 = (f32[1,384,2048]{2,1,0:T(8,128)}, f32[1,384,2048]{2,1,0:T(8,128)S(1)}, u32[]{:S(2)}) copy-start(f32[1,384,2048]{2,1,0:T(8,128)S(1)} %get-tuple-element.155) | copy-start | bytes 9437188 | tf_op jit(solution)/shard_map/cond
  175.2 1.7 copy-start.1
  192.6 78.1 %all-to-all-start.4 = ((f32[32,64,384]{2,1,0:T(8,128)}), f32[32,64,384]{2,1,0:T(8,128)S(1)}, u32[]{:S(2)}, u32[]{:S(2)}) async-start(f32[32,64,384]{2,1,0:T(8,128)} %bitcast.44), calls=%async_computation.4 | async-start | bytes 6291456 | tf_op jit(solution)/shard_map/cond/branch_1_fun/all_to_all | solution.py:542
  291.6 55.6 %copy-start.4 = (f32[1,384,2048]{2,1,0:T(8,128)S(1)}, f32[1,384,2048]{2,1,0:T(8,128)}, u32[]{:S(2)}) copy-start(f32[1,384,2048]{2,1,0:T(8,128)} %copy-done.3) | copy-start | bytes 9437188 | tf_op jit(solution)/shard_map/cond

commit v3 on v2

--- a/solution.py
+++ b/solution.py
@@ -14,7 +14,33 @@
 MESH = pl.DeviceIdType.MESH
 
 masked_score = -1e30
-ROOM = 64
+ROOM = 56
+LANES = 128
+GROUP = 8
+SLOTS = 96
+TALL = 768
+f32, bf16 = jnp.float32, jnp.bfloat16
+NN = (((1,), (0,)), ((), ()))
+NT = (((1,), (1,)), ((), ()))
+TN = (((0,), (0,)), ((), ()))
+BIG = 48 * 2**20
+
+
+def dot(left, right, dims=NN):
+    return lax.dot_general(left, right, dims, preferred_element_type=f32)
+
+
+def halves(matrix):
+    upper = matrix.astype(bf16)
+    return upper, (matrix - upper.astype(f32)).astype(bf16)
+
+
+def dot3(left, right, dims=NN):
+    a, b = left
+    c, d = right
+    first = jnp.concatenate([a, b, a], axis=dims[0][0][0])
+    second = jnp.concatenate([c, c, d], axis=dims[0][1][0])
+    return dot(first, second, dims)
 
 
 def position():
@@ -54,11 +80,70 @@
 
 
 GATHER_COPIES = 3 + 7 + 7 + 3 + 8 + 4
-
-
-def gather_kernel(qk_ref, value_ref, out_ref, local_sem, send_sem, recv_sem):
+ROUTE_COPIES = 3 + 7 + 3 + 1
+CLUSTERS = 256
+OWNERS = 32
+PITCH = 64
+
+
+def count_rows(cluster_ref, heads):
+    length = cluster_ref.shape[1]
+    line = lax.broadcasted_iota(jnp.int32, (8, length), 0)
+    counts = jnp.zeros((8, CLUSTERS), f32)
+    for head in range(heads):
+        counts += dot(one(line == head), members(cluster_ref, head), NT)
+    return counts
+
+
+def one(condition):
+    return jnp.where(condition, 1.0, 0.0).astype(bf16)
+
+
+def members(cluster_ref, head):
+    length = cluster_ref.shape[1]
+    label = lax.broadcasted_iota(jnp.int32, (CLUSTERS, length), 0)
+    return one(label == cluster_ref[head : head + 1, :])
+
+
+def deal_order(counts):
+    lane = lax.broadcasted_iota(jnp.int32, counts.shape, 1)
+    return counts * CLUSTERS + (CLUSTERS - 1 - lane).astype(f32)
+
+
+def route_head(cluster_ref, head, keys, tall_keys, earlier, base):
+    larger = jnp.where(tall_keys[:, head : head + 1] > keys[head : head + 1, :], 1.0, 0.0)
+    place = jnp.sum(larger, axis=0, keepdims=True).astype(jnp.int32)
+    turn = place // OWNERS
+    seat = place % OWNERS
+    seat = jnp.where(turn % 2 == 0, seat, OWNERS - 1 - seat)
+    seat = (seat + 8 * head) % OWNERS
+    line = lax.broadcasted_iota(jnp.int32, (8, CLUSTERS), 0)
+    table = jnp.where(line == 0, seat, jnp.where(line == 1, turn, 0)).astype(f32).astype(bf16)
+    chosen = members(cluster_ref, head)
+    looked = dot(table, chosen).astype(jnp.int32)
+    owner, turn = looked[0:1, :], looked[1:2, :]
+    within = jnp.sum(chosen.astype(f32) * dot(chosen, earlier), axis=0, keepdims=True)
+    label = lax.broadcasted_iota(jnp.int32, (OWNERS, owner.shape[1]), 0)
+    owned = one(label == owner)
+    many = owned.astype(f32)
+    rank = jnp.sum(many * (dot(owned, earlier) + base), axis=0, keepdims=True)
+    base = base + jnp.sum(many, axis=1, keepdims=True)
+    ids = (head * CL_DEV + turn) * 3 + within.astype(jnp.int32)
+    return owner, rank.astype(jnp.int32), ids, base
+
+
+def gather_kernel(
+    qk_ref, value_ref, cluster_ref, grad_ref,
+    out_ref, early_ref, slots_ref,
+    counts_y, counts_z, most, ids_row, slots_row, pay, early_out,
+    local_sem, send_sem, recv_sem, route_send, route_recv, early_send, early_recv,
+):
     rep, y, z = position()
+    me = lax.axis_index("ctx")
+    x = lax.axis_index("tp")
     width = qk_ref.shape[1]
+    heads = width // HD
+    length = cluster_ref.shape[1]
 
     def along_y(step):
         return {"ctx": lax.rem(y + step, NY) * NZ + z}
@@ -66,6 +151,12 @@
     def along_z(step):
         return {"ctx": y * NZ + lax.rem(z + step, NZ)}
 
+    def along_x(step):
+        return {"tp": lax.rem(x + step, 4)}
+
+    def around(step):
+        return {"ctx": lax.rem(me + step, OWNERS)}
+
     def plane(step):
         return out_ref.at[rep, :, lax.rem(z + step, NZ), pl.ds(0, HALF), :]
 
@@ -76,24 +167,50 @@
         return out_ref.at[rep, lax.rem(y + step, NY), :, pl.ds(HALF, HALF), :]
 
     right, left, other = along_z(1), along_z(NZ - 1), {"rep": 1 - rep}
-    greet([along_y(1), along_y(2), along_y(3), right, left, other])
-    copies = Copies(send_sem, recv_sem)
     mine = out_ref.at[rep, y, z]
     first = pltpu.make_async_copy(qk_ref, mine.at[:, pl.ds(0, width)], local_sem.at[0])
     second = pltpu.make_async_copy(value_ref, mine.at[:, pl.ds(width, width)], local_sem.at[1])
     first.start()
     second.start()
+    barrier = pltpu.get_barrier_semaphore()
+
+    @pl.loop(1, OWNERS)
+    def _(step):
+        pl.semaphore_signal(barrier, inc=1, device_id=around(step), device_id_type=MESH)
+
+    for partner in (other, along_x(1), along_x(2), along_x(3)):
+        pl.semaphore_signal(barrier, inc=1, device_id=partner, device_id_type=MESH)
+    counts_y[0] = count_rows(cluster_ref, heads)
+    pl.semaphore_wait(barrier, OWNERS - 1 + 4)
+
+    routes = Copies(route_send, route_recv)
+    counted = [
+        routes.start(counts_y.at[0], counts_y.at[step], along_y(step)) for step in (1, 2, 3)
+    ]
     first.wait()
     second.wait()
-
+    copies = Copies(send_sem, recv_sem)
     own = out_ref.at[rep, y, z, pl.ds(0, HALF), :]
     shared = [copies.start(own, own, along_y(step)) for step in (1, 3, 2)]
     pieces = [(copies.start(piece(0), piece(0), right), copies.start(piece(0), piece(0), left))]
+
+    for head in range(heads):
+        upper, lower = halves(grad_ref[:, head * HD : (head + 1) * HD])
+        pay[pl.ds(head * length, length), :HD] = upper
+        pay[pl.ds(head * length, length), HD:] = lower
+
+    for copy in counted:
+        copy.wait_recv()
+    counts_z[0] = counts_y[0] + counts_y[1] + counts_y[2] + counts_y[3]
+    counted = [
+        routes.start(counts_z.at[0], counts_z.at[step], along_z(step)) for step in range(1, NZ)
+    ]
     for copy in shared:
         copy.wait_recv()
     planes = [(copies.start(plane(0), plane(0), right), copies.start(plane(0), plane(0), left))]
     across = [copies.start(plane(0), plane(0), other)]
-    for step in range(4):
+
+    def turn_pieces(step):
         rightward, leftward = pieces[step]
         rightward.wait_recv()
         if leftward is not None:
@@ -104,45 +221,151 @@
                 copies.start(after, after, right),
                 copies.start(before, before, left) if step < 2 else None,
             ))
-    lines = [copies.start(line(0), line(0), along_y(step)) for step in (1, 3, 2)]
-    across.append(copies.start(line(0), line(0), other))
-    for step in range(4):
+
+    def turn_planes(step):
         rightward, leftward = planes[step]
         after, before = plane(NZ - 1 - step), plane(1 + step)
         rightward.wait_recv()
         if step < 3:
             going = copies.start(after, after, right)
-        across.append(copies.start(after, after, other))
         if leftward is not None:
             leftward.wait_recv()
             coming = copies.start(before, before, left) if step < 2 else None
-            across.append(copies.start(before, before, other))
         if step < 3:
             planes.append((going, coming if step < 2 else None))
+        across.append(copies.start(after, after, other))
+        if leftward is not None:
+            across.append(copies.start(before, before, other))
+
+    turn_pieces(0)
+    for copy in counted:
+        copy.wait_recv()
+    total = counts_z[0]
+    for step in range(1, NZ):
+        total += counts_z[step]
+    keys = deal_order(total)
+    tall_keys = jnp.concatenate([keys] + [jnp.zeros_like(keys)] * 15, axis=0).T
+    earlier = one(
+        lax.broadcasted_iota(jnp.int32, (length, length), 0)
+        < lax.broadcasted_iota(jnp.int32, (length, length), 1)
+    )
+    base = jnp.zeros((OWNERS, 1), f32)
+    highest = jnp.zeros((1, 1), f32)
+    slots_ref[...] = jnp.full(slots_ref.shape, -1, jnp.int32)
+    for head in range(heads):
+        owner, rank, ids, base = route_head(cluster_ref, head, keys, tall_keys, earlier, base)
+        highest = jnp.maximum(highest, jnp.max(rank.astype(f32), axis=1, keepdims=True) + 1)
+        slots_ref[head : head + 1, :] = jnp.where(rank < ROOM, owner * ROOM + rank, -1)
+        here = pl.ds(head * length, length)
+        slots_row[:, here] = jnp.where(rank < ROOM, owner * PITCH + rank, -1)
+        ids_row[:, here] = jnp.broadcast_to((ids + 1).astype(f32).astype(bf16), (8, length))
+        if head < 3:
+            turn_pieces(head + 1)
+    most[0] = jnp.broadcast_to(highest, (8, LANES))
+    fullest = [routes.start(most.at[0], most.at[step], along_x(step)) for step in (1, 2, 3)]
+    lines = [copies.start(line(0), line(0), along_y(step)) for step in (1, 3, 2)]
+    across.append(copies.start(line(0), line(0), other))
+    turn_planes(0)
+    for copy in fullest:
+        copy.wait_recv()
+    most[4] = jnp.maximum(jnp.maximum(most[0], most[1]), jnp.maximum(most[2], most[3]))
+    fullest = routes.start(most.at[4], most.at[5], other)
+
+    @pl.loop(0, OWNERS // 4)
+    def _(block):
+        rows = 4 * PITCH
+        place = lax.broadcasted_iota(jnp.int32, (rows, heads * length), 0) + block * rows
+        chosen = one(place == slots_row[...])
+        both = dot(chosen, pay[...])
+        both = both[:, :HD] + both[:, HD:]
+        marks = dot(ids_row[...], chosen, NT)
+        for lane in range(4):
+            early_out[block * 4 + lane] = both[lane * PITCH : (lane + 1) * PITCH]
+            early_out[block * 4 + lane, pl.ds(ROOM, 8), pl.ds(0, PITCH)] = marks[
+                :, lane * PITCH : (lane + 1) * PITCH
+            ]
+
+    fullest.wait_recv()
+    overall = jnp.maximum(most[4], most[5])[:, :PITCH]
+
+    @pl.loop(0, OWNERS)
+    def _(block):
+        early_out[block, pl.ds(ROOM, 8), pl.ds(PITCH, PITCH)] = overall
+
+    def early(step):
+        there = lax.rem(me + step, OWNERS)
+        return pltpu.make_async_remote_copy(
+            src_ref=early_out.at[there],
+            dst_ref=early_ref.at[me],
+            send_sem=early_send.at[step],
+            recv_sem=early_recv.at[step],
+            device_id={"ctx": there},
+            device_id_type=MESH,
+        )
+
+    @pl.loop(1, OWNERS)
+    def _(step):
+        early(step).start()
+
+    stay = pltpu.make_async_copy(early_out.at[me], early_ref.at[me], local_sem.at[0])
+    stay.start()
+    for step in range(1, 4):
+        turn_planes(step)
     for copy, step in zip(lines, (3, 1, 2)):
         copy.wait_recv()
         across.append(copies.start(line(step), line(step), other))
     for copy in across:
         copy.wait_recv()
     copies.finish()
-    assert len(copies.all) == GATHER_COPIES
-
-
-def gather_weights(qk_weight, value_weight):
+    routes.finish()
+    stay.wait()
+
+    @pl.loop(1, OWNERS)
+    def _(step):
+        early(step).wait()
+
+    assert len(copies.all) == GATHER_COPIES and len(routes.all) == ROUTE_COPIES
+
+
+def gather_weights(qk_weight, value_weight, clusters, upstream):
     width = qk_weight.shape[1]
+    length = clusters.shape[1]
+    rows = width // HD * length
     return pl.pallas_call(
         gather_kernel,
-        out_shape=jax.ShapeDtypeStruct((2, NY, NZ, ROWS, 2 * width), jnp.float32),
-        in_specs=[pl.BlockSpec(memory_space=pl.ANY)] * 2,
-        out_specs=pl.BlockSpec(memory_space=pl.ANY),
+        out_shape=(
+            jax.ShapeDtypeStruct((2, NY, NZ, ROWS, 2 * width), f32),
+            jax.ShapeDtypeStruct((OWNERS, PITCH, HD), f32),
+            jax.ShapeDtypeStruct((8, length), jnp.int32),
+        ),
+        in_specs=[pl.BlockSpec(memory_space=pl.ANY)] * 2
+        + [pl.BlockSpec(memory_space=pltpu.VMEM)] * 2,
+        out_specs=(
+            pl.BlockSpec(memory_space=pl.ANY),
+            pl.BlockSpec(memory_space=pl.ANY),
+            pl.BlockSpec(memory_space=pltpu.VMEM),
+        ),
         scratch_shapes=[
+            pltpu.VMEM((NY, 8, CLUSTERS), f32),
+            pltpu.VMEM((NZ, 8, CLUSTERS), f32),
+            pltpu.VMEM((6, 8, LANES), f32),
+            pltpu.VMEM((8, rows), bf16),
+            pltpu.VMEM((1, rows), jnp.int32),
+            pltpu.VMEM((rows, 2 * HD), bf16),
+            pltpu.VMEM((OWNERS, PITCH, HD), f32),
             pltpu.SemaphoreType.DMA((2,)),
             pltpu.SemaphoreType.DMA((GATHER_COPIES,)),
             pltpu.SemaphoreType.DMA((GATHER_COPIES,)),
+            pltpu.SemaphoreType.DMA((ROUTE_COPIES,)),
+            pltpu.SemaphoreType.DMA((ROUTE_COPIES,)),
+            pltpu.SemaphoreType.DMA((OWNERS,)),
+            pltpu.SemaphoreType.DMA((OWNERS,)),
         ],
-        compiler_params=pltpu.CompilerParams(collective_id=0, has_side_effects=True),
+        compiler_params=pltpu.CompilerParams(
+            collective_id=0, has_side_effects=True, vmem_limit_bytes=BIG
+        ),
         name="gather_weights",
-    )(qk_weight, value_weight)
+    )(qk_weight, value_weight, clusters, upstream)
 
 
 SCATTER_COPIES = 3 + 12 + 7 + 3 + 7 + 3
@@ -327,39 +550,9 @@
     )(token_terms, weight_terms.reshape(2, NY, NZ, ROWS, both))
 
 
-LANES = 128
-GROUP = 8
-SLOTS = 96
-TALL = 768
-MIXERS = (1, 77, 181, 111)
-f32, bf16 = jnp.float32, jnp.bfloat16
-NN = (((1,), (0,)), ((), ()))
-NT = (((1,), (1,)), ((), ()))
-TN = (((0,), (0,)), ((), ()))
-BIG = 48 * 2**20
-
-
-def dot(left, right, dims=NN):
-    return lax.dot_general(left, right, dims, preferred_element_type=f32)
-
-
-def halves(matrix):
-    upper = matrix.astype(bf16)
-    return upper, (matrix - upper.astype(f32)).astype(bf16)
-
-
-def dot3(left, right, dims=NN):
-    a, b = left
-    c, d = right
-    first = jnp.concatenate([a, b, a], axis=dims[0][0][0])
-    second = jnp.concatenate([c, c, d], axis=dims[0][1][0])
-    return dot(first, second, dims)
-
-
-def pack_kernel(tokens_ref, full_ref, grad_ref, slots_ref, ids_ref, rows_ref, marks_ref, acc, pay):
+def pack_kernel(tokens_ref, full_ref, slots_ref, rows_ref, acc, pay):
     step = pl.program_id(0)
-    width = grad_ref.shape[1]
-    length = grad_ref.shape[0]
+    length, both = acc.shape
     rows = rows_ref.shape[0]
 
     @pl.when(step == 0)
@@ -372,55 +565,42 @@
 
     @pl.when(step == 7)
     def _():
-        for head in range(width // HD):
+        for head in range(both // (2 * HD)):
             here = pl.ds(head * length, length)
-            for part, source in enumerate((
-                acc[:, head * HD : (head + 1) * HD],
-                acc[:, width + head * HD : width + (head + 1) * HD],
-                grad_ref[:, head * HD : (head + 1) * HD],
-            )):
-                upper, lower = halves(source)
+            for part in range(2):
+                column = part * both // 2 + head * HD
+                upper, lower = halves(acc[:, column : column + HD])
                 pay[here, part * HD : (part + 1) * HD] = upper
-                pay[here, (3 + part) * HD : (4 + part) * HD] = lower
+                pay[here, (2 + part) * HD : (3 + part) * HD] = lower
 
     @pl.when(step >= 8)
     def _():
         place = lax.broadcasted_iota(jnp.int32, (rows, slots_ref.shape[1]), 0) + (step - 8) * rows
-        chosen = (place == slots_ref[...]).astype(f32).astype(bf16)
-        both = dot(chosen, pay[...])
-        rows_ref[...] = both[:, : 3 * HD] + both[:, 3 * HD :]
-        marks_ref[0] = dot(ids_ref[...].astype(bf16), chosen, NT)
-
-
-def pack_rows(inputs, full, upstream, slots, ids, room):
+        moved = dot(one(place == slots_ref[...]), pay[...])
+        rows_ref[...] = moved[:, : 2 * HD] + moved[:, 2 * HD :]
+
+
+def pack_rows(inputs, full, slots, room):
     length, depth = inputs.shape
-    width = upstream.shape[1]
+    both = full.shape[1]
     total = slots.shape[1]
     return pl.pallas_call(
         pack_kernel,
         grid=(16,),
-        out_shape=(
-            jax.ShapeDtypeStruct((32 * room, 3 * HD), f32),
-            jax.ShapeDtypeStruct((8, 8, 4 * room), f32),
-        ),
+        out_shape=jax.ShapeDtypeStruct((OWNERS * room, 2 * HD), f32),
         in_specs=[
             pl.BlockSpec((length, depth // 8), lambda i: (0, jnp.minimum(i, 7))),
-            pl.BlockSpec((depth // 8, 2 * width), lambda i: (jnp.minimum(i, 7), 0)),
-            pl.BlockSpec((length, width), lambda i: (0, 0)),
+            pl.BlockSpec((depth // 8, both), lambda i: (jnp.minimum(i, 7), 0)),
             pl.BlockSpec((1, total), lambda i: (0, 0)),
-            pl.BlockSpec((8, total), lambda i: (0, 0)),
         ],
-        out_specs=(
-            pl.BlockSpec((4 * room, 3 * HD), lambda i: (jnp.maximum(i - 8, 0), 0)),
-            pl.BlockSpec((1, 8, 4 * room), lambda i: (jnp.maximum(i - 8, 0), 0, 0)),
-        ),
-        scratch_shapes=[pltpu.VMEM((length, 2 * width), f32), pltpu.VMEM((total, 6 * HD), bf16)],
+        out_specs=pl.BlockSpec((4 * room, 2 * HD), lambda i: (jnp.maximum(i - 8, 0), 0)),
+        scratch_shapes=[pltpu.VMEM((length, both), f32), pltpu.VMEM((total, 4 * HD), bf16)],
         compiler_params=pltpu.CompilerParams(vmem_limit_bytes=BIG),
         name="project_and_pack",
-    )(inputs, full, upstream, slots, ids)
-
-
-def attend_kernel(marks_ref, rows_ref, replies_ref, spread, seats, valid, answer):
+    )(inputs, full, slots)
+
+
+def attend_kernel(marks_ref, rows_ref, early_ref, replies_ref, spread, seats, valid, answer):
     groups = marks_ref.shape[0]
     wide = marks_ref.shape[2]
     owned = spread.shape[1]
@@ -431,10 +611,15 @@
     def _(group):
         here = pl.ds(pl.multiple_of(group * wide, wide), wide)
         place = lax.broadcasted_iota(jnp.int32, (TALL, wide), 0)
-        chosen = (place == marks_ref[group]).astype(f32).astype(bf16)
+        chosen = one(place == marks_ref[group])
         seats[group] = chosen
         upper, lower = halves(rows_ref[here, :])
-        moved = dot(chosen, jnp.concatenate([upper, lower, jnp.ones((wide, LANES), bf16)], axis=1))
+        early = early_ref[pl.ds(group * GROUP, GROUP), pl.ds(0, wide // GROUP), :]
+        early_upper, early_lower = halves(early.reshape(wide, HD))
+        present = jnp.ones((wide, LANES), bf16)
+        moved = dot(
+            chosen, jnp.concatenate([upper, early_upper, lower, early_lower, present], axis=1)
+        )
         spread[group] = (moved[:, : 3 * HD] + moved[:, 3 * HD : 6 * HD]).reshape(owned, seat, 3 * HD)
         valid[group] = moved[:, 6 * HD :].reshape(owned, seat, LANES)
 
@@ -467,14 +652,14 @@
         replies_ref[here, :] = moved[:, : 2 * HD] + moved[:, 2 * HD :]
 
 
-def attend(rows, marks, room):
-    groups = 32 // GROUP
+def attend(rows, early, marks, room):
+    groups = OWNERS // GROUP
     owned = TALL // (3 * GROUP)
     seat = 3 * GROUP
     return pl.pallas_call(
         attend_kernel,
-        out_shape=jax.ShapeDtypeStruct((32 * room, 2 * HD), f32),
-        in_specs=[pl.BlockSpec(memory_space=pltpu.VMEM)] * 2,
+        out_shape=jax.ShapeDtypeStruct((OWNERS * room, 2 * HD), f32),
+        in_specs=[pl.BlockSpec(memory_space=pltpu.VMEM)] * 3,
         out_specs=pl.BlockSpec(memory_space=pltpu.VMEM),
         scratch_shapes=[
             pltpu.VMEM((groups, owned, seat, 3 * HD), f32),
@@ -484,7 +669,7 @@
         ],
         compiler_params=pltpu.CompilerParams(vmem_limit_bytes=BIG),
         name="attend",
-    )(marks, rows)
+    )(marks, rows, early)
 
 
 def grads_kernel(returned_ref, slots_ref, tokens_ref, full_ref, terms_ref, sums_ref, high, low):
@@ -498,7 +683,7 @@
         source = jnp.concatenate([upper, lower], axis=1)
         for head in range(width // HD):
             place = lax.broadcasted_iota(jnp.int32, (length, total), 1)
-            chosen = (place == slots_ref[:, head : head + 1]).astype(f32).astype(bf16)
+            chosen = one(place == slots_ref[:, head : head + 1])
             both = dot(chosen, source)
             upper, lower = halves(both[:, : 2 * HD] + both[:, 2 * HD :])
             for part in range(2):
@@ -542,52 +727,57 @@
     return lax.all_to_all(array, "ctx", split_axis=0, concat_axis=0, tiled=True)
 
 
-def middle_part(room, inputs, full, upstream, owner, rank, ids):
-    heads_here, length = owner.shape
-    slots = owner * room + rank
-    rows, marks = pack_rows(
-        inputs, full, upstream, slots.reshape(1, -1),
-        jnp.broadcast_to((ids + 1).astype(f32).reshape(1, -1), (8, ids.size)), room,
-    )
-    marks = exchange(marks[:, 0, :].reshape(32, room))
-    rows = exchange(rows.reshape(32, room, 3 * HD)).reshape(32 * room, 3 * HD)
+def middle_part(room, inputs, full, early, marks, slots):
+    rows = pack_rows(inputs, full, slots.reshape(1, -1), room)
+    rows = exchange(rows.reshape(OWNERS, room, 2 * HD)).reshape(OWNERS * room, 2 * HD)
     marks = marks.astype(jnp.int32) - 1
     source = lax.broadcasted_iota(jnp.int32, marks.shape, 0) % GROUP
     seats = (marks // 3) * (3 * GROUP) + source * 3 + marks % 3
-    seats = jnp.where(marks < 0, -1, seats).reshape(32 // GROUP, 1, GROUP * room)
-    replies = attend(rows, seats, room)
-    returned = exchange(replies.reshape(32, room, 2 * HD)).reshape(32 * room, 2 * HD)
+    seats = jnp.where(marks < 0, -1, seats).reshape(OWNERS // GROUP, 1, GROUP * room)
+    replies = attend(rows, early, seats, room)
+    returned = exchange(replies.reshape(OWNERS, room, 2 * HD)).reshape(OWNERS * room, 2 * HD)
     return local_grads(returned, slots.T, inputs, full)
+
+
+def roomy_part(inputs, full, upstream, cluster):
+    heads, length = cluster.shape
+    order = jnp.arange(length, dtype=jnp.int32)
+    earlier = order[:, None] < order[None, :]
+    alike = cluster[:, :, None] == cluster[:, None, :]
+    within = jnp.sum((alike & earlier).astype(jnp.int32), axis=1)
+    head = jnp.arange(heads, dtype=jnp.int32)[:, None]
+    ids = (head * CL_DEV + cluster % CL_DEV) * 3 + within
+    slots = cluster // CL_DEV * SLOTS + ids
+    marks = jnp.zeros((OWNERS * SLOTS,), f32).at[slots.reshape(-1)].set(
+        (ids + 1).astype(f32).reshape(-1)
+    )
+    rows = upstream.reshape(length, heads, HD).transpose(1, 0, 2).reshape(-1, HD)
+    early = jnp.zeros((OWNERS * SLOTS, HD), f32).at[slots.reshape(-1)].set(rows)
+    early = exchange(early.reshape(OWNERS, SLOTS, HD))
+    marks = exchange(marks.reshape(OWNERS, SLOTS))
+    return middle_part(SLOTS, inputs, full, early, marks, slots)
 
 
 def per_device(tokens, qk_weight, value_weight, grad_out, assign):
     inputs = tokens[0]
-    length = inputs.shape[0]
-    clusters = CL_DEV * lax.axis_size("ctx")
     heads_here = qk_weight.shape[1] // HD
     width = heads_here * HD
-    mixers = jnp.asarray(MIXERS, jnp.int32)[:, None]
-    cluster = (assign[:, 0, :, 0] * mixers) % clusters
-    owner = cluster // CL_DEV
-    order = jnp.arange(length, dtype=jnp.int32)
-    earlier = order[:, None] < order[None, :]
-    within = jnp.sum(
-        ((cluster[:, :, None] == cluster[:, None, :]) & earlier).astype(jnp.int32), axis=1
+    cluster = assign[:, 0, :, 0]
+    full, early, slots = gather_weights(
+        qk_weight, value_weight, jnp.pad(cluster, ((0, 8 - heads_here), (0, 0))), grad_out[0]
     )
-    flat = owner.reshape(-1)
-    order = jnp.arange(flat.size, dtype=jnp.int32)
-    earlier = order[:, None] < order[None, :]
-    rank = jnp.sum(((flat[:, None] == flat[None, :]) & earlier).astype(jnp.int32), axis=0)
-    rank = rank.reshape(owner.shape)
-    head_ids = jnp.arange(heads_here, dtype=jnp.int32)[:, None]
-    ids = (head_ids * CL_DEV + cluster % CL_DEV) * 3 + within
-    fullest = lax.pmax(jnp.max(rank) + 1, ("rep", "ctx", "tp"))
-    full = gather_weights(qk_weight, value_weight).reshape(-1, 2 * width)
+    full = full.reshape(-1, 2 * width)
+    fullest = jnp.max(early[:, ROOM, PITCH])
+
+    def snug(inputs, full, upstream, cluster, early, slots):
+        marks = early[:, ROOM, :ROOM]
+        return middle_part(ROOM, inputs, full, early, marks, slots[:heads_here])
+
+    def roomy(inputs, full, upstream, cluster, early, slots):
+        return roomy_part(inputs, full, upstream, cluster)
+
     token_terms, weight_terms = lax.cond(
-        fullest <= ROOM,
-        lambda *operands: middle_part(ROOM, *operands),
-        lambda *operands: middle_part(SLOTS, *operands),
-        inputs, full, grad_out[0], owner, rank, ids,
+        fullest <= ROOM, snug, roomy, inputs, full, grad_out[0], cluster, early, slots
     )
     grad_tokens, grad_qk_weight, grad_value_weight = scatter_sums(token_terms, weight_terms)
     return (grad_tokens[None], grad_qk_weight, grad_value_weight)

time: 416 us -> 299 us (0.72)
  blocking collectives: 150 us -> 51.4 us
  waiting for transfers between devices: 73.2 us -> 44.3 us
  Pallas kernels: 160 us -> 188 us
  other arithmetic: 13.2 us -> 1.13 us
  local copies, waits for them, and re-layouts: 11.5 us -> 6.52 us
    pmax x1 -> x0, blocking collectives: 78.7 us -> none  [per_device(): fullest = lax.pmax(jnp.max(rank) + 1, ('rep', 'ctx', 'tp'))]
    all_to_all x1, waiting for transfers between devices: 73.2 us -> 44.3 us  [exchange(): return lax.all_to_all(array, 'ctx', split_axis=0, concat_axis=0, tiled=True)]
    pallas_call x3, Pallas kernels: 95.5 us -> 120 us  [the longest x1 84.4 us: gather_weights(): pl.pallas_call(gather_kernel, out_shape=(jax.ShapeDtypeStruct((2, NY, NZ,...]
    all_to_all x2 -> x1, blocking collectives: 71.2 us -> 51.4 us  [exchange(): return lax.all_to_all(array, 'ctx', split_axis=0, concat_axis=0, tiled=True)]
where the time goes in v3:
time: 299 us; the launch traced here: 297 us
  Pallas kernels  188 us (63%)
  blocking collectives  51.4 us (17%)
  waiting for transfers between devices  44.3 us (15%)
  local copies, waits for them, and re-layouts  6.52 us (2%)
  starting transfers between devices  4.82 us (2%)
    pallas_call x1, Pallas kernels, gather_weights(): pl.pallas_call(gather_kernel, out_shape=(jax.ShapeDtypeStruct((2, NY, NZ,...  84.4 us
    all_to_all x1, blocking collectives, exchange(): return lax.all_to_all(array, 'ctx', split_axis=0, concat_axis=0, tiled=True)  51.4 us
    pallas_call x1, Pallas kernels, scatter_sums(): pl.pallas_call(scatter_kernel, out_shape=(jax.ShapeDtypeStruct((length, w...  50.4 us
    all_to_all x1, waiting for transfers between devices, exchange(): return lax.all_to_all(array, 'ctx', split_axis=0, concat_axis=0, tiled=True)  44.3 us
    pallas_call x1, Pallas kernels, attend(): pl.pallas_call(attend_kernel, out_shape=jax.ShapeDtypeStruct((OWNERS * ro...  20.7 us
    pallas_call x1, Pallas kernels, local_grads(): pl.pallas_call(grads_kernel, grid=(8,), out_shape=(jax.ShapeDtypeStruct((...  17.4 us
    pallas_call x1, Pallas kernels, pack_rows(): pl.pallas_call(pack_kernel, grid=(16,), out_shape=jax.ShapeDtypeStruct((O...  14.7 us
  transfers between devices with their start and end apart: 1, of which 1 were waited for; matrix products, arithmetic and copies ran while one was open for 0% of the time, Pallas kernels for 0%

profile of v3, /device:TPU:2, one launch (start us, length us, event | category | flops | bytes accessed | tf_op | source)
XLA Modules:
  0.0 297.4 jit_solution(7809891878018777184)
XLA Ops:
  0.6 0.7 copy.68
  1.3 0.8 copy-done.1
  2.2 0.8 copy-done.2
  3.0 84.4 %gather_weights.1 = (f32[2,4,8,32,1024]{4,3,2,1,0:T(8,128)}, f32[32,64,128]{2,1,0:T(8,128)S(1)}, s32[8,384]{1,0:T(8,128)S(1)}) custom-call(f32[32,512]{1,0:T(8,128)S(1)} %copy-done.1, f32[32,512]{1,0:T(8,128)S(1)} %copy-done.2, s32[8,384]{1,0:T(8,128)S(1)} %pad.4.cluster_ref, f32[384,512]{1,0:T(8,128)} %bitcast.53), custom_call_target="tpu_custom_call" | custom-call | tf_op jit(solution)/shard_map/gather_weights/pallas_call | solution.py:334
  87.4 0.7 slice_reduce_fusion
  88.7 156.0 %conditional.1 = (f32[384,2048]{1,0:T(8,128)}, f32[2,4,8,32,1024]{4,3,2,1,0:T(8,128)}) conditional(s32[]{:T(128)} %convert_element_type.31, (s32[4,384]{1,0:T(4,128)S(1)}, s32[4,1,384,1]{2,3,1,0:T(1,128)}, f32[384,2048]{1,0:T(8,128)}, f32[2048,1024]{1,0:T(8,128)}, f32[1,384,512]{2,1,0:T(8,128)}) %tuple.47, (f32[32,64,128]{2,1,0:T(8,128)S(1)}, ...), branch_computations={%region_1.5_spmd, %region_5.6_spmd} | conditional | flops 2620740 | bytes 50259624 | solution.py:779
  89.0 0.1 copy.60
  89.3 14.7 %project_and_pack.3 = f32[1792,256]{1,0:T(8,128)S(1)} custom-call(f32[384,2048]{1,0:T(8,128)} %get-tuple-element.31.tokens_ref, f32[2048,1024]{1,0:T(8,128)} %get-tuple-element.32.full_ref, s32[1,1536]{1,0:T(1,128)S(1)} %bitcast.48), custom_call_target="tpu_custom_call" | custom-call | tf_op jit(solution)/shard_map/cond/branch_1_fun/project_and_pack/pallas_call | solution.py:587
  103.9 1.3 copy-done
  105.2 4.8 %all-to-all-start = ((f32[32,56,256]{2,1,0:T(8,128)}), f32[32,56,256]{2,1,0:T(8,128)S(1)}, u32[]{:S(2)}, u32[]{:S(2)}) async-start(f32[32,56,256]{2,1,0:T(8,128)} %bitcast.43), calls=%async_computation | async-start | bytes 3670016 | tf_op jit(solution)/shard_map/cond/branch_1_fun/all_to_all | solution.py:727
  110.1 0.1 compare_reduce_fusion
  110.2 0.1 ne.129
  110.5 0.1 mul.59
  110.6 0.1 divide_reduce_fusion
  110.7 0.1 div.43
  110.8 0.1 rem.87
  111.0 44.3 %all-to-all-done = f32[32,56,256]{2,1,0:T(8,128)S(1)} async-done(((f32[32,56,256]{2,1,0:T(8,128)}), f32[32,56,256]{2,1,0:T(8,128)S(1)}, u32[]{:S(2)}, u32[]{:S(2)}) %all-to-all-start) | async-done | bytes 1835040 | tf_op jit(solution)/shard_map/cond/branch_1_fun/all_to_all | solution.py:727
  155.3 20.7 %attend.3 = f32[1792,256]{1,0:T(8,128)S(1)} custom-call(s32[4,1,448]{2,1,0:T(1,128)S(1)} %fusion.1.marks_ref, f32[1792,256]{1,0:T(8,128)S(1)} %bitcast.41, f32[32,64,128]{2,1,0:T(8,128)S(1)} %get-tuple-element.30.early_ref), custom_call_target="tpu_custom_call" | custom-call | tf_op jit(solution)/shard_map/cond/branch_1_fun/attend/pallas_call | solution.py:659
  176.0 51.4 %all_to_all.28 = f32[32,56,256]{2,1,0:T(8,128)S(1)} all-to-all(f32[32,56,256]{2,1,0:T(8,128)S(1)} %bitcast.42), channel_id=1, replica_groups=mesh['rep'=2,'ctx'=32,'tp'=4] {'ctx'}, dimensions={0} | all-to-all | bytes 3670016 | tf_op jit(solution)/shard_map/cond/branch_1_fun/all_to_all | solution.py:727
  227.4 17.4 %unpack_and_grads.3 = (f32[384,2048]{1,0:T(8,128)}, f32[2048,1024]{1,0:T(8,128)}) custom-call(f32[1792,256]{1,0:T(8,128)S(1)} %bitcast.40, s32[384,4]{1,0:T(8,128)S(1)} %get-tuple-element.108.slots_ref, f32[384,2048]{1,0:T(8,128)} %get-tuple-element.31.tokens_ref, f32[2048,1024]{1,0:T(8,128)S(1)} %copy-done.3), custom_call_target="tpu_custom_call" | custom-call | tf_op jit(solution)/shard_map/cond/branch_1_fun/unpack_and_grads/pallas_call | solution.py:703
  244.8 50.4 %scatter_sums.1 = (f32[384,512]{1,0:T(8,128)S(1)}, f32[32,512]{1,0:T(8,128)S(1)}, f32[32,512]{1,0:T(8,128)S(1)}) custom-call(f32[384,2048]{1,0:T(8,128)} %get-tuple-element.50.terms_ref, f32[2,4,8,32,1024]{4,3,2,1,0:T(8,128)} %get-tuple-element.51.sums_ref), custom_call_target="tpu_custom_call" | custom-call | tf_op jit(solution)/shard_map/scatter_sums/pallas_call | solution.py:526
  295.2 0.9 copy.76
  296.1 0.6 copy.77
  296.7 0.6 copy.78
  (14 shorter events, 0.4 us)
Async XLA Ops:
  1.3 0.8 copy-start.1
  2.2 0.8 copy-start.2
  103.9 1.3 copy-start
  105.2 50.1 %all-to-all-start = ((f32[32,56,256]{2,1,0:T(8,128)}), f32[32,56,256]{2,1,0:T(8,128)S(1)}, u32[]{:S(2)}, u32[]{:S(2)}) async-start(f32[32,56,256]{2,1,0:T(8,128)} %bitcast.43), calls=%async_computation | async-start | bytes 3670016 | tf_op jit(solution)/shard_map/cond/branch_1_fun/all_to_all | solution.py:727
  155.3 72.1 %copy-start.3 = (f32[2048,1024]{1,0:T(8,128)S(1)}, f32[2048,1024]{1,0:T(8,128)}, u32[]{:S(2)}) copy-start(f32[2048,1024]{1,0:T(8,128)} %get-tuple-element.32.full_ref) | copy-start | bytes 25165828 | tf_op jit(solution)/shard_map/cond

commit v4 on v3

--- a/solution.py
+++ b/solution.py
@@ -79,7 +79,7 @@
             copy.wait_send()
 
 
-GATHER_COPIES = 3 + 7 + 7 + 3 + 8 + 4
+GATHER_COPIES = 3 + 7 + 14 + 21 + 16 + 4
 ROUTE_COPIES = 3 + 7 + 3 + 1
 CLUSTERS = 256
 OWNERS = 32
@@ -128,14 +128,13 @@
     many = owned.astype(f32)
     rank = jnp.sum(many * (dot(owned, earlier) + base), axis=0, keepdims=True)
     base = base + jnp.sum(many, axis=1, keepdims=True)
-    ids = (head * CL_DEV + turn) * 3 + within.astype(jnp.int32)
-    return owner, rank.astype(jnp.int32), ids, base
+    return owner, rank.astype(jnp.int32), head * CL_DEV + turn, within, base
 
 
 def gather_kernel(
-    qk_ref, value_ref, cluster_ref, grad_ref,
-    out_ref, early_ref, slots_ref,
-    counts_y, counts_z, most, ids_row, slots_row, pay, early_out,
+    qk_ref, value_ref, cluster_ref, grad_ref, tokens_ref,
+    full_ref, early_ref, slots_ref, tall_slots_ref, pay_ref,
+    out_ref, tokens, acc, counts_y, counts_z, most, ids_row, slots_row, pay, early_out,
     local_sem, send_sem, recv_sem, route_send, route_recv, early_send, early_recv,
 ):
     rep, y, z = position()
@@ -157,8 +156,9 @@
     def around(step):
         return {"ctx": lax.rem(me + step, OWNERS)}
 
-    def plane(step):
-        return out_ref.at[rep, :, lax.rem(z + step, NZ), pl.ds(0, HALF), :]
+    def plane(step, part):
+        there = pl.ds(part * width, width)
+        return out_ref.at[rep, :, lax.rem(z + step, NZ), pl.ds(0, HALF), there]
 
     def piece(step):
         return out_ref.at[rep, y, lax.rem(z + step, NZ), pl.ds(HALF, HALF), :]
@@ -168,6 +168,8 @@
 
     right, left, other = along_z(1), along_z(NZ - 1), {"rep": 1 - rep}
     mine = out_ref.at[rep, y, z]
+    fetch = pltpu.make_async_copy(tokens_ref, tokens, local_sem.at[2])
+    fetch.start()
     first = pltpu.make_async_copy(qk_ref, mine.at[:, pl.ds(0, width)], local_sem.at[0])
     second = pltpu.make_async_copy(value_ref, mine.at[:, pl.ds(width, width)], local_sem.at[1])
     first.start()
@@ -190,8 +192,7 @@
     first.wait()
     second.wait()
     copies = Copies(send_sem, recv_sem)
-    own = out_ref.at[rep, y, z, pl.ds(0, HALF), :]
-    shared = [copies.start(own, own, along_y(step)) for step in (1, 3, 2)]
+    shared = [copies.start(mine, mine, along_y(step)) for step in (1, 3, 2)]
     pieces = [(copies.start(piece(0), piece(0), right), copies.start(piece(0), piece(0), left))]
 
     for head in range(heads):
@@ -207,24 +208,39 @@
     ]
     for copy in shared:
         copy.wait_recv()
-    planes = [(copies.start(plane(0), plane(0), right), copies.start(plane(0), plane(0), left))]
-    across = [copies.start(plane(0), plane(0), other)]
+    planes = []
+    for part in range(2):
+        here = plane(0, part)
+        planes.append([(copies.start(here, here, right), copies.start(here, here, left))])
+    across = [copies.start(plane(0, part), plane(0, part), other) for part in range(2)]
+    passed = {1: [], 2: [], 3: []}
+
+    def pass_on(here):
+        for step in (1, 3, 2):
+            passed[step].append(copies.start(here, here, along_y(step)))
 
     def turn_pieces(step):
         rightward, leftward = pieces[step]
+        after, before = piece(NZ - 1 - step), piece(1 + step)
         rightward.wait_recv()
         if leftward is not None:
             leftward.wait_recv()
         if step < 3:
-            after, before = piece(NZ - 1 - step), piece(1 + step)
             pieces.append((
                 copies.start(after, after, right),
                 copies.start(before, before, left) if step < 2 else None,
             ))
+        pass_on(after)
+        if leftward is not None:
+            pass_on(before)
 
     def turn_planes(step):
-        rightward, leftward = planes[step]
-        after, before = plane(NZ - 1 - step), plane(1 + step)
+        for part in range(2):
+            turn_plane(step, part)
+
+    def turn_plane(step, part):
+        rightward, leftward = planes[part][step]
+        after, before = plane(NZ - 1 - step, part), plane(1 + step, part)
         rightward.wait_recv()
         if step < 3:
             going = copies.start(after, after, right)
@@ -232,7 +248,7 @@
             leftward.wait_recv()
             coming = copies.start(before, before, left) if step < 2 else None
         if step < 3:
-            planes.append((going, coming if step < 2 else None))
+            planes[part].append((going, coming if step < 2 else None))
         across.append(copies.start(after, after, other))
         if leftward is not None:
             across.append(copies.start(before, before, other))
@@ -251,19 +267,28 @@
     )
     base = jnp.zeros((OWNERS, 1), f32)
     highest = jnp.zeros((1, 1), f32)
-    slots_ref[...] = jnp.full(slots_ref.shape, -1, jnp.int32)
+    row = lax.broadcasted_iota(jnp.int32, (8, length), 0)
+    slots_list = []
     for head in range(heads):
-        owner, rank, ids, base = route_head(cluster_ref, head, keys, tall_keys, earlier, base)
+        owner, rank, held, within, base = route_head(
+            cluster_ref, head, keys, tall_keys, earlier, base
+        )
         highest = jnp.maximum(highest, jnp.max(rank.astype(f32), axis=1, keepdims=True) + 1)
-        slots_ref[head : head + 1, :] = jnp.where(rank < ROOM, owner * ROOM + rank, -1)
         here = pl.ds(head * length, length)
+        slots_ref[:, here] = jnp.where(rank < ROOM, owner * ROOM + rank, -1)
         slots_row[:, here] = jnp.where(rank < ROOM, owner * PITCH + rank, -1)
-        ids_row[:, here] = jnp.broadcast_to((ids + 1).astype(f32).astype(bf16), (8, length))
+        within = within + (3 * lax.rem(me, GROUP)).astype(f32)
+        marked = jnp.where(row == 0, (held + 1).astype(f32), jnp.where(row == 1, within, 0.0))
+        ids_row[:, here] = marked.astype(bf16)
+        slots_list.append(jnp.where(rank < ROOM, owner * ROOM + rank, -1))
         if head < 3:
             turn_pieces(head + 1)
     most[0] = jnp.broadcast_to(highest, (8, LANES))
+    tall = jnp.concatenate(
+        slots_list + [jnp.zeros((LANES - heads, length), jnp.int32)], axis=0
+    )
+    tall_slots_ref[...] = tall.astype(f32).T.astype(jnp.int32)
     fullest = [routes.start(most.at[0], most.at[step], along_x(step)) for step in (1, 2, 3)]
-    lines = [copies.start(line(0), line(0), along_y(step)) for step in (1, 3, 2)]
     across.append(copies.start(line(0), line(0), other))
     turn_planes(0)
     for copy in fullest:
@@ -311,14 +336,43 @@
     stay.start()
     for step in range(1, 4):
         turn_planes(step)
-    for copy, step in zip(lines, (3, 1, 2)):
-        copy.wait_recv()
-        across.append(copies.start(line(step), line(step), other))
+    for step in (1, 3, 2):
+        for copy in passed[step]:
+            copy.wait_recv()
+        across.append(copies.start(line(NY - step), line(NY - step), other))
+    fetch.wait()
+
+    def project(half, there):
+        start = pl.multiple_of((half * NY + there) * (NZ * ROWS), NZ * ROWS)
+        some = halves(tokens[:, pl.ds(start, NZ * ROWS)])
+        return dot3(some, halves(out_ref[half, there].reshape(NZ * ROWS, 2 * width)))
+
+    acc[...] = project(rep, 0)
+
+    @pl.loop(1, NY)
+    def _(there):
+        acc[...] += project(rep, there)
+
     for copy in across:
         copy.wait_recv()
+    save = pltpu.make_async_copy(out_ref, full_ref, local_sem.at[1])
+    save.start()
+
+    @pl.loop(0, NY)
+    def _(there):
+        acc[...] += project(1 - rep, there)
+
+    for part in range(2):
+        for head in range(heads):
+            here = pl.ds(head * length, length)
+            column = part * width + head * HD
+            upper, lower = halves(acc[:, column : column + HD])
+            pay_ref[part, here, :HD] = upper
+            pay_ref[part, here, HD:] = lower
     copies.finish()
     routes.finish()
     stay.wait()
+    save.wait()
 
     @pl.loop(1, OWNERS)
     def _(step):
@@ -327,25 +381,26 @@
     assert len(copies.all) == GATHER_COPIES and len(routes.all) == ROUTE_COPIES
 
 
-def gather_weights(qk_weight, value_weight, clusters, upstream):
+def gather_and_project(qk_weight, value_weight, clusters, upstream, inputs):
     width = qk_weight.shape[1]
     length = clusters.shape[1]
     rows = width // HD * length
+    vmem, anywhere = pl.BlockSpec(memory_space=pltpu.VMEM), pl.BlockSpec(memory_space=pl.ANY)
     return pl.pallas_call(
         gather_kernel,
         out_shape=(
             jax.ShapeDtypeStruct((2, NY, NZ, ROWS, 2 * width), f32),
             jax.ShapeDtypeStruct((OWNERS, PITCH, HD), f32),
-            jax.ShapeDtypeStruct((8, length), jnp.int32),
+            jax.ShapeDtypeStruct((1, rows), jnp.int32),
+            jax.ShapeDtypeStruct((length, LANES), jnp.int32),
+            jax.ShapeDtypeStruct((2, rows, 2 * HD), bf16),
         ),
-        in_specs=[pl.BlockSpec(memory_space=pl.ANY)] * 2
-        + [pl.BlockSpec(memory_space=pltpu.VMEM)] * 2,
-        out_specs=(
-            pl.BlockSpec(memory_space=pl.ANY),
-            pl.BlockSpec(memory_space=pl.ANY),
-            pl.BlockSpec(memory_space=pltpu.VMEM),
-        ),
+        in_specs=[anywhere, anywhere, vmem, vmem, anywhere],
+        out_specs=(anywhere, anywhere, vmem, vmem, vmem),
         scratch_shapes=[
+            pltpu.VMEM((2, NY, NZ, ROWS, 2 * width), f32),
+            pltpu.VMEM(inputs.shape, f32),
+            pltpu.VMEM((length, 2 * width), f32),
             pltpu.VMEM((NY, 8, CLUSTERS), f32),
             pltpu.VMEM((NZ, 8, CLUSTERS), f32),
             pltpu.VMEM((6, 8, LANES), f32),
@@ -353,7 +408,7 @@
             pltpu.VMEM((1, rows), jnp.int32),
             pltpu.VMEM((rows, 2 * HD), bf16),
             pltpu.VMEM((OWNERS, PITCH, HD), f32),
-            pltpu.SemaphoreType.DMA((2,)),
+            pltpu.SemaphoreType.DMA((3,)),
             pltpu.SemaphoreType.DMA((GATHER_COPIES,)),
             pltpu.SemaphoreType.DMA((GATHER_COPIES,)),
             pltpu.SemaphoreType.DMA((ROUTE_COPIES,)),
@@ -364,8 +419,8 @@
         compiler_params=pltpu.CompilerParams(
             collective_id=0, has_side_effects=True, vmem_limit_bytes=BIG
         ),
-        name="gather_weights",
-    )(qk_weight, value_weight, clusters, upstream)
+        name="gather_and_project",
+    )(qk_weight, value_weight, clusters, upstream, inputs)
 
 
 SCATTER_COPIES = 3 + 12 + 7 + 3 + 7 + 3
@@ -672,15 +727,211 @@
     )(marks, rows, early)
 
 
-def grads_kernel(returned_ref, slots_ref, tokens_ref, full_ref, terms_ref, sums_ref, high, low):
+QK, VALUE, GRAD_VALUE, GRAD_QK = range(4)
+
+
+def cluster_kernel(
+    pay_ref, slots_ref, marks_ref, early_ref, back_qk_ref, back_value_ref,
+    leaving, landed, seats, spread, valid, weights, answer,
+    local_sem, send_sem, recv_sem,
+):
+    me = lax.axis_index("ctx")
+    groups, _, wide = marks_ref.shape
+    owned, seat = spread.shape[2], spread.shape[3]
+    size = groups * seat
+    rows = 4 * ROOM
+
+    barrier = pltpu.get_barrier_semaphore()
+
+    @pl.loop(1, OWNERS)
+    def _(step):
+        there = {"ctx": lax.rem(me + step, OWNERS)}
+        pl.semaphore_signal(barrier, inc=1, device_id=there, device_id_type=MESH)
+
+    def target(kind):
+        if kind == GRAD_QK:
+            return back_qk_ref
+        return back_value_ref if kind == GRAD_VALUE else landed.at[kind]
+
+    def remote(kind, step):
+        there = lax.rem(me + step, OWNERS)
+        return pltpu.make_async_remote_copy(
+            src_ref=leaving.at[kind, there],
+            dst_ref=target(kind).at[me],
+            send_sem=send_sem.at[kind, step],
+            recv_sem=recv_sem.at[kind, step],
+            device_id={"ctx": there},
+            device_id_type=MESH,
+        )
+
+    def stay(kind):
+        return pltpu.make_async_copy(leaving.at[kind, me], target(kind).at[me], local_sem.at[kind])
+
+    def start(kind, there):
+        @pl.when(there == me)
+        def _():
+            stay(kind).start()
+
+        @pl.when(there != me)
+        def _():
+            remote(kind, lax.rem(there - me + OWNERS, OWNERS)).start()
+
+    def arrive(kind):
+        stay(kind).wait()
+
+        @pl.loop(1, OWNERS)
+        def _(step):
+            remote(kind, step).wait_recv()
+
+    def pack(kind, block):
+        place = lax.broadcasted_iota(jnp.int32, (rows, slots_ref.shape[1]), 0) + block * rows
+        moved = dot(one(place == slots_ref[...]), pay_ref[kind])
+        moved = moved[:, :HD] + moved[:, HD:]
+        for lane in range(4):
+            leaving[kind, block * 4 + lane] = moved[lane * ROOM : (lane + 1) * ROOM]
+
+    def take(kind, group, source):
+        upper, lower = halves(source)
+        moved = dot(seats[group], jnp.concatenate([upper, lower], axis=1))
+        spread[kind, group] = (moved[:, :HD] + moved[:, HD:]).reshape(owned, seat, HD)
+
+    def give(kind):
+        @pl.loop(0, groups)
+        def _(index):
+            group = lax.rem(lax.div(me, GROUP) + index, groups)
+            upper, lower = halves(answer[group].reshape(TALL, HD))
+            moved = dot(seats[group], jnp.concatenate([upper, lower], axis=1), TN)
+            moved = (moved[:, :HD] + moved[:, HD:]).reshape(GROUP, ROOM, HD)
+            leaving[kind, pl.ds(group * GROUP, GROUP)] = moved
+            for lane in range(GROUP):
+                start(kind, group * GROUP + lane)
+
+    def first_block():
+        return lax.div(me, 4)
+
+    pack(QK, first_block())
+    pl.semaphore_wait(barrier, OWNERS - 1)
+    for lane in range(4):
+        start(QK, first_block() * 4 + lane)
+
+    @pl.loop(1, OWNERS // 4)
+    def _(index):
+        block = lax.rem(first_block() + index, OWNERS // 4)
+        pack(QK, block)
+        for lane in range(4):
+            start(QK, block * 4 + lane)
+
+    @pl.loop(0, OWNERS // 4)
+    def _(block):
+        pack(VALUE, block)
+
+    @pl.loop(0, groups)
+    def _(group):
+        place = lax.broadcasted_iota(jnp.int32, (TALL, wide), 0)
+        chosen = one(place == marks_ref[group])
+        seats[group] = chosen
+        early = early_ref[pl.ds(group * GROUP, GROUP), pl.ds(0, ROOM), :].reshape(wide, HD)
+        upper, lower = halves(early)
+        present = jnp.ones((wide, LANES), bf16)
+        moved = dot(chosen, jnp.concatenate([upper, lower, present], axis=1))
+        spread[2, group] = (moved[:, :HD] + moved[:, HD : 2 * HD]).reshape(owned, seat, HD)
+        valid[group] = moved[:, 2 * HD :].reshape(owned, seat, LANES)
+
+    arrive(QK)
+
+    @pl.loop(0, OWNERS)
+    def _(index):
+        start(VALUE, lax.rem(me + index, OWNERS))
+
+    @pl.loop(0, groups)
+    def _(group):
+        take(QK, group, landed[QK, pl.ds(group * GROUP, GROUP)].reshape(wide, HD))
+
+    def cluster(kind, index):
+        return halves(spread[kind, :, index].reshape(size, HD))
+
+    @pl.loop(0, owned // 4)
+    def _(block):
+        for lane in range(4):
+            index = block * 4 + lane
+            present = valid[:, index].reshape(size, LANES)[:, :size] > 0.5
+            qk = cluster(QK, index)
+            scores = jnp.where(present, dot3(qk, qk, NT) / HD, masked_score)
+            raised = jnp.exp(scores - jnp.max(scores, axis=0, keepdims=True))
+            raised = raised / jnp.sum(raised, axis=0, keepdims=True)
+            weights[index] = raised
+            answer[:, index] = dot3(halves(raised), cluster(2, index)).reshape(groups, seat, HD)
+
+    give(GRAD_VALUE)
+    arrive(VALUE)
+
+    @pl.loop(0, groups)
+    def _(group):
+        take(VALUE, group, landed[VALUE, pl.ds(group * GROUP, GROUP)].reshape(wide, HD))
+
+    @pl.loop(0, owned // 4)
+    def _(block):
+        for lane in range(4):
+            index = block * 4 + lane
+            raised = weights[index]
+            slopes = dot3(cluster(VALUE, index), cluster(2, index), NT)
+            middle = jnp.sum(raised * slopes, axis=0, keepdims=True)
+            slopes = raised * (slopes - middle)
+            grad_qk = dot3(halves(slopes + slopes.T), cluster(QK, index)) / HD
+            answer[:, index] = grad_qk.reshape(groups, seat, HD)
+
+    give(GRAD_QK)
+    arrive(GRAD_VALUE)
+    arrive(GRAD_QK)
+
+    @pl.loop(1, OWNERS)
+    def _(step):
+        for kind in range(4):
+            remote(kind, step).wait_send()
+
+
+def cluster_part(pay, slots, marks, early):
+    groups = OWNERS // GROUP
+    owned = TALL // (3 * GROUP)
+    seat = 3 * GROUP
+    size = groups * seat
+    rows = jax.ShapeDtypeStruct((OWNERS, ROOM, HD), f32)
+    return pl.pallas_call(
+        cluster_kernel,
+        out_shape=(rows, rows),
+        in_specs=[pl.BlockSpec(memory_space=pltpu.VMEM)] * 4,
+        out_specs=(pl.BlockSpec(memory_space=pl.ANY),) * 2,
+        scratch_shapes=[
+            pltpu.VMEM((4, OWNERS, ROOM, HD), f32),
+            pltpu.VMEM((2, OWNERS, ROOM, HD), f32),
+            pltpu.VMEM((groups, TALL, GROUP * ROOM), bf16),
+            pltpu.VMEM((3, groups, owned, seat, HD), f32),
+            pltpu.VMEM((groups, owned, seat, LANES), f32),
+            pltpu.VMEM((owned, size, size), f32),
+            pltpu.VMEM((groups, owned, seat, HD), f32),
+            pltpu.SemaphoreType.DMA((4,)),
+            pltpu.SemaphoreType.DMA((4, OWNERS)),
+            pltpu.SemaphoreType.DMA((4, OWNERS)),
+        ],
+        compiler_params=pltpu.CompilerParams(
+            collective_id=2, has_side_effects=True, vmem_limit_bytes=BIG
+        ),
+        name="exchange_and_attend",
+    )(pay, slots, marks, early)
+
+
+def grads_kernel(
+    back_qk_ref, back_value_ref, slots_ref, tokens_ref, full_ref, terms_ref, sums_ref, high, low
+):
     length = tokens_ref.shape[0]
     width = high.shape[1] // 2
-    total = returned_ref.shape[0]
+    total = back_qk_ref.shape[0]
 
     @pl.when(pl.program_id(0) == 0)
     def _():
-        upper, lower = halves(returned_ref[...])
-        source = jnp.concatenate([upper, lower], axis=1)
+        qk_upper, qk_lower = halves(back_qk_ref[...])
+        upper, lower = halves(back_value_ref[...])
+        source = jnp.concatenate([qk_upper, upper, qk_lower, lower], axis=1)
         for head in range(width // HD):
             place = lax.broadcasted_iota(jnp.int32, (length, total), 1)
             chosen = one(place == slots_ref[:, head : head + 1])
@@ -696,10 +947,10 @@
     sums_ref[...] = dot3(halves(tokens_ref[...]), combined, TN)
 
 
-def local_grads(returned, slots, inputs, full):
+def local_grads(back_qk, back_value, slots, inputs, full):
     length, depth = inputs.shape
     both = full.shape[1]
-    total = returned.shape[0]
+    total = back_qk.shape[0]
     return pl.pallas_call(
         grads_kernel,
         grid=(8,),
@@ -708,7 +959,8 @@
             jax.ShapeDtypeStruct((depth, both), f32),
         ),
         in_specs=[
-            pl.BlockSpec((total, 2 * HD), lambda i: (0, 0)),
+            pl.BlockSpec((total, HD), lambda i: (0, 0)),
+            pl.BlockSpec((total, HD), lambda i: (0, 0)),
             pl.BlockSpec(slots.shape, lambda i: (0, 0)),
             pl.BlockSpec((length, depth // 8), lambda i: (0, i)),
             pl.BlockSpec((depth // 8, both), lambda i: (i, 0)),
@@ -720,23 +972,304 @@
         scratch_shapes=[pltpu.VMEM((length, both), bf16)] * 2,
         compiler_params=pltpu.CompilerParams(vmem_limit_bytes=BIG),
         name="unpack_and_grads",
-    )(returned, slots, inputs, full)
+    )(back_qk, back_value, slots, inputs, full)
+
+
+FINISH_COPIES = 14 + 7 + 6
+
+
+def finish_kernel(
+    back_qk_ref, back_value_ref, slots_ref, tokens_ref, full_ref,
+    tokens_out, qk_out, value_out,
+    tokens, full, high, low, terms, away, own, cross_in,
+    column_in, ring_a, ring_b, line_in, plane_in,
+    load_sem, send_sem, recv_sem, column_send, column_recv, cross_send, cross_recv,
+    line_send, line_recv,
+):
+    rep, y, z = position()
+    x = lax.axis_index("tp")
+    length = tokens.shape[0]
+    both = full.shape[1]
+    width = both // 2
+    total = back_qk_ref.shape[0]
+    per_line = NZ * ROWS
+
+    def along_y(step):
+        return {"ctx": lax.rem(y + step, NY) * NZ + z}
+
+    def along_z(step):
+        return {"ctx": y * NZ + lax.rem(z + step, NZ)}
+
+    def along_x(step):
+        return {"tp": lax.rem(x + step, 4)}
+
+    loads = [
+        pltpu.make_async_copy(tokens_ref, tokens, load_sem.at[0]),
+        pltpu.make_async_copy(full_ref, full, load_sem.at[1]),
+    ]
+    for load in loads:
+        load.start()
+    right, left, other = along_z(1), along_z(NZ - 1), {"rep": 1 - rep}
+    barrier = pltpu.get_barrier_semaphore()
+    partners = [along_y(1), along_y(2), along_y(3), right, left, other]
+    partners += [along_x(1), along_x(2), along_x(3)]
+    for partner in partners:
+        pl.semaphore_signal(barrier, inc=1, device_id=partner, device_id_type=MESH)
+
+    qk_upper, qk_lower = halves(back_qk_ref[...])
+    upper, lower = halves(back_value_ref[...])
+    source = jnp.concatenate([qk_upper, upper, qk_lower, lower], axis=1)
+    for head in range(width // HD):
+        place = lax.broadcasted_iota(jnp.int32, (length, total), 1)
+        moved = dot(one(place == slots_ref[:, head : head + 1]), source)
+        upper, lower = halves(moved[:, : 2 * HD] + moved[:, 2 * HD :])
+        for part in range(2):
+            there = pl.ds(part * width + head * HD, HD)
+            high[:, there] = upper[:, part * HD : (part + 1) * HD]
+            low[:, there] = lower[:, part * HD : (part + 1) * HD]
+
+    for load in loads:
+        load.wait()
+    pl.semaphore_wait(barrier, len(partners))
+
+    def columns(step):
+        start = pl.multiple_of(lax.rem(x + step, 4) * width, width)
+        return dot3((high[...], low[...]), halves(full[pl.ds(start, width), :]), NT)
+
+    def sideways(step):
+        return pltpu.make_async_remote_copy(
+            src_ref=terms.at[step - 1],
+            dst_ref=column_in.at[step - 1],
+            send_sem=column_send.at[step - 1],
+            recv_sem=column_recv.at[step - 1],
+            device_id=along_x(step),
+            device_id_type=MESH,
+        )
+
+    @pl.loop(1, 4)
+    def _(step):
+        terms[step - 1] = columns(step)
+        sideways(step).start()
+
+    def line_sum(half, there):
+        start = pl.multiple_of(half * (NY * per_line) + there * per_line, per_line)
+        some = halves(tokens[:, pl.ds(start, per_line)])
+        return dot3(some, (high[...], low[...]), TN).reshape(NZ, ROWS, both)
+
+    def cross(step):
+        there = lax.rem(y + step, NY)
+        return pltpu.make_async_remote_copy(
+            src_ref=away.at[there],
+            dst_ref=cross_in.at[there],
+            send_sem=cross_send.at[step],
+            recv_sem=cross_recv.at[step],
+            device_id=other,
+            device_id_type=MESH,
+        )
+
+    @pl.loop(0, 4)
+    def _(index):
+        step = lax.rem(index + 1, 4)
+        there = lax.rem(y + step, NY)
+        away[there] = line_sum(1 - rep, there)
+        cross(step).start()
+
+    def depth(turn):
+        return lax.rem(z + turn, NZ)
+
+    def piece(step, turn):
+        return pltpu.make_async_remote_copy(
+            src_ref=own.at[lax.rem(y + step, NY), depth(turn), pl.ds(HALF, HALF), :],
+            dst_ref=line_in.at[step - 1, depth(turn)],
+            send_sem=line_send.at[step - 1, turn],
+            recv_sem=line_recv.at[step - 1, turn],
+            device_id=along_y(step),
+            device_id_type=MESH,
+        )
+
+    def own_line(step):
+        there = lax.rem(y + step, NY)
+        mine = line_sum(rep, there)
+        cross(step).wait_recv()
+        own[there] = mine + cross_in[there]
+
+    @pl.loop(1, 4)
+    def _(step):
+        own_line(step)
+        for turn in (4, 5, 3, 6, 2, 7, 1, 0):
+            piece(step, turn).start()
+
+    own_line(0)
+
+    copies = Copies(send_sem, recv_sem)
+
+    def plane(turn, part):
+        return own.at[:, depth(turn), pl.ds(0, HALF), pl.ds(part * width, width)]
+
+    def turn_a(turn, part, before):
+        if turn == 0:
+            return (
+                copies.start(plane(4, part), ring_a.at[part, 0], right),
+                copies.start(plane(5, part), ring_a.at[part, 4], left),
+            )
+        rightward, leftward = before
+        rightward.wait_recv()
+        ring_a[part, turn - 1] += plane(4 - turn, part)[...]
+        rightward = copies.start(ring_a.at[part, turn - 1], ring_a.at[part, turn], right)
+        if turn < 3:
+            leftward.wait_recv()
+            ring_a[part, 3 + turn] += plane(5 + turn, part)[...]
+            leftward = copies.start(ring_a.at[part, 3 + turn], ring_a.at[part, 4 + turn], left)
+        return rightward, leftward
+
+    def along_lines(turn):
+        for step in (1, 2, 3):
+            piece(step, turn).wait_recv()
+        here = depth(turn)
+        return own[y, here, pl.ds(HALF, HALF), :] + (
+            line_in[0, here] + line_in[1, here] + line_in[2, here]
+        )
+
+    def turn_b(turn, before):
+        if turn == 0:
+            own[y, depth(4), pl.ds(HALF, HALF), :] = along_lines(4)
+            own[y, depth(5), pl.ds(HALF, HALF), :] = along_lines(5)
+            return (
+                copies.start(own.at[y, depth(4), pl.ds(HALF, HALF), :], ring_b.at[0], right),
+                copies.start(own.at[y, depth(5), pl.ds(HALF, HALF), :], ring_b.at[4], left),
+            )
+        rightward, leftward = before
+        mine = along_lines(4 - turn)
+        rightward.wait_recv()
+        ring_b[turn - 1] += mine
+        rightward = copies.start(ring_b.at[turn - 1], ring_b.at[turn], right)
+        if turn < 3:
+            mine = along_lines(5 + turn)
+            leftward.wait_recv()
+            ring_b[3 + turn] += mine
+            leftward = copies.start(ring_b.at[3 + turn], ring_b.at[4 + turn], left)
+        return rightward, leftward
+
+    flow_a, flow_b = [None, None], None
+    for turn in range(4):
+        for part in range(2):
+            flow_a[part] = turn_a(turn, part, flow_a[part])
+        if turn == 0:
+            tokens_out[...] = columns(0)
+        flow_b = turn_b(turn, flow_b)
+    planes = []
+    for part in range(2):
+        for copy in flow_a[part]:
+            copy.wait_recv()
+        own[:, z, pl.ds(0, HALF), pl.ds(part * width, width)] = plane(0, part)[...] + (
+            ring_a[part, 3] + ring_a[part, 6]
+        )
+        for step in (1, 3, 2):
+            planes.append(copies.start(
+                own.at[lax.rem(y + step, NY), z, pl.ds(0, HALF), pl.ds(part * width, width)],
+                plane_in.at[part, step - 1],
+                along_y(step),
+            ))
+    mine = along_lines(0)
+    for copy in flow_b:
+        copy.wait_recv()
+    lower = mine + ring_b[3] + ring_b[6]
+    qk_out[pl.ds(HALF, HALF), :] = lower[:, :width]
+    value_out[pl.ds(HALF, HALF), :] = lower[:, width:]
+
+    @pl.loop(1, 4)
+    def _(step):
+        sideways(step).wait()
+
+    @pl.loop(0, length // 8)
+    def _(block):
+        here = pl.ds(pl.multiple_of(block * 8, 8), 8)
+        tokens_out[here, :] += column_in[0, here, :] + column_in[1, here, :] + column_in[2, here, :]
+
+    for copy in planes:
+        copy.wait_recv()
+    for part, out in enumerate((qk_out, value_out)):
+        out[pl.ds(0, HALF), :] = own[y, z, pl.ds(0, HALF), pl.ds(part * width, width)] + (
+            plane_in[part, 0] + plane_in[part, 1] + plane_in[part, 2]
+        )
+
+    @pl.loop(0, 4)
+    def _(step):
+        cross(step).wait_send()
+
+    @pl.loop(1, 4)
+    def _(step):
+        for turn in range(NZ):
+            piece(step, turn).wait_send()
+
+    copies.finish()
+    assert len(copies.all) == FINISH_COPIES
+
+
+def finish(back_qk, back_value, slots, inputs, full):
+    length, depth = inputs.shape
+    both = full.shape[1]
+    width = both // 2
+    vmem, anywhere = pl.BlockSpec(memory_space=pltpu.VMEM), pl.BlockSpec(memory_space=pl.ANY)
+    return pl.pallas_call(
+        finish_kernel,
+        out_shape=(
+            jax.ShapeDtypeStruct((length, width), f32),
+            jax.ShapeDtypeStruct((ROWS, width), f32),
+            jax.ShapeDtypeStruct((ROWS, width), f32),
+        ),
+        in_specs=[vmem, vmem, vmem, anywhere, anywhere],
+        out_specs=(vmem,) * 3,
+        scratch_shapes=[
+            pltpu.VMEM((length, depth), f32),
+            pltpu.VMEM((depth, both), f32),
+            pltpu.VMEM((length, both), bf16),
+            pltpu.VMEM((length, both), bf16),
+            pltpu.VMEM((3, length, width), f32),
+            pltpu.VMEM((NY, NZ, ROWS, both), f32),
+            pltpu.VMEM((NY, NZ, ROWS, both), f32),
+            pltpu.VMEM((NY, NZ, ROWS, both), f32),
+            pltpu.VMEM((3, length, width), f32),
+            pltpu.VMEM((2, 7, NY, HALF, width), f32),
+            pltpu.VMEM((7, HALF, both), f32),
+            pltpu.VMEM((3, NZ, HALF, both), f32),
+            pltpu.VMEM((2, 3, HALF, width), f32),
+            pltpu.SemaphoreType.DMA((2,)),
+            pltpu.SemaphoreType.DMA((FINISH_COPIES,)),
+            pltpu.SemaphoreType.DMA((FINISH_COPIES,)),
+            pltpu.SemaphoreType.DMA((3,)),
+            pltpu.SemaphoreType.DMA((3,)),
+            pltpu.SemaphoreType.DMA((4,)),
+            pltpu.SemaphoreType.DMA((4,)),
+            pltpu.SemaphoreType.DMA((3, NZ)),
+            pltpu.SemaphoreType.DMA((3, NZ)),
+        ],
+        compiler_params=pltpu.CompilerParams(
+            collective_id=3, has_side_effects=True, vmem_limit_bytes=52 * 2**20
+        ),
+        name="grads_and_scatter",
+    )(back_qk, back_value, slots, inputs, full)
 
 
 def exchange(array):
     return lax.all_to_all(array, "ctx", split_axis=0, concat_axis=0, tiled=True)
 
 
-def middle_part(room, inputs, full, early, marks, slots):
-    rows = pack_rows(inputs, full, slots.reshape(1, -1), room)
-    rows = exchange(rows.reshape(OWNERS, room, 2 * HD)).reshape(OWNERS * room, 2 * HD)
+def seat_numbers(marks, room):
     marks = marks.astype(jnp.int32) - 1
     source = lax.broadcasted_iota(jnp.int32, marks.shape, 0) % GROUP
     seats = (marks // 3) * (3 * GROUP) + source * 3 + marks % 3
-    seats = jnp.where(marks < 0, -1, seats).reshape(OWNERS // GROUP, 1, GROUP * room)
-    replies = attend(rows, early, seats, room)
-    returned = exchange(replies.reshape(OWNERS, room, 2 * HD)).reshape(OWNERS * room, 2 * HD)
-    return local_grads(returned, slots.T, inputs, full)
+    return jnp.where(marks < 0, -1, seats).reshape(OWNERS // GROUP, 1, GROUP * room)
+
+
+def snug_part(inputs, full, pay, early, slots, tall_slots):
+    marks = early[:, ROOM : ROOM + 2, :ROOM]
+    held, place = marks[:, 0], marks[:, 1]
+    seats = jnp.where(held > 0.5, (held - 1) * (3 * GROUP) + place, -1.0).astype(jnp.int32)
+    seats = seats.reshape(OWNERS // GROUP, 1, GROUP * ROOM)
+    back = cluster_part(pay, slots, seats, early)
+    back_qk, back_value = (rows.reshape(OWNERS * ROOM, HD) for rows in back)
+    return finish(back_qk, back_value, tall_slots, inputs, full)
 
 
 def roomy_part(inputs, full, upstream, cluster):
@@ -755,7 +1288,13 @@
     early = jnp.zeros((OWNERS * SLOTS, HD), f32).at[slots.reshape(-1)].set(rows)
     early = exchange(early.reshape(OWNERS, SLOTS, HD))
     marks = exchange(marks.reshape(OWNERS, SLOTS))
-    return middle_part(SLOTS, inputs, full, early, marks, slots)
+    rows = pack_rows(inputs, full, slots.reshape(1, -1), SLOTS)
+    rows = exchange(rows.reshape(OWNERS, SLOTS, 2 * HD)).reshape(OWNERS * SLOTS, 2 * HD)
+    replies = attend(rows, early, seat_numbers(marks, SLOTS), SLOTS)
+    returned = exchange(replies.reshape(OWNERS, SLOTS, 2 * HD)).reshape(OWNERS * SLOTS, 2 * HD)
+    return scatter_sums(
+        *local_grads(returned[:, :HD], returned[:, HD:], slots.T, inputs, full)
+    )
 
 
 def per_device(tokens, qk_weight, value_weight, grad_out, assign):
@@ -763,23 +1302,23 @@
     heads_here = qk_weight.shape[1] // HD
     width = heads_here * HD
     cluster = assign[:, 0, :, 0]
-    full, early, slots = gather_weights(
-        qk_weight, value_weight, jnp.pad(cluster, ((0, 8 - heads_here), (0, 0))), grad_out[0]
+    full, early, slots, tall_slots, pay = gather_and_project(
+        qk_weight, value_weight, jnp.pad(cluster, ((0, 8 - heads_here), (0, 0))), grad_out[0],
+        inputs,
     )
     full = full.reshape(-1, 2 * width)
     fullest = jnp.max(early[:, ROOM, PITCH])
 
-    def snug(inputs, full, upstream, cluster, early, slots):
-        marks = early[:, ROOM, :ROOM]
-        return middle_part(ROOM, inputs, full, early, marks, slots[:heads_here])
-
-    def roomy(inputs, full, upstream, cluster, early, slots):
+    def snug(inputs, full, upstream, cluster, *routed):
+        return snug_part(inputs, full, *routed)
+
+    def roomy(inputs, full, upstream, cluster, *routed):
         return roomy_part(inputs, full, upstream, cluster)
 
-    token_terms, weight_terms = lax.cond(
-        fullest <= ROOM, snug, roomy, inputs, full, grad_out[0], cluster, early, slots
+    grad_tokens, grad_qk_weight, grad_value_weight = lax.cond(
+        fullest <= ROOM, snug, roomy,
+        inputs, full, grad_out[0], cluster, pay, early, slots, tall_slots,
     )
-    grad_tokens, grad_qk_weight, grad_value_weight = scatter_sums(token_terms, weight_terms)
     return (grad_tokens[None], grad_qk_weight, grad_value_weight)
 
 

time: 299 us -> 252 us (0.84)
  Pallas kernels: 188 us -> 242 us
  blocking collectives: 51.4 us -> 0 us
  waiting for transfers between devices: 44.3 us -> 0 us
  starting transfers between devices: 4.82 us -> 0 us
    pallas_call x5 -> x3, Pallas kernels: 188 us -> 242 us  [the longest x1 91.7 us: cluster_part(): pl.pallas_call(cluster_kernel, out_shape=(rows, rows), in_specs=[pl.Block...]
    all_to_all x1 -> x0, blocking collectives: 51.4 us -> none  [exchange(): return lax.all_to_all(array, 'ctx', split_axis=0, concat_axis=0, tiled=True)]
    all_to_all x1 -> x0, waiting for transfers between devices: 44.3 us -> none  [exchange(): return lax.all_to_all(array, 'ctx', split_axis=0, concat_axis=0, tiled=True)]
    all_to_all x1 -> x0, starting transfers between devices: 4.82 us -> none  [exchange(): return lax.all_to_all(array, 'ctx', split_axis=0, concat_axis=0, tiled=True)]
  transfers between devices with their start and end apart: 1 -> 0, of which waited for: 1 -> 0; matrix products, arithmetic and copies ran while one was open for 0% -> 0% of each run, Pallas kernels for 0% -> 0%
where the time goes in v4:
time: 252 us; the launch traced here: 251 us
  Pallas kernels  242 us (96%)
  local copies, waits for them, and re-layouts  5.65 us (2%)
    pallas_call x1, Pallas kernels, cluster_part(): pl.pallas_call(cluster_kernel, out_shape=(rows, rows), in_specs=[pl.Block...  91.7 us
    pallas_call x1, Pallas kernels, gather_and_project(): pl.pallas_call(gather_kernel, out_shape=(jax.ShapeDtypeStruct((2, NY, NZ,...  88.8 us
    pallas_call x1, Pallas kernels, finish(): pl.pallas_call(finish_kernel, out_shape=(jax.ShapeDtypeStruct((length, wi...  61.3 us
    unnamed x14, local copies, waits for them, and re-layouts  5.55 us

profile of v4, /device:TPU:2, one launch (start us, length us, event | category | flops | bytes accessed | tf_op | source)
XLA Modules:
  0.0 251.2 jit_solution(17783544190952823100)
XLA Ops:
  0.6 0.0 copy-start.6
  0.6 0.8 copy.50
  1.4 0.0 copy-start.1
  1.4 0.8 copy-done.1
  2.2 0.0 copy-start.2
  2.2 0.8 copy-done.2
  3.1 0.0 copy-start.4
  3.1 88.8 %gather_and_project.1 = (f32[2,4,8,32,1024]{4,3,2,1,0:T(8,128)}, f32[32,64,128]{2,1,0:T(8,128)S(1)}, s32[1,1536]{1,0:T(1,128)S(1)}, s32[384,128]{1,0:T(8,128)S(1)}, bf16[2,1536,256]{2,1,0:T(8,128)(2,1)S(1)}) custom-call(f32[32,512]{1,0:T(8,128)S(1)} %copy-done.1, f32[32,512]{1,0:T(8,128)S(1)} %copy-done.2, s32[8,384]{1,0:T(8,128)S(1)} %pad.4.cluster_ref, ...), custom_call_target="tpu_custom_call" | custom-call | tf_op jit(solution)/shard_map/gather_and_project/pallas_call | solution.py:389
  91.9 0.0 copy-start.5
  91.9 1.0 copy-done.5
  92.9 0.7 slice_reduce_fusion
  94.2 0.0 copy-done.6
  94.2 0.0 copy-done.4
  94.2 154.8 %conditional.1 = (f32[32,512]{1,0:T(8,128)S(1)}, f32[32,512]{1,0:T(8,128)S(1)}, f32[1,384,512]{2,1,0:T(8,128)S(1)}) conditional(s32[]{:T(128)} %convert_element_type.30, (s32[4,384]{1,0:T(4,128)S(1)}, s32[4,1,384,1]{2,3,1,0:T(1,128)S(1)}, f32[384,2048]{1,0:T(8,128)}, f32[2048,1024]{1,0:T(8,128)}, f32[1,384,512]{2,1,0:T(8,128)S(1)}) %tuple.42, ...), branch_computations={%region_1.5_spmd, %region_5.6_spmd} | conditional | flops 2620740 | bytes 82510656 | solution.py:1318
  94.5 1.1 fusion.1
  95.6 0.1 reshape.292.marks_ref
  95.6 91.7 %exchange_and_attend.1 = (f32[32,56,128]{2,1,0:T(8,128)S(1)}, f32[32,56,128]{2,1,0:T(8,128)S(1)}) custom-call(bf16[2,1536,256]{2,1,0:T(8,128)(2,1)S(1)} %get-tuple-element.39.pay_ref, s32[1,1536]{1,0:T(1,128)S(1)} %get-tuple-element.40.slots_ref, s32[4,1,448]{2,1,0:T(1,128)S(1)} %reshape.292.marks_ref, f32[32,64,128]{2,1,0:T(8,128)} %get-tuple-element.41.early_ref), custom_call_target="tpu_custom_call" | custom-call | tf_op jit(solution)/shard_map/cond/branch_1_fun/exchange_and_attend/pallas_call | solution.py:899
  187.4 61.3 %grads_and_scatter.1 = (f32[384,512]{1,0:T(8,128)S(1)}, f32[32,512]{1,0:T(8,128)S(1)}, f32[32,512]{1,0:T(8,128)S(1)}) custom-call(f32[1792,128]{1,0:T(8,128)S(1)} %bitcast.33, f32[1792,128]{1,0:T(8,128)S(1)} %bitcast.34, s32[384,128]{1,0:T(8,128)S(1)} %get-tuple-element.44.slots_ref, f32[384,2048]{1,0:T(8,128)} %get-tuple-element.45.tokens_ref, ...), custom_call_target="tpu_custom_call" | custom-call | tf_op jit(solution)/shard_map/cond/branch_1_fun/grads_and_scatter/pallas_call | solution.py:1214
  249.0 0.9 copy.60
  249.9 0.6 copy.61
  250.6 0.6 copy.62
  (1 shorter events, 0.0 us)
Async XLA Ops:
  0.6 93.6 %copy-start.6 = (s32[4,1,384,1]{2,3,1,0:T(1,128)S(1)}, s32[4,1,384,1]{2,3,1,0:T(1,128)}, u32[]{:S(2)}) copy-start(s32[4,1,384,1]{2,3,1,0:T(1,128)} %param.11) | copy-start | bytes 18436
  1.4 0.8 copy-start.1
  2.2 0.8 copy-start.2
  3.1 91.2 %copy-start.4 = (f32[1,384,512]{2,1,0:T(8,128)S(1)}, f32[1,384,512]{2,1,0:T(8,128)}, u32[]{:S(2)}) copy-start(f32[1,384,512]{2,1,0:T(8,128)} %param.10) | copy-start | bytes 2359300
  91.9 1.0 copy-start.5

commit v5 on v4

--- a/solution.py
+++ b/solution.py
@@ -281,23 +281,16 @@
         marked = jnp.where(row == 0, (held + 1).astype(f32), jnp.where(row == 1, within, 0.0))
         ids_row[:, here] = marked.astype(bf16)
         slots_list.append(jnp.where(rank < ROOM, owner * ROOM + rank, -1))
-        if head < 3:
-            turn_pieces(head + 1)
     most[0] = jnp.broadcast_to(highest, (8, LANES))
     tall = jnp.concatenate(
         slots_list + [jnp.zeros((LANES - heads, length), jnp.int32)], axis=0
     )
     tall_slots_ref[...] = tall.astype(f32).T.astype(jnp.int32)
     fullest = [routes.start(most.at[0], most.at[step], along_x(step)) for step in (1, 2, 3)]
-    across.append(copies.start(line(0), line(0), other))
+    turn_pieces(1)
     turn_planes(0)
-    for copy in fullest:
-        copy.wait_recv()
-    most[4] = jnp.maximum(jnp.maximum(most[0], most[1]), jnp.maximum(most[2], most[3]))
-    fullest = routes.start(most.at[4], most.at[5], other)
-
-    @pl.loop(0, OWNERS // 4)
-    def _(block):
+
+    def pack_early(block):
         rows = 4 * PITCH
         place = lax.broadcasted_iota(jnp.int32, (rows, heads * length), 0) + block * rows
         chosen = one(place == slots_row[...])
@@ -310,6 +303,23 @@
                 :, lane * PITCH : (lane + 1) * PITCH
             ]
 
+    @pl.loop(0, OWNERS // 8)
+    def _(block):
+        pack_early(block)
+
+    for copy in fullest:
+        copy.wait_recv()
+    most[4] = jnp.maximum(jnp.maximum(most[0], most[1]), jnp.maximum(most[2], most[3]))
+    fullest = routes.start(most.at[4], most.at[5], other)
+    turn_pieces(2)
+
+    @pl.loop(OWNERS // 8, OWNERS // 4)
+    def _(block):
+        pack_early(block)
+
+    turn_pieces(3)
+    turn_planes(1)
+    across.append(copies.start(line(0), line(0), other))
     fullest.wait_recv()
     overall = jnp.maximum(most[4], most[5])[:, :PITCH]
 
@@ -328,14 +338,19 @@
             device_id_type=MESH,
         )
 
-    @pl.loop(1, OWNERS)
+    @pl.loop(1, OWNERS // 2)
     def _(step):
         early(step).start()
 
     stay = pltpu.make_async_copy(early_out.at[me], early_ref.at[me], local_sem.at[0])
     stay.start()
-    for step in range(1, 4):
-        turn_planes(step)
+    turn_planes(2)
+    turn_planes(3)
+
+    @pl.loop(OWNERS // 2, OWNERS)
+    def _(step):
+        early(step).start()
+
     for step in (1, 3, 2):
         for copy in passed[step]:
             copy.wait_recv()
@@ -975,15 +990,15 @@
     )(back_qk, back_value, slots, inputs, full)
 
 
-FINISH_COPIES = 14 + 7 + 6
+FINISH_COPIES = 2 + 14 + 14 + 4 + 6
 
 
 def finish_kernel(
     back_qk_ref, back_value_ref, slots_ref, tokens_ref, full_ref,
     tokens_out, qk_out, value_out,
     tokens, full, high, low, terms, away, own, cross_in,
-    column_in, ring_a, ring_b, line_in, plane_in,
-    load_sem, send_sem, recv_sem, column_send, column_recv, cross_send, cross_recv,
+    column_in, passing, ring_a, ring_b, line_in, plane_in,
+    load_sem, send_sem, recv_sem, cross_send, cross_recv,
     line_send, line_recv,
 ):
     rep, y, z = position()
@@ -1012,195 +1027,227 @@
     right, left, other = along_z(1), along_z(NZ - 1), {"rep": 1 - rep}
     barrier = pltpu.get_barrier_semaphore()
     partners = [along_y(1), along_y(2), along_y(3), right, left, other]
-    partners += [along_x(1), along_x(2), along_x(3)]
+    partners += [along_x(1), along_x(3)]
     for partner in partners:
         pl.semaphore_signal(barrier, inc=1, device_id=partner, device_id_type=MESH)
 
-    qk_upper, qk_lower = halves(back_qk_ref[...])
-    upper, lower = halves(back_value_ref[...])
-    source = jnp.concatenate([qk_upper, upper, qk_lower, lower], axis=1)
-    for head in range(width // HD):
-        place = lax.broadcasted_iota(jnp.int32, (length, total), 1)
-        moved = dot(one(place == slots_ref[:, head : head + 1]), source)
-        upper, lower = halves(moved[:, : 2 * HD] + moved[:, 2 * HD :])
-        for part in range(2):
+    def unpack(part, back_ref):
+        source = jnp.concatenate(halves(back_ref[...]), axis=1)
+        for head in range(width // HD):
+            place = lax.broadcasted_iota(jnp.int32, (length, total), 1)
+            moved = dot(one(place == slots_ref[:, head : head + 1]), source)
             there = pl.ds(part * width + head * HD, HD)
-            high[:, there] = upper[:, part * HD : (part + 1) * HD]
-            low[:, there] = lower[:, part * HD : (part + 1) * HD]
-
-    for load in loads:
-        load.wait()
-    pl.semaphore_wait(barrier, len(partners))
+            high[:, there], low[:, there] = halves(moved[:, :HD] + moved[:, HD:])
+
+    def line_sum(half, there, part):
+        start = pl.multiple_of(half * (NY * per_line) + there * per_line, per_line)
+        some = halves(tokens[:, pl.ds(start, per_line)])
+        here = pl.ds(part * width, width)
+        return dot3(some, (high[:, here], low[:, here]), TN).reshape(NZ, ROWS, width)
+
+    def cross(step, part):
+        there = lax.rem(y + step, NY)
+        return pltpu.make_async_remote_copy(
+            src_ref=away.at[part, there],
+            dst_ref=cross_in.at[part, there],
+            send_sem=cross_send.at[part, step],
+            recv_sem=cross_recv.at[part, step],
+            device_id=other,
+            device_id_type=MESH,
+        )
+
+    def away_lines(part):
+        @pl.loop(0, NY)
+        def _(step):
+            there = lax.rem(y + step, NY)
+            away[part, there] = line_sum(1 - rep, there, part)
+            cross(step, part).start()
+
+    def own_lines(part):
+        @pl.loop(0, NY)
+        def _(step):
+            there = lax.rem(y + step, NY)
+            mine = line_sum(rep, there, part)
+            cross(step, part).wait_recv()
+            own[part, there] = mine + cross_in[part, there]
+
+    def depth(turn):
+        return lax.rem(z + turn, NZ)
+
+    def piece(step, turn, part):
+        return pltpu.make_async_remote_copy(
+            src_ref=own.at[part, lax.rem(y + step, NY), depth(turn), pl.ds(HALF, HALF), :],
+            dst_ref=line_in.at[part, step - 1, depth(turn)],
+            send_sem=line_send.at[part, step - 1, turn],
+            recv_sem=line_recv.at[part, step - 1, turn],
+            device_id=along_y(step),
+            device_id_type=MESH,
+        )
+
+    def send_pieces(part):
+        for turn in (4, 5, 3, 6, 2, 7, 1, 0):
+            for step in (1, 3, 2):
+                piece(step, turn, part).start()
+
+    copies = Copies(send_sem, recv_sem)
+
+    def plane(turn, part):
+        return own.at[part, :, depth(turn), pl.ds(0, HALF), :]
+
+    flow_a, flow_b = [None, None], [None, None]
+
+    def turn_a(turn, part):
+        ring = ring_a.at[part]
+        if turn == 0:
+            flow_a[part] = (
+                copies.start(plane(4, part), ring.at[0], right),
+                copies.start(plane(5, part), ring.at[4], left),
+            )
+            return
+        rightward, leftward = flow_a[part]
+        rightward.wait_recv()
+        ring_a[part, turn - 1] += plane(4 - turn, part)[...]
+        rightward = copies.start(ring.at[turn - 1], ring.at[turn], right)
+        if turn < 3:
+            leftward.wait_recv()
+            ring_a[part, 3 + turn] += plane(5 + turn, part)[...]
+            leftward = copies.start(ring.at[3 + turn], ring.at[4 + turn], left)
+        flow_a[part] = rightward, leftward
+
+    def along_lines(turn, part):
+        for step in (1, 2, 3):
+            piece(step, turn, part).wait_recv()
+        here = depth(turn)
+        return own[part, y, here, pl.ds(HALF, HALF), :] + (
+            line_in[part, 0, here] + line_in[part, 1, here] + line_in[part, 2, here]
+        )
+
+    def turn_b(turn, part):
+        ring = ring_b.at[part]
+        if turn == 0:
+            first = own.at[part, y, depth(4), pl.ds(HALF, HALF), :]
+            second = own.at[part, y, depth(5), pl.ds(HALF, HALF), :]
+            first[...] = along_lines(4, part)
+            rightward = copies.start(first, ring.at[0], right)
+            second[...] = along_lines(5, part)
+            flow_b[part] = rightward, copies.start(second, ring.at[4], left)
+            return
+        rightward, leftward = flow_b[part]
+        mine = along_lines(4 - turn, part)
+        rightward.wait_recv()
+        ring_b[part, turn - 1] += mine
+        rightward = copies.start(ring.at[turn - 1], ring.at[turn], right)
+        if turn < 3:
+            mine = along_lines(5 + turn, part)
+            leftward.wait_recv()
+            ring_b[part, 3 + turn] += mine
+            leftward = copies.start(ring.at[3 + turn], ring.at[4 + turn], left)
+        flow_b[part] = rightward, leftward
+
+    planes = [[], []]
+
+    def end_a(part):
+        for copy in flow_a[part]:
+            copy.wait_recv()
+        own[part, :, z, pl.ds(0, HALF), :] = plane(0, part)[...] + (
+            ring_a[part, 3] + ring_a[part, 6]
+        )
+        for step in (1, 3, 2):
+            planes[part].append(copies.start(
+                own.at[part, lax.rem(y + step, NY), z, pl.ds(0, HALF), :],
+                plane_in.at[part, step - 1],
+                along_y(step),
+            ))
+
+    def end_b(part, out):
+        mine = along_lines(0, part)
+        for copy in flow_b[part]:
+            copy.wait_recv()
+        out[pl.ds(HALF, HALF), :] = mine + ring_b[part, 3] + ring_b[part, 6]
+
+    middle = length // 2
+    upper_rows, lower_rows = pl.ds(0, middle), pl.ds(middle, middle)
 
     def columns(step):
         start = pl.multiple_of(lax.rem(x + step, 4) * width, width)
         return dot3((high[...], low[...]), halves(full[pl.ds(start, width), :]), NT)
 
-    def sideways(step):
-        return pltpu.make_async_remote_copy(
-            src_ref=terms.at[step - 1],
-            dst_ref=column_in.at[step - 1],
-            send_sem=column_send.at[step - 1],
-            recv_sem=column_recv.at[step - 1],
-            device_id=along_x(step),
-            device_id_type=MESH,
-        )
-
-    @pl.loop(1, 4)
-    def _(step):
-        terms[step - 1] = columns(step)
-        sideways(step).start()
-
-    def line_sum(half, there):
-        start = pl.multiple_of(half * (NY * per_line) + there * per_line, per_line)
-        some = halves(tokens[:, pl.ds(start, per_line)])
-        return dot3(some, (high[...], low[...]), TN).reshape(NZ, ROWS, both)
-
-    def cross(step):
-        there = lax.rem(y + step, NY)
-        return pltpu.make_async_remote_copy(
-            src_ref=away.at[there],
-            dst_ref=cross_in.at[there],
-            send_sem=cross_send.at[step],
-            recv_sem=cross_recv.at[step],
-            device_id=other,
-            device_id_type=MESH,
-        )
-
-    @pl.loop(0, 4)
-    def _(index):
-        step = lax.rem(index + 1, 4)
-        there = lax.rem(y + step, NY)
-        away[there] = line_sum(1 - rep, there)
-        cross(step).start()
-
-    def depth(turn):
-        return lax.rem(z + turn, NZ)
-
-    def piece(step, turn):
-        return pltpu.make_async_remote_copy(
-            src_ref=own.at[lax.rem(y + step, NY), depth(turn), pl.ds(HALF, HALF), :],
-            dst_ref=line_in.at[step - 1, depth(turn)],
-            send_sem=line_send.at[step - 1, turn],
-            recv_sem=line_recv.at[step - 1, turn],
-            device_id=along_y(step),
-            device_id_type=MESH,
-        )
-
-    def own_line(step):
-        there = lax.rem(y + step, NY)
-        mine = line_sum(rep, there)
-        cross(step).wait_recv()
-        own[there] = mine + cross_in[there]
-
-    @pl.loop(1, 4)
-    def _(step):
-        own_line(step)
-        for turn in (4, 5, 3, 6, 2, 7, 1, 0):
-            piece(step, turn).start()
-
-    own_line(0)
-
-    copies = Copies(send_sem, recv_sem)
-
-    def plane(turn, part):
-        return own.at[:, depth(turn), pl.ds(0, HALF), pl.ds(part * width, width)]
-
-    def turn_a(turn, part, before):
-        if turn == 0:
-            return (
-                copies.start(plane(4, part), ring_a.at[part, 0], right),
-                copies.start(plane(5, part), ring_a.at[part, 4], left),
-            )
-        rightward, leftward = before
-        rightward.wait_recv()
-        ring_a[part, turn - 1] += plane(4 - turn, part)[...]
-        rightward = copies.start(ring_a.at[part, turn - 1], ring_a.at[part, turn], right)
-        if turn < 3:
-            leftward.wait_recv()
-            ring_a[part, 3 + turn] += plane(5 + turn, part)[...]
-            leftward = copies.start(ring_a.at[part, 3 + turn], ring_a.at[part, 4 + turn], left)
-        return rightward, leftward
-
-    def along_lines(turn):
-        for step in (1, 2, 3):
-            piece(step, turn).wait_recv()
-        here = depth(turn)
-        return own[y, here, pl.ds(HALF, HALF), :] + (
-            line_in[0, here] + line_in[1, here] + line_in[2, here]
-        )
-
-    def turn_b(turn, before):
-        if turn == 0:
-            own[y, depth(4), pl.ds(HALF, HALF), :] = along_lines(4)
-            own[y, depth(5), pl.ds(HALF, HALF), :] = along_lines(5)
-            return (
-                copies.start(own.at[y, depth(4), pl.ds(HALF, HALF), :], ring_b.at[0], right),
-                copies.start(own.at[y, depth(5), pl.ds(HALF, HALF), :], ring_b.at[4], left),
-            )
-        rightward, leftward = before
-        mine = along_lines(4 - turn)
-        rightward.wait_recv()
-        ring_b[turn - 1] += mine
-        rightward = copies.start(ring_b.at[turn - 1], ring_b.at[turn], right)
-        if turn < 3:
-            mine = along_lines(5 + turn)
-            leftward.wait_recv()
-            ring_b[3 + turn] += mine
-            leftward = copies.start(ring_b.at[3 + turn], ring_b.at[4 + turn], left)
-        return rightward, leftward
-
-    flow_a, flow_b = [None, None], None
-    for turn in range(4):
-        for part in range(2):
-            flow_a[part] = turn_a(turn, part, flow_a[part])
-        if turn == 0:
-            tokens_out[...] = columns(0)
-        flow_b = turn_b(turn, flow_b)
-    planes = []
-    for part in range(2):
-        for copy in flow_a[part]:
-            copy.wait_recv()
-        own[:, z, pl.ds(0, HALF), pl.ds(part * width, width)] = plane(0, part)[...] + (
-            ring_a[part, 3] + ring_a[part, 6]
-        )
-        for step in (1, 3, 2):
-            planes.append(copies.start(
-                own.at[lax.rem(y + step, NY), z, pl.ds(0, HALF), pl.ds(part * width, width)],
-                plane_in.at[part, step - 1],
-                along_y(step),
-            ))
-    mine = along_lines(0)
-    for copy in flow_b:
+    unpack(1, back_value_ref)
+    loads[0].wait()
+    pl.semaphore_wait(barrier, len(partners))
+    away_lines(1)
+    own_lines(1)
+    turn_a(0, 1)
+    send_pieces(1)
+    unpack(0, back_qk_ref)
+    turn_a(1, 1)
+    away_lines(0)
+    turn_b(0, 1)
+    turn_a(2, 1)
+    own_lines(0)
+    turn_a(0, 0)
+    send_pieces(0)
+    turn_b(1, 1)
+    loads[1].wait()
+    terms[1] = columns(2)
+    by_right = copies.start(terms.at[1, upper_rows], passing.at[0], along_x(1))
+    by_left = copies.start(terms.at[1, lower_rows], passing.at[1], along_x(3))
+    turn_a(3, 1)
+    turn_b(2, 1)
+    terms[0] = columns(1)
+    sideways = [copies.start(terms.at[0, lower_rows], column_in.at[0, lower_rows], along_x(1))]
+    turn_a(1, 0)
+    turn_b(3, 1)
+    terms[2] = columns(3)
+    sideways.append(
+        copies.start(terms.at[2, upper_rows], column_in.at[1, upper_rows], along_x(3))
+    )
+    turn_b(0, 0)
+    end_a(1)
+    turn_a(2, 0)
+    by_right.wait_recv()
+    terms[0, upper_rows, :] += passing[0]
+    sideways.append(
+        copies.start(terms.at[0, upper_rows], column_in.at[0, upper_rows], along_x(1))
+    )
+    by_left.wait_recv()
+    terms[2, lower_rows, :] += passing[1]
+    sideways.append(
+        copies.start(terms.at[2, lower_rows], column_in.at[1, lower_rows], along_x(3))
+    )
+    turn_b(1, 0)
+    turn_a(3, 0)
+    end_b(1, value_out)
+    turn_b(2, 0)
+    tokens_out[...] = columns(0)
+    turn_b(3, 0)
+    end_a(0)
+    end_b(0, qk_out)
+    for copy in sideways:
         copy.wait_recv()
-    lower = mine + ring_b[3] + ring_b[6]
-    qk_out[pl.ds(HALF, HALF), :] = lower[:, :width]
-    value_out[pl.ds(HALF, HALF), :] = lower[:, width:]
-
-    @pl.loop(1, 4)
-    def _(step):
-        sideways(step).wait()
 
     @pl.loop(0, length // 8)
     def _(block):
         here = pl.ds(pl.multiple_of(block * 8, 8), 8)
-        tokens_out[here, :] += column_in[0, here, :] + column_in[1, here, :] + column_in[2, here, :]
-
-    for copy in planes:
-        copy.wait_recv()
-    for part, out in enumerate((qk_out, value_out)):
-        out[pl.ds(0, HALF), :] = own[y, z, pl.ds(0, HALF), pl.ds(part * width, width)] + (
+        tokens_out[here, :] += column_in[0, here, :] + column_in[1, here, :]
+
+    for part, out in ((1, value_out), (0, qk_out)):
+        for copy in planes[part]:
+            copy.wait_recv()
+        out[pl.ds(0, HALF), :] = own[part, y, z, pl.ds(0, HALF), :] + (
             plane_in[part, 0] + plane_in[part, 1] + plane_in[part, 2]
         )
 
-    @pl.loop(0, 4)
+    @pl.loop(0, NY)
     def _(step):
-        cross(step).wait_send()
-
-    @pl.loop(1, 4)
+        for part in range(2):
+            cross(step, part).wait_send()
+
+    @pl.loop(1, NY)
     def _(step):
-        for turn in range(NZ):
-            piece(step, turn).wait_send()
+        for part in range(2):
+            for turn in range(NZ):
+                piece(step, turn, part).wait_send()
 
     copies.finish()
     assert len(copies.all) == FINISH_COPIES
@@ -1226,23 +1273,22 @@
             pltpu.VMEM((length, both), bf16),
             pltpu.VMEM((length, both), bf16),
             pltpu.VMEM((3, length, width), f32),
-            pltpu.VMEM((NY, NZ, ROWS, both), f32),
-            pltpu.VMEM((NY, NZ, ROWS, both), f32),
-            pltpu.VMEM((NY, NZ, ROWS, both), f32),
-            pltpu.VMEM((3, length, width), f32),
+            pltpu.VMEM((2, NY, NZ, ROWS, width), f32),
+            pltpu.VMEM((2, NY, NZ, ROWS, width), f32),
+            pltpu.VMEM((2, NY, NZ, ROWS, width), f32),
+            pltpu.VMEM((2, length, width), f32),
+            pltpu.VMEM((2, length // 2, width), f32),
             pltpu.VMEM((2, 7, NY, HALF, width), f32),
-            pltpu.VMEM((7, HALF, both), f32),
-            pltpu.VMEM((3, NZ, HALF, both), f32),
+            pltpu.VMEM((2, 7, HALF, width), f32),
+            pltpu.VMEM((2, 3, NZ, HALF, width), f32),
             pltpu.VMEM((2, 3, HALF, width), f32),
             pltpu.SemaphoreType.DMA((2,)),
             pltpu.SemaphoreType.DMA((FINISH_COPIES,)),
             pltpu.SemaphoreType.DMA((FINISH_COPIES,)),
-            pltpu.SemaphoreType.DMA((3,)),
-            pltpu.SemaphoreType.DMA((3,)),
-            pltpu.SemaphoreType.DMA((4,)),
-            pltpu.SemaphoreType.DMA((4,)),
-            pltpu.SemaphoreType.DMA((3, NZ)),
-            pltpu.SemaphoreType.DMA((3, NZ)),
+            pltpu.SemaphoreType.DMA((2, NY)),
+            pltpu.SemaphoreType.DMA((2, NY)),
+            pltpu.SemaphoreType.DMA((2, 3, NZ)),
+            pltpu.SemaphoreType.DMA((2, 3, NZ)),
         ],
         compiler_params=pltpu.CompilerParams(
             collective_id=3, has_side_effects=True, vmem_limit_bytes=52 * 2**20

time: 252 us -> 227 us (0.901)
  Pallas kernels: 242 us -> 217 us
    pallas_call x1, Pallas kernels: 88.8 us -> 74.7 us  [gather_and_project(): pl.pallas_call(gather_kernel, out_shape=(jax.ShapeDtypeStruct((2, NY, NZ,...]
    pallas_call x1, Pallas kernels: 61.3 us -> 52.2 us  [finish(): pl.pallas_call(finish_kernel, out_shape=(jax.ShapeDtypeStruct((length, wi...]
where the time goes in v5:
time: 227 us; the launch traced here: 226 us
  Pallas kernels  217 us (96%)
  local copies, waits for them, and re-layouts  5.65 us (2%)
    pallas_call x1, Pallas kernels, cluster_part(): pl.pallas_call(cluster_kernel, out_shape=(rows, rows), in_specs=[pl.Block...  89.8 us
    pallas_call x1, Pallas kernels, gather_and_project(): pl.pallas_call(gather_kernel, out_shape=(jax.ShapeDtypeStruct((2, NY, NZ,...  74.7 us
    pallas_call x1, Pallas kernels, finish(): pl.pallas_call(finish_kernel, out_shape=(jax.ShapeDtypeStruct((length, wi...  52.2 us
    unnamed x14, local copies, waits for them, and re-layouts  5.55 us

profile of v5, /device:TPU:2, one launch (start us, length us, event | category | flops | bytes accessed | tf_op | source)
XLA Modules:
  0.0 226.0 jit_solution(10623597306994494843)
XLA Ops:
  0.6 0.0 copy-start.6
  0.6 0.8 copy.50
  1.4 0.0 copy-start.1
  1.4 0.8 copy-done.1
  2.2 0.0 copy-start.2
  2.2 0.8 copy-done.2
  3.1 0.0 copy-start.4
  3.1 74.7 %gather_and_project.1 = (f32[2,4,8,32,1024]{4,3,2,1,0:T(8,128)}, f32[32,64,128]{2,1,0:T(8,128)S(1)}, s32[1,1536]{1,0:T(1,128)S(1)}, s32[384,128]{1,0:T(8,128)S(1)}, bf16[2,1536,256]{2,1,0:T(8,128)(2,1)S(1)}) custom-call(f32[32,512]{1,0:T(8,128)S(1)} %copy-done.1, f32[32,512]{1,0:T(8,128)S(1)} %copy-done.2, s32[8,384]{1,0:T(8,128)S(1)} %pad.4.cluster_ref, ...), custom_call_target="tpu_custom_call" | custom-call | tf_op jit(solution)/shard_map/gather_and_project/pallas_call | solution.py:404
  77.7 0.0 copy-start.5
  77.8 1.0 copy-done.5
  78.7 0.7 slice_reduce_fusion
  80.1 0.0 copy-done.6
  80.1 0.0 copy-done.4
  80.1 143.7 %conditional.1 = (f32[32,512]{1,0:T(8,128)S(1)}, f32[32,512]{1,0:T(8,128)S(1)}, f32[1,384,512]{2,1,0:T(8,128)S(1)}) conditional(s32[]{:T(128)} %convert_element_type.30, (s32[4,384]{1,0:T(4,128)S(1)}, s32[4,1,384,1]{2,3,1,0:T(1,128)S(1)}, f32[384,2048]{1,0:T(8,128)}, f32[2048,1024]{1,0:T(8,128)}, f32[1,384,512]{2,1,0:T(8,128)S(1)}) %tuple.42, ...), branch_computations={%region_1.5_spmd, %region_5.6_spmd} | conditional | flops 2620740 | bytes 82510656 | solution.py:1364
  80.3 1.1 fusion.1
  81.4 0.1 reshape.292.marks_ref
  81.5 89.8 %exchange_and_attend.1 = (f32[32,56,128]{2,1,0:T(8,128)S(1)}, f32[32,56,128]{2,1,0:T(8,128)S(1)}) custom-call(bf16[2,1536,256]{2,1,0:T(8,128)(2,1)S(1)} %get-tuple-element.39.pay_ref, s32[1,1536]{1,0:T(1,128)S(1)} %get-tuple-element.40.slots_ref, s32[4,1,448]{2,1,0:T(1,128)S(1)} %reshape.292.marks_ref, f32[32,64,128]{2,1,0:T(8,128)} %get-tuple-element.41.early_ref), custom_call_target="tpu_custom_call" | custom-call | tf_op jit(solution)/shard_map/cond/branch_1_fun/exchange_and_attend/pallas_call | solution.py:914
  171.3 52.2 %grads_and_scatter.1 = (f32[384,512]{1,0:T(8,128)S(1)}, f32[32,512]{1,0:T(8,128)S(1)}, f32[32,512]{1,0:T(8,128)S(1)}) custom-call(f32[1792,128]{1,0:T(8,128)S(1)} %bitcast.33, f32[1792,128]{1,0:T(8,128)S(1)} %bitcast.34, s32[384,128]{1,0:T(8,128)S(1)} %get-tuple-element.44.slots_ref, f32[384,2048]{1,0:T(8,128)} %get-tuple-element.45.tokens_ref, ...), custom_call_target="tpu_custom_call" | custom-call | tf_op jit(solution)/shard_map/cond/branch_1_fun/grads_and_scatter/pallas_call | solution.py:1261
  223.8 0.9 copy.60
  224.7 0.6 copy.61
  225.3 0.6 copy.62
  (1 shorter events, 0.0 us)
Async XLA Ops:
  0.6 79.5 %copy-start.6 = (s32[4,1,384,1]{2,3,1,0:T(1,128)S(1)}, s32[4,1,384,1]{2,3,1,0:T(1,128)}, u32[]{:S(2)}) copy-start(s32[4,1,384,1]{2,3,1,0:T(1,128)} %param.11) | copy-start | bytes 18436
  1.4 0.8 copy-start.1
  2.2 0.8 copy-start.2
  3.1 77.0 %copy-start.4 = (f32[1,384,512]{2,1,0:T(8,128)S(1)}, f32[1,384,512]{2,1,0:T(8,128)}, u32[]{:S(2)}) copy-start(f32[1,384,512]{2,1,0:T(8,128)} %param.10) | copy-start | bytes 2359300
  77.7 1.0 copy-start.5

commit v6 on v5

--- a/solution.py
+++ b/solution.py
@@ -79,7 +79,7 @@
             copy.wait_send()
 
 
-GATHER_COPIES = 3 + 7 + 14 + 21 + 16 + 4
+GATHER_COPIES = 6 + 7 + 14 + 21 + 16 + 4
 ROUTE_COPIES = 3 + 7 + 3 + 1
 CLUSTERS = 256
 OWNERS = 32
@@ -192,8 +192,11 @@
     first.wait()
     second.wait()
     copies = Copies(send_sem, recv_sem)
-    shared = [copies.start(mine, mine, along_y(step)) for step in (1, 3, 2)]
+    top, bottom = mine.at[pl.ds(0, HALF), :], mine.at[pl.ds(HALF, HALF), :]
+    shared = [copies.start(top, top, along_y(step)) for step in (1, 3, 2)]
     pieces = [(copies.start(piece(0), piece(0), right), copies.start(piece(0), piece(0), left))]
+
+    below = [copies.start(bottom, bottom, along_y(step)) for step in (1, 3, 2)]
 
     for head in range(heads):
         upper, lower = halves(grad_ref[:, head * HD : (head + 1) * HD])
@@ -338,7 +341,7 @@
             device_id_type=MESH,
         )
 
-    @pl.loop(1, OWNERS // 2)
+    @pl.loop(1, OWNERS // 4)
     def _(step):
         early(step).start()
 
@@ -347,10 +350,12 @@
     turn_planes(2)
     turn_planes(3)
 
-    @pl.loop(OWNERS // 2, OWNERS)
+    @pl.loop(OWNERS // 4, OWNERS)
     def _(step):
         early(step).start()
 
+    for copy in below:
+        copy.wait_recv()
     for step in (1, 3, 2):
         for copy in passed[step]:
             copy.wait_recv()
@@ -742,15 +747,37 @@
     )(marks, rows, early)
 
 
+def unpack_rows(back, slots_ref, high, low, heads):
+    source = jnp.concatenate(halves(back), axis=1)
+    length = slots_ref.shape[0]
+    for head in range(heads):
+        place = lax.broadcasted_iota(jnp.int32, (length, back.shape[0]), 1)
+        moved = dot(one(place == slots_ref[:, head : head + 1]), source)
+        there = pl.ds(head * HD, HD)
+        high[:, there], low[:, there] = halves(moved[:, :HD] + moved[:, HD:])
+
+
+def line_of_sums(tokens, half, there, gradients):
+    per_line = NZ * ROWS
+    start = pl.multiple_of((half * NY + there) * per_line, per_line)
+    sums = dot3(halves(tokens[:, pl.ds(start, per_line)]), gradients, TN)
+    return sums.reshape(NZ, ROWS, sums.shape[1])
+
+
 QK, VALUE, GRAD_VALUE, GRAD_QK = range(4)
 
 
 def cluster_kernel(
-    pay_ref, slots_ref, marks_ref, early_ref, back_qk_ref, back_value_ref,
-    leaving, landed, seats, spread, valid, weights, answer,
-    local_sem, send_sem, recv_sem,
+    pay_ref, slots_ref, marks_ref, early_ref, tall_slots_ref, tokens_ref,
+    back_qk_ref, high_ref, low_ref, own_ref,
+    leaving, landed, seats, spread, valid, weights, answer, tokens, away, cross_in,
+    local_sem, send_sem, recv_sem, cross_send, cross_recv,
 ):
     me = lax.axis_index("ctx")
+    rep, y, _ = position()
+    other = {"rep": 1 - rep}
+    fetch = pltpu.make_async_copy(tokens_ref, tokens, local_sem.at[4])
+    fetch.start()
     groups, _, wide = marks_ref.shape
     owned, seat = spread.shape[2], spread.shape[3]
     size = groups * seat
@@ -763,10 +790,10 @@
         there = {"ctx": lax.rem(me + step, OWNERS)}
         pl.semaphore_signal(barrier, inc=1, device_id=there, device_id_type=MESH)
 
+    pl.semaphore_signal(barrier, inc=1, device_id=other, device_id_type=MESH)
+
     def target(kind):
-        if kind == GRAD_QK:
-            return back_qk_ref
-        return back_value_ref if kind == GRAD_VALUE else landed.at[kind]
+        return back_qk_ref if kind == GRAD_QK else landed.at[kind]
 
     def remote(kind, step):
         there = lax.rem(me + step, OWNERS)
@@ -825,7 +852,7 @@
         return lax.div(me, 4)
 
     pack(QK, first_block())
-    pl.semaphore_wait(barrier, OWNERS - 1)
+    pl.semaphore_wait(barrier, OWNERS)
     for lane in range(4):
         start(QK, first_block() * 4 + lane)
 
@@ -897,7 +924,40 @@
 
     give(GRAD_QK)
     arrive(GRAD_VALUE)
+
+    back = landed[GRAD_VALUE].reshape(OWNERS * ROOM, HD)
+    unpack_rows(back, tall_slots_ref, high_ref, low_ref, high_ref.shape[1] // HD)
+    fetch.wait()
+
+    def cross(step):
+        there = lax.rem(y + step, NY)
+        return pltpu.make_async_remote_copy(
+            src_ref=away.at[there],
+            dst_ref=cross_in.at[there],
+            send_sem=cross_send.at[step],
+            recv_sem=cross_recv.at[step],
+            device_id=other,
+            device_id_type=MESH,
+        )
+
+    @pl.loop(0, NY)
+    def _(step):
+        there = lax.rem(y + step, NY)
+        away[there] = line_of_sums(tokens, 1 - rep, there, (high_ref[...], low_ref[...]))
+        cross(step).start()
+
+    @pl.loop(0, NY)
+    def _(step):
+        there = lax.rem(y + step, NY)
+        mine = line_of_sums(tokens, rep, there, (high_ref[...], low_ref[...]))
+        cross(step).wait_recv()
+        own_ref[there] = mine + cross_in[there]
+
     arrive(GRAD_QK)
+
+    @pl.loop(0, NY)
+    def _(step):
+        cross(step).wait_send()
 
     @pl.loop(1, OWNERS)
     def _(step):
@@ -905,34 +965,46 @@
             remote(kind, step).wait_send()
 
 
-def cluster_part(pay, slots, marks, early):
+def cluster_part(pay, slots, marks, early, tall_slots, inputs):
     groups = OWNERS // GROUP
     owned = TALL // (3 * GROUP)
     seat = 3 * GROUP
     size = groups * seat
-    rows = jax.ShapeDtypeStruct((OWNERS, ROOM, HD), f32)
+    length = inputs.shape[0]
+    width = pay.shape[1] // length * HD
+    vmem, anywhere = pl.BlockSpec(memory_space=pltpu.VMEM), pl.BlockSpec(memory_space=pl.ANY)
     return pl.pallas_call(
         cluster_kernel,
-        out_shape=(rows, rows),
-        in_specs=[pl.BlockSpec(memory_space=pltpu.VMEM)] * 4,
-        out_specs=(pl.BlockSpec(memory_space=pl.ANY),) * 2,
+        out_shape=(
+            jax.ShapeDtypeStruct((OWNERS, ROOM, HD), f32),
+            jax.ShapeDtypeStruct((length, width), bf16),
+            jax.ShapeDtypeStruct((length, width), bf16),
+            jax.ShapeDtypeStruct((NY, NZ, ROWS, width), f32),
+        ),
+        in_specs=[vmem, vmem, vmem, vmem, vmem, anywhere],
+        out_specs=(anywhere, vmem, vmem, vmem),
         scratch_shapes=[
             pltpu.VMEM((4, OWNERS, ROOM, HD), f32),
-            pltpu.VMEM((2, OWNERS, ROOM, HD), f32),
+            pltpu.VMEM((3, OWNERS, ROOM, HD), f32),
             pltpu.VMEM((groups, TALL, GROUP * ROOM), bf16),
             pltpu.VMEM((3, groups, owned, seat, HD), f32),
             pltpu.VMEM((groups, owned, seat, LANES), f32),
             pltpu.VMEM((owned, size, size), f32),
             pltpu.VMEM((groups, owned, seat, HD), f32),
-            pltpu.SemaphoreType.DMA((4,)),
+            pltpu.VMEM(inputs.shape, f32),
+            pltpu.VMEM((NY, NZ, ROWS, width), f32),
+            pltpu.VMEM((NY, NZ, ROWS, width), f32),
+            pltpu.SemaphoreType.DMA((5,)),
             pltpu.SemaphoreType.DMA((4, OWNERS)),
             pltpu.SemaphoreType.DMA((4, OWNERS)),
+            pltpu.SemaphoreType.DMA((NY,)),
+            pltpu.SemaphoreType.DMA((NY,)),
         ],
         compiler_params=pltpu.CompilerParams(
             collective_id=2, has_side_effects=True, vmem_limit_bytes=BIG
         ),
         name="exchange_and_attend",
-    )(pay, slots, marks, early)
+    )(pay, slots, marks, early, tall_slots, inputs)
 
 
 def grads_kernel(
@@ -994,7 +1066,7 @@
 
 
 def finish_kernel(
-    back_qk_ref, back_value_ref, slots_ref, tokens_ref, full_ref,
+    back_qk_ref, high_ref, low_ref, sums_ref, slots_ref, tokens_ref, full_ref,
     tokens_out, qk_out, value_out,
     tokens, full, high, low, terms, away, own, cross_in,
     column_in, passing, ring_a, ring_b, line_in, plane_in,
@@ -1006,8 +1078,6 @@
     length = tokens.shape[0]
     both = full.shape[1]
     width = both // 2
-    total = back_qk_ref.shape[0]
-    per_line = NZ * ROWS
 
     def along_y(step):
         return {"ctx": lax.rem(y + step, NY) * NZ + z}
@@ -1021,8 +1091,9 @@
     loads = [
         pltpu.make_async_copy(tokens_ref, tokens, load_sem.at[0]),
         pltpu.make_async_copy(full_ref, full, load_sem.at[1]),
+        pltpu.make_async_copy(sums_ref, own.at[1], load_sem.at[2]),
     ]
-    for load in loads:
+    for load in reversed(loads):
         load.start()
     right, left, other = along_z(1), along_z(NZ - 1), {"rep": 1 - rep}
     barrier = pltpu.get_barrier_semaphore()
@@ -1031,45 +1102,34 @@
     for partner in partners:
         pl.semaphore_signal(barrier, inc=1, device_id=partner, device_id_type=MESH)
 
-    def unpack(part, back_ref):
-        source = jnp.concatenate(halves(back_ref[...]), axis=1)
-        for head in range(width // HD):
-            place = lax.broadcasted_iota(jnp.int32, (length, total), 1)
-            moved = dot(one(place == slots_ref[:, head : head + 1]), source)
-            there = pl.ds(part * width + head * HD, HD)
-            high[:, there], low[:, there] = halves(moved[:, :HD] + moved[:, HD:])
-
-    def line_sum(half, there, part):
-        start = pl.multiple_of(half * (NY * per_line) + there * per_line, per_line)
-        some = halves(tokens[:, pl.ds(start, per_line)])
-        here = pl.ds(part * width, width)
-        return dot3(some, (high[:, here], low[:, here]), TN).reshape(NZ, ROWS, width)
-
-    def cross(step, part):
+    def cross(step):
         there = lax.rem(y + step, NY)
         return pltpu.make_async_remote_copy(
-            src_ref=away.at[part, there],
-            dst_ref=cross_in.at[part, there],
-            send_sem=cross_send.at[part, step],
-            recv_sem=cross_recv.at[part, step],
+            src_ref=away.at[there],
+            dst_ref=cross_in.at[there],
+            send_sem=cross_send.at[step],
+            recv_sem=cross_recv.at[step],
             device_id=other,
             device_id_type=MESH,
         )
 
-    def away_lines(part):
+    def line_sum(half, there):
+        return line_of_sums(tokens, half, there, (high[:, :width], low[:, :width]))
+
+    def away_lines():
         @pl.loop(0, NY)
         def _(step):
             there = lax.rem(y + step, NY)
-            away[part, there] = line_sum(1 - rep, there, part)
-            cross(step, part).start()
-
-    def own_lines(part):
+            away[there] = line_sum(1 - rep, there)
+            cross(step).start()
+
+    def own_lines():
         @pl.loop(0, NY)
         def _(step):
             there = lax.rem(y + step, NY)
-            mine = line_sum(rep, there, part)
-            cross(step, part).wait_recv()
-            own[part, there] = mine + cross_in[part, there]
+            mine = line_sum(rep, there)
+            cross(step).wait_recv()
+            own[0, there] = mine + cross_in[there]
 
     def depth(turn):
         return lax.rem(z + turn, NZ)
@@ -1172,39 +1232,41 @@
         start = pl.multiple_of(lax.rem(x + step, 4) * width, width)
         return dot3((high[...], low[...]), halves(full[pl.ds(start, width), :]), NT)
 
-    unpack(1, back_value_ref)
-    loads[0].wait()
     pl.semaphore_wait(barrier, len(partners))
-    away_lines(1)
-    own_lines(1)
+    loads[2].wait()
     turn_a(0, 1)
     send_pieces(1)
-    unpack(0, back_qk_ref)
+    high[:, pl.ds(width, width)] = high_ref[...]
+    low[:, pl.ds(width, width)] = low_ref[...]
+    unpack_rows(back_qk_ref[...], slots_ref, high, low, width // HD)
+    loads[0].wait()
+    away_lines()
     turn_a(1, 1)
-    away_lines(0)
+    own_lines()
+    turn_a(0, 0)
+    send_pieces(0)
     turn_b(0, 1)
     turn_a(2, 1)
-    own_lines(0)
-    turn_a(0, 0)
-    send_pieces(0)
-    turn_b(1, 1)
     loads[1].wait()
     terms[1] = columns(2)
     by_right = copies.start(terms.at[1, upper_rows], passing.at[0], along_x(1))
     by_left = copies.start(terms.at[1, lower_rows], passing.at[1], along_x(3))
+    turn_b(1, 1)
+    turn_a(1, 0)
     turn_a(3, 1)
-    turn_b(2, 1)
     terms[0] = columns(1)
     sideways = [copies.start(terms.at[0, lower_rows], column_in.at[0, lower_rows], along_x(1))]
-    turn_a(1, 0)
-    turn_b(3, 1)
+    turn_b(0, 0)
+    turn_b(2, 1)
+    turn_a(2, 0)
     terms[2] = columns(3)
     sideways.append(
         copies.start(terms.at[2, upper_rows], column_in.at[1, upper_rows], along_x(3))
     )
-    turn_b(0, 0)
+    turn_b(1, 0)
     end_a(1)
-    turn_a(2, 0)
+    turn_b(3, 1)
+    turn_a(3, 0)
     by_right.wait_recv()
     terms[0, upper_rows, :] += passing[0]
     sideways.append(
@@ -1215,10 +1277,8 @@
     sideways.append(
         copies.start(terms.at[2, lower_rows], column_in.at[1, lower_rows], along_x(3))
     )
-    turn_b(1, 0)
-    turn_a(3, 0)
+    turn_b(2, 0)
     end_b(1, value_out)
-    turn_b(2, 0)
     tokens_out[...] = columns(0)
     turn_b(3, 0)
     end_a(0)
@@ -1240,8 +1300,7 @@
 
     @pl.loop(0, NY)
     def _(step):
-        for part in range(2):
-            cross(step, part).wait_send()
+        cross(step).wait_send()
 
     @pl.loop(1, NY)
     def _(step):
@@ -1253,7 +1312,7 @@
     assert len(copies.all) == FINISH_COPIES
 
 
-def finish(back_qk, back_value, slots, inputs, full):
+def finish(back_qk, high, low, sums, slots, inputs, full):
     length, depth = inputs.shape
     both = full.shape[1]
     width = both // 2
@@ -1265,7 +1324,7 @@
             jax.ShapeDtypeStruct((ROWS, width), f32),
             jax.ShapeDtypeStruct((ROWS, width), f32),
         ),
-        in_specs=[vmem, vmem, vmem, anywhere, anywhere],
+        in_specs=[vmem, vmem, vmem, anywhere, vmem, anywhere, anywhere],
         out_specs=(vmem,) * 3,
         scratch_shapes=[
             pltpu.VMEM((length, depth), f32),
@@ -1273,20 +1332,20 @@
             pltpu.VMEM((length, both), bf16),
             pltpu.VMEM((length, both), bf16),
             pltpu.VMEM((3, length, width), f32),
+            pltpu.VMEM((NY, NZ, ROWS, width), f32),
             pltpu.VMEM((2, NY, NZ, ROWS, width), f32),
-            pltpu.VMEM((2, NY, NZ, ROWS, width), f32),
-            pltpu.VMEM((2, NY, NZ, ROWS, width), f32),
+            pltpu.VMEM((NY, NZ, ROWS, width), f32),
             pltpu.VMEM((2, length, width), f32),
             pltpu.VMEM((2, length // 2, width), f32),
             pltpu.VMEM((2, 7, NY, HALF, width), f32),
             pltpu.VMEM((2, 7, HALF, width), f32),
             pltpu.VMEM((2, 3, NZ, HALF, width), f32),
             pltpu.VMEM((2, 3, HALF, width), f32),
-            pltpu.SemaphoreType.DMA((2,)),
+            pltpu.SemaphoreType.DMA((3,)),
             pltpu.SemaphoreType.DMA((FINISH_COPIES,)),
             pltpu.SemaphoreType.DMA((FINISH_COPIES,)),
-            pltpu.SemaphoreType.DMA((2, NY)),
-            pltpu.SemaphoreType.DMA((2, NY)),
+            pltpu.SemaphoreType.DMA((NY,)),
+            pltpu.SemaphoreType.DMA((NY,)),
             pltpu.SemaphoreType.DMA((2, 3, NZ)),
             pltpu.SemaphoreType.DMA((2, 3, NZ)),
         ],
@@ -1294,7 +1353,7 @@
             collective_id=3, has_side_effects=True, vmem_limit_bytes=52 * 2**20
         ),
         name="grads_and_scatter",
-    )(back_qk, back_value, slots, inputs, full)
+    )(back_qk, high, low, sums, slots, inputs, full)
 
 
 def exchange(array):
@@ -1313,9 +1372,9 @@
     held, place = marks[:, 0], marks[:, 1]
     seats = jnp.where(held > 0.5, (held - 1) * (3 * GROUP) + place, -1.0).astype(jnp.int32)
     seats = seats.reshape(OWNERS // GROUP, 1, GROUP * ROOM)
-    back = cluster_part(pay, slots, seats, early)
-    back_qk, back_value = (rows.reshape(OWNERS * ROOM, HD) for rows in back)
-    return finish(back_qk, back_value, tall_slots, inputs, full)
+    back_qk, high, low, sums = cluster_part(pay, slots, seats, early, tall_slots, inputs)
+    back_qk = back_qk.reshape(OWNERS * ROOM, HD)
+    return finish(back_qk, high, low, sums, tall_slots, inputs, full)
 
 
 def roomy_part(inputs, full, upstream, cluster):

time: 227 us -> 218 us (0.960)
  Pallas kernels: 217 us -> 207 us
    pallas_call x1, Pallas kernels: 74.7 us -> 70 us  [gather_and_project(): pl.pallas_call(gather_kernel, out_shape=(jax.ShapeDtypeStruct((2, NY, NZ,...]
    pallas_call x1, Pallas kernels: 52.2 us -> 48.1 us  [finish(): pl.pallas_call(finish_kernel, out_shape=(jax.ShapeDtypeStruct((length, wi...]
where the time goes in v6:
time: 218 us
  Pallas kernels  207 us (95%)
  local copies, waits for them, and re-layouts  7.05 us (3%)
    pallas_call x1, Pallas kernels, cluster_part(): pl.pallas_call(cluster_kernel, out_shape=(jax.ShapeDtypeStruct((OWNERS, R...  88.8 us
    pallas_call x1, Pallas kernels, gather_and_project(): pl.pallas_call(gather_kernel, out_shape=(jax.ShapeDtypeStruct((2, NY, NZ,...  70 us
    pallas_call x1, Pallas kernels, finish(): pl.pallas_call(finish_kernel, out_shape=(jax.ShapeDtypeStruct((length, wi...  48.1 us
    unnamed x14, local copies, waits for them, and re-layouts  5.56 us

profile of v6, /device:TPU:2, one launch (start us, length us, event | category | flops | bytes accessed | tf_op | source)
XLA Modules:
  0.0 217.7 jit_solution(6316830808619499934)
XLA Ops:
  0.6 0.0 copy-start.8
  0.6 0.8 copy.50
  1.4 0.0 copy-start.2
  1.4 0.8 copy-done.2
  2.2 0.0 copy-start.3
  2.2 0.8 copy-done.3
  3.1 70.0 %gather_and_project.1 = (f32[2,4,8,32,1024]{4,3,2,1,0:T(8,128)}, f32[32,64,128]{2,1,0:T(8,128)S(1)}, s32[1,1536]{1,0:T(1,128)S(1)}, s32[384,128]{1,0:T(8,128)S(1)}, bf16[2,1536,256]{2,1,0:T(8,128)(2,1)S(1)}) custom-call(f32[32,512]{1,0:T(8,128)S(1)} %copy-done.2, f32[32,512]{1,0:T(8,128)S(1)} %copy-done.3, s32[8,384]{1,0:T(8,128)S(1)} %pad.4.cluster_ref, ...), custom_call_target="tpu_custom_call" | custom-call | tf_op jit(solution)/shard_map/gather_and_project/pallas_call | solution.py:409
  73.1 0.0 copy-start.7
  73.2 1.0 copy-done.7
  74.1 0.7 slice_reduce_fusion
  75.5 0.0 copy-done.8
  75.5 0.0 copy-done.6
  75.5 140.0 %conditional.1 = (f32[32,512]{1,0:T(8,128)S(1)}, f32[32,512]{1,0:T(8,128)S(1)}, f32[1,384,512]{2,1,0:T(8,128)S(1)}) conditional(s32[]{:T(128)} %convert_element_type.30, (s32[4,384]{1,0:T(4,128)S(1)}, s32[4,1,384,1]{2,3,1,0:T(1,128)S(1)}, f32[384,2048]{1,0:T(8,128)}, f32[2048,1024]{1,0:T(8,128)}, f32[1,384,512]{2,1,0:T(8,128)S(1)}) %tuple.42, ...), branch_computations={%region_1.5_spmd, %region_5.6_spmd} | conditional | flops 2620740 | bytes 57344792 | solution.py:1423
  75.7 1.1 fusion.1
  76.8 0.1 reshape.289.marks_ref
  76.9 0.0 copy-start.5
  76.9 88.8 %exchange_and_attend.1 = (f32[32,56,128]{2,1,0:T(8,128)S(1)}, bf16[384,512]{1,0:T(8,128)(2,1)S(1)}, bf16[384,512]{1,0:T(8,128)(2,1)S(1)}, f32[4,8,32,512]{3,2,1,0:T(8,128)S(1)}) custom-call(bf16[2,1536,256]{2,1,0:T(8,128)(2,1)S(1)} %get-tuple-element.39.pay_ref, s32[1,1536]{1,0:T(1,128)S(1)} %get-tuple-element.40.slots_ref, ...), custom_call_target="tpu_custom_call" | custom-call | tf_op jit(solution)/shard_map/cond/branch_1_fun/exchange_and_attend/pallas_call | solution.py:976
  165.7 0.0 copy-start.1
  165.7 1.4 copy-done.1
  167.1 0.0 copy-done.5
  167.1 48.1 %grads_and_scatter.1 = (f32[384,512]{1,0:T(8,128)S(1)}, f32[32,512]{1,0:T(8,128)S(1)}, f32[32,512]{1,0:T(8,128)S(1)}) custom-call(f32[1792,128]{1,0:T(8,128)S(1)} %bitcast.32, bf16[384,512]{1,0:T(8,128)(2,1)S(1)} %get-tuple-element.45.high_ref, bf16[384,512]{1,0:T(8,128)(2,1)S(1)} %get-tuple-element.46.low_ref, f32[4,8,32,512]{3,2,1,0:T(8,128)} %copy-done.1, ...), custom_call_target="tpu_custom_call" | custom-call | tf_op jit(solution)/shard_map/cond/branch_1_fun/grads_and_scatter/pallas_call | solution.py:1320
  215.5 0.9 copy.60
  216.4 0.6 copy.61
  217.1 0.6 copy.62
  (2 shorter events, 0.0 us)
Async XLA Ops:
  0.6 74.9 %copy-start.8 = (s32[4,1,384,1]{2,3,1,0:T(1,128)S(1)}, s32[4,1,384,1]{2,3,1,0:T(1,128)}, u32[]{:S(2)}) copy-start(s32[4,1,384,1]{2,3,1,0:T(1,128)} %param.11) | copy-start | bytes 18436
  1.4 0.8 copy-start.2
  2.2 0.8 copy-start.3
  3.1 72.4 %copy-start.6 = (f32[1,384,512]{2,1,0:T(8,128)S(1)}, f32[1,384,512]{2,1,0:T(8,128)}, u32[]{:S(2)}) copy-start(f32[1,384,512]{2,1,0:T(8,128)} %param.10) | copy-start | bytes 2359300
  73.1 1.0 copy-start.7
  76.9 90.2 %copy-start.5 = (f32[384,2048]{1,0:T(8,128)S(1)}, f32[384,2048]{1,0:T(8,128)}, u32[]{:S(2)}) copy-start(f32[384,2048]{1,0:T(8,128)} %get-tuple-element.43.tokens_ref) | copy-start | bytes 9437188 | tf_op jit(solution)/shard_map/cond
  165.7 1.4 copy-start.1

commit v7 on v6

--- a/solution.py
+++ b/solution.py
@@ -437,7 +437,7 @@
             pltpu.SemaphoreType.DMA((OWNERS,)),
         ],
         compiler_params=pltpu.CompilerParams(
-            collective_id=0, has_side_effects=True, vmem_limit_bytes=BIG
+            collective_id=0, has_side_effects=True, vmem_limit_bytes=60 * 2**20
         ),
         name="gather_and_project",
     )(qk_weight, value_weight, clusters, upstream, inputs)
@@ -769,8 +769,8 @@
 
 def cluster_kernel(
     pay_ref, slots_ref, marks_ref, early_ref, tall_slots_ref, tokens_ref,
-    back_qk_ref, high_ref, low_ref, own_ref,
-    leaving, landed, seats, spread, valid, weights, answer, tokens, away, cross_in,
+    back_qk_ref, high_ref, low_ref, sums_ref,
+    leaving, landed, seats, spread, valid, weights, answer, tokens, away, cross_in, own,
     local_sem, send_sem, recv_sem, cross_send, cross_recv,
 ):
     me = lax.axis_index("ctx")
@@ -951,9 +951,12 @@
         there = lax.rem(y + step, NY)
         mine = line_of_sums(tokens, rep, there, (high_ref[...], low_ref[...]))
         cross(step).wait_recv()
-        own_ref[there] = mine + cross_in[there]
-
+        own[there] = mine + cross_in[there]
+
+    save = pltpu.make_async_copy(own, sums_ref, local_sem.at[5])
+    save.start()
     arrive(GRAD_QK)
+    save.wait()
 
     @pl.loop(0, NY)
     def _(step):
@@ -982,7 +985,7 @@
             jax.ShapeDtypeStruct((NY, NZ, ROWS, width), f32),
         ),
         in_specs=[vmem, vmem, vmem, vmem, vmem, anywhere],
-        out_specs=(anywhere, vmem, vmem, vmem),
+        out_specs=(anywhere, vmem, vmem, anywhere),
         scratch_shapes=[
             pltpu.VMEM((4, OWNERS, ROOM, HD), f32),
             pltpu.VMEM((3, OWNERS, ROOM, HD), f32),
@@ -994,14 +997,15 @@
             pltpu.VMEM(inputs.shape, f32),
             pltpu.VMEM((NY, NZ, ROWS, width), f32),
             pltpu.VMEM((NY, NZ, ROWS, width), f32),
-            pltpu.SemaphoreType.DMA((5,)),
+            pltpu.VMEM((NY, NZ, ROWS, width), f32),
+            pltpu.SemaphoreType.DMA((6,)),
             pltpu.SemaphoreType.DMA((4, OWNERS)),
             pltpu.SemaphoreType.DMA((4, OWNERS)),
             pltpu.SemaphoreType.DMA((NY,)),
             pltpu.SemaphoreType.DMA((NY,)),
         ],
         compiler_params=pltpu.CompilerParams(
-            collective_id=2, has_side_effects=True, vmem_limit_bytes=BIG
+            collective_id=2, has_side_effects=True, vmem_limit_bytes=60 * 2**20
         ),
         name="exchange_and_attend",
     )(pay, slots, marks, early, tall_slots, inputs)
@@ -1350,7 +1354,7 @@
             pltpu.SemaphoreType.DMA((2, 3, NZ)),
         ],
         compiler_params=pltpu.CompilerParams(
-            collective_id=3, has_side_effects=True, vmem_limit_bytes=52 * 2**20
+            collective_id=3, has_side_effects=True, vmem_limit_bytes=60 * 2**20
         ),
         name="grads_and_scatter",
     )(back_qk, high, low, sums, slots, inputs, full)

time: 218 us -> 222 us (1.018)
  Pallas kernels: 207 us -> 211 us
    pallas_call x1, Pallas kernels: 88.8 us -> 91.3 us  [cluster_part(): pl.pallas_call(cluster_kernel, out_shape=(jax.ShapeDtypeStruct((OWNERS, R...]
    unnamed x14 -> x8, local copies, waits for them, and re-layouts: 5.56 us -> 4.61 us
where the time goes in v7:
time: 222 us
  Pallas kernels  211 us (95%)
  local copies, waits for them, and re-layouts  5.9 us (3%)
  other arithmetic  2.71 us (1%)
    pallas_call x1, Pallas kernels, cluster_part(): pl.pallas_call(cluster_kernel, out_shape=(jax.ShapeDtypeStruct((OWNERS, R...  91.3 us
    pallas_call x1, Pallas kernels, gather_and_project(): pl.pallas_call(gather_kernel, out_shape=(jax.ShapeDtypeStruct((2, NY, NZ,...  71 us
    pallas_call x1, Pallas kernels, finish(): pl.pallas_call(finish_kernel, out_shape=(jax.ShapeDtypeStruct((length, wi...  48.8 us
    unnamed x8, local copies, waits for them, and re-layouts  4.61 us

profile of v7, /device:TPU:2, one launch (start us, length us, event | category | flops | bytes accessed | tf_op | source)
XLA Modules:
  0.0 221.6 jit_solution(12739875259126467476)
XLA Ops:
  0.6 0.0 copy-start.4
  0.6 0.0 copy-start.3
  0.7 0.8 copy.50
  1.4 0.6 pad.4.cluster_ref
  2.0 71.0 %gather_and_project.1 = (f32[2,4,8,32,1024]{4,3,2,1,0:T(8,128)}, f32[32,64,128]{2,1,0:T(8,128)}, s32[1,1536]{1,0:T(1,128)}, s32[384,128]{1,0:T(8,128)S(1)}, bf16[2,1536,256]{2,1,0:T(8,128)(2,1)}) custom-call(f32[32,512]{1,0:T(8,128)} %qk_ref.1, f32[32,512]{1,0:T(8,128)} %value_ref.1, s32[8,384]{1,0:T(8,128)} %pad.4.cluster_ref, f32[384,512]{1,0:T(8,128)} %bitcast.41, ...), custom_call_target="tpu_custom_call" | custom-call | tf_op jit(solution)/shard_map/gather_and_project/pallas_call | solution.py:409
  73.0 1.6 slice_reduce_fusion
  75.3 0.0 copy-done.4
  75.3 0.0 copy-done.3
  75.3 142.4 %conditional.1 = (f32[32,512]{1,0:T(8,128)}, f32[32,512]{1,0:T(8,128)}, f32[1,384,512]{2,1,0:T(8,128)S(1)}) conditional(s32[]{:T(128)} %convert_element_type.30, (s32[4,384]{1,0:T(4,128)S(1)}, s32[4,1,384,1]{2,3,1,0:T(1,128)S(1)}, f32[384,2048]{1,0:T(8,128)}, f32[2048,1024]{1,0:T(8,128)}, f32[1,384,512]{2,1,0:T(8,128)S(1)}) %tuple.41, ...), branch_computations={%region_1.5_spmd, %region_5.6_spmd} | conditional | flops 2620740 | bytes 57344792 | solution.py:1427
  75.5 1.1 fusion.1
  76.6 0.7 reshape.289.marks_ref
  77.3 0.0 copy-start.2
  77.3 91.3 %exchange_and_attend.1 = (f32[32,56,128]{2,1,0:T(8,128)}, bf16[384,512]{1,0:T(8,128)(2,1)}, bf16[384,512]{1,0:T(8,128)(2,1)}, f32[4,8,32,512]{3,2,1,0:T(8,128)}) custom-call(bf16[2,1536,256]{2,1,0:T(8,128)(2,1)} %get-tuple-element.39.pay_ref, s32[1,1536]{1,0:T(1,128)} %get-tuple-element.40.slots_ref, s32[4,1,448]{2,1,0:T(1,128)} %reshape.289.marks_ref, ...), custom_call_target="tpu_custom_call" | custom-call | tf_op jit(solution)/shard_map/cond/branch_1_fun/exchange_and_attend/pallas_call | solution.py:979
  168.6 0.0 copy-done.2
  168.6 48.8 %grads_and_scatter.1 = (f32[384,512]{1,0:T(8,128)S(1)}, f32[32,512]{1,0:T(8,128)}, f32[32,512]{1,0:T(8,128)}) custom-call(f32[1792,128]{1,0:T(8,128)} %bitcast.43, bf16[384,512]{1,0:T(8,128)(2,1)} %get-tuple-element.45.high_ref, bf16[384,512]{1,0:T(8,128)(2,1)} %get-tuple-element.46.low_ref, f32[4,8,32,512]{3,2,1,0:T(8,128)} %get-tuple-element.47.sums_ref, ...), custom_call_target="tpu_custom_call" | custom-call | tf_op jit(solution)/shard_map/cond/branch_1_fun/grads_and_scatter/pallas_call | solution.py:1324
  217.7 0.9 copy.60
  218.6 1.5 copy.61
  220.1 1.5 copy.62
Async XLA Ops:
  0.6 74.7 %copy-start.4 = (s32[4,1,384,1]{2,3,1,0:T(1,128)S(1)}, s32[4,1,384,1]{2,3,1,0:T(1,128)}, u32[]{:S(2)}) copy-start(s32[4,1,384,1]{2,3,1,0:T(1,128)} %param.11) | copy-start | bytes 18436
  0.6 74.7 %copy-start.3 = (f32[1,384,512]{2,1,0:T(8,128)S(1)}, f32[1,384,512]{2,1,0:T(8,128)}, u32[]{:S(2)}) copy-start(f32[1,384,512]{2,1,0:T(8,128)} %param.10) | copy-start | bytes 2359300
  77.3 91.3 %copy-start.2 = (f32[384,2048]{1,0:T(8,128)S(1)}, f32[384,2048]{1,0:T(8,128)}, u32[]{:S(2)}) copy-start(f32[384,2048]{1,0:T(8,128)} %get-tuple-element.43.tokens_ref) | copy-start | bytes 9437188 | tf_op jit(solution)/shard_map/cond

commit v8 on v6

--- a/solution.py
+++ b/solution.py
@@ -437,7 +437,7 @@
             pltpu.SemaphoreType.DMA((OWNERS,)),
         ],
         compiler_params=pltpu.CompilerParams(
-            collective_id=0, has_side_effects=True, vmem_limit_bytes=BIG
+            collective_id=0, has_side_effects=True, vmem_limit_bytes=60 * 2**20
         ),
         name="gather_and_project",
     )(qk_weight, value_weight, clusters, upstream, inputs)
@@ -1324,7 +1324,7 @@
             jax.ShapeDtypeStruct((ROWS, width), f32),
             jax.ShapeDtypeStruct((ROWS, width), f32),
         ),
-        in_specs=[vmem, vmem, vmem, anywhere, vmem, anywhere, anywhere],
+        in_specs=[vmem, vmem, vmem, vmem, vmem, anywhere, anywhere],
         out_specs=(vmem,) * 3,
         scratch_shapes=[
             pltpu.VMEM((length, depth), f32),

time: 218 us -> 216 us (level)
    unnamed x14 -> x8, local copies, waits for them, and re-layouts: 5.56 us -> 2.92 us
where the time goes in v8:
time: 216 us
  Pallas kernels  208 us (96%)
  local copies, waits for them, and re-layouts  5.01 us (2%)
    pallas_call x1, Pallas kernels, cluster_part(): pl.pallas_call(cluster_kernel, out_shape=(jax.ShapeDtypeStruct((OWNERS, R...  89.4 us
    pallas_call x1, Pallas kernels, gather_and_project(): pl.pallas_call(gather_kernel, out_shape=(jax.ShapeDtypeStruct((2, NY, NZ,...  70.4 us
    pallas_call x1, Pallas kernels, finish(): pl.pallas_call(finish_kernel, out_shape=(jax.ShapeDtypeStruct((length, wi...  48.6 us

profile of v8, /device:TPU:2, one launch (start us, length us, event | category | flops | bytes accessed | tf_op | source)
XLA Modules:
  0.0 216.2 jit_solution(13480479061399596364)
XLA Ops:
  0.6 0.0 copy-start.6
  0.6 0.0 copy-start.4
  0.7 0.8 copy.50
  1.4 0.6 pad.4.cluster_ref
  2.0 70.4 %gather_and_project.1 = (f32[2,4,8,32,1024]{4,3,2,1,0:T(8,128)}, f32[32,64,128]{2,1,0:T(8,128)S(1)}, s32[1,1536]{1,0:T(1,128)S(1)}, s32[384,128]{1,0:T(8,128)}, bf16[2,1536,256]{2,1,0:T(8,128)(2,1)S(1)}) custom-call(f32[32,512]{1,0:T(8,128)} %qk_ref.1, f32[32,512]{1,0:T(8,128)} %value_ref.1, s32[8,384]{1,0:T(8,128)} %pad.4.cluster_ref, f32[384,512]{1,0:T(8,128)} %bitcast.42, ...), custom_call_target="tpu_custom_call" | custom-call | tf_op jit(solution)/shard_map/gather_and_project/pallas_call | solution.py:409
  72.4 0.7 slice_reduce_fusion
  73.8 0.0 copy-done.6
  73.8 0.0 copy-done.4
  73.8 140.2 %conditional.1 = (f32[32,512]{1,0:T(8,128)S(1)}, f32[32,512]{1,0:T(8,128)S(1)}, f32[1,384,512]{2,1,0:T(8,128)S(1)}) conditional(s32[]{:T(128)} %convert_element_type.30, (s32[4,384]{1,0:T(4,128)S(1)}, s32[4,1,384,1]{2,3,1,0:T(1,128)S(1)}, f32[384,2048]{1,0:T(8,128)}, f32[2048,1024]{1,0:T(8,128)}, f32[1,384,512]{2,1,0:T(8,128)S(1)}) %tuple.41, ...), branch_computations={%region_1.5_spmd, %region_5.6_spmd} | conditional | flops 2620740 | bytes 57344792 | solution.py:1423
  74.1 0.1 fusion.1
  74.2 0.1 reshape.289.marks_ref
  74.2 0.0 copy-start.3
  74.3 0.0 copy-start.5
  74.3 89.4 %exchange_and_attend.1 = (f32[32,56,128]{2,1,0:T(8,128)S(1)}, bf16[384,512]{1,0:T(8,128)(2,1)S(1)}, bf16[384,512]{1,0:T(8,128)(2,1)S(1)}, f32[4,8,32,512]{3,2,1,0:T(8,128)S(1)}) custom-call(bf16[2,1536,256]{2,1,0:T(8,128)(2,1)S(1)} %get-tuple-element.39.pay_ref, s32[1,1536]{1,0:T(1,128)S(1)} %get-tuple-element.40.slots_ref, ...), custom_call_target="tpu_custom_call" | custom-call | tf_op jit(solution)/shard_map/cond/branch_1_fun/exchange_and_attend/pallas_call | solution.py:976
  163.7 0.0 copy-start.1
  163.7 1.4 copy-done.1
  165.1 0.0 copy-done.3
  165.1 0.0 copy-done.5
  165.1 48.6 %grads_and_scatter.1 = (f32[384,512]{1,0:T(8,128)S(1)}, f32[32,512]{1,0:T(8,128)S(1)}, f32[32,512]{1,0:T(8,128)S(1)}) custom-call(f32[1792,128]{1,0:T(8,128)S(1)} %bitcast.32, bf16[384,512]{1,0:T(8,128)(2,1)S(1)} %get-tuple-element.45.high_ref, bf16[384,512]{1,0:T(8,128)(2,1)S(1)} %get-tuple-element.46.low_ref, f32[4,8,32,512]{3,2,1,0:T(8,128)} %copy-done.1, ...), custom_call_target="tpu_custom_call" | custom-call | tf_op jit(solution)/shard_map/cond/branch_1_fun/grads_and_scatter/pallas_call | solution.py:1320
  214.0 0.9 copy.60
  214.9 0.6 copy.61
  215.5 0.6 copy.62
Async XLA Ops:
  0.6 73.2 %copy-start.6 = (s32[4,1,384,1]{2,3,1,0:T(1,128)S(1)}, s32[4,1,384,1]{2,3,1,0:T(1,128)}, u32[]{:S(2)}) copy-start(s32[4,1,384,1]{2,3,1,0:T(1,128)} %param.11) | copy-start | bytes 18436
  0.6 73.2 %copy-start.4 = (f32[1,384,512]{2,1,0:T(8,128)S(1)}, f32[1,384,512]{2,1,0:T(8,128)}, u32[]{:S(2)}) copy-start(f32[1,384,512]{2,1,0:T(8,128)} %param.10) | copy-start | bytes 2359300
  74.2 90.8 %copy-start.3 = (f32[384,2048]{1,0:T(8,128)S(1)}, f32[384,2048]{1,0:T(8,128)}, u32[]{:S(2)}) copy-start(f32[384,2048]{1,0:T(8,128)} %get-tuple-element.43.tokens_ref) | copy-start | bytes 9437188 | tf_op jit(solution)/shard_map/cond
  74.3 90.8 %copy-start.5 = (s32[384,128]{1,0:T(8,128)S(1)}, s32[384,128]{1,0:T(8,128)}, u32[]{:S(2)}) copy-start(s32[384,128]{1,0:T(8,128)} %get-tuple-element.42.tall_slots_ref.slots_ref) | copy-start | bytes 589828 | tf_op jit(solution)/shard_map/cond
  163.7 1.4 copy-start.1
